TPU v7x, 128 devices: a whole 4x4x4 slice. The times are simulated.
128 devices in a mesh: dp: 32 (over y, z_lo, x), rep: 4 (over z_hi, core).
Axes of the slice: x: 4, y: 4, z: 4 (z_hi: 2, z_lo: 2; z = z_hi * 2 + z_lo), core: 2. Of those that a mesh axis runs over, the one named last changes fastest.
Arguments:
- hidden_in: bfloat16 [98304, 4096], P(('dp', 'rep'))
- value_grad: bfloat16 [98304, 512], P(('dp', 'rep')), may hold values from -0.375 to 0.375
- value_weight: bfloat16 [4096, 512], replicated, may hold values from -0.09375 to 0.09375
- norm_gain: bfloat16 [4096], replicated, may hold values from 0.5 to 1.5
- owner_map: int32 [2], replicated, may hold values from 0 to 31, as said below
- mat_first: float32 [32, 4096, 512], P('dp', 'rep'), may hold values from -4 to 4
- mat_second: float32 [32, 4096, 512], P('dp', 'rep'), may hold values from 0.05 to 2
- vec_first: float32 [32, 4096], P('dp', 'rep'), may hold values from -4 to 4
- vec_second: float32 [32, 4096], P('dp', 'rep'), may hold values from 0.05 to 2
- next_hidden: bfloat16 [98304, 4096], P(('dp', 'rep'))
Outputs:
- new_weight: bfloat16 [4096, 512], replicated
- new_gain: bfloat16 [4096], replicated
- new_mat_first: float32 [32, 4096, 512], P('dp', 'rep')
- new_mat_second: float32 [32, 4096, 512], P('dp', 'rep')
- new_vec_first: float32 [32, 4096], P('dp', 'rep')
- new_vec_second: float32 [32, 4096], P('dp', 'rep')
- next_values: bfloat16 [98304, 512], P(('dp', 'rep'))
Inputs may be any that keep to these rules, and one draw needn't show every extreme that they name: `owner_map`: entry 0 names the owner of the value projection, entry 1 the owner of the norm gain; the two differ, and one of them is 31.
All inputs are finite; a program needn't handle non-finite values.
Results may differ from a plain program's by a relative error of at most 0.0013.
The roundings to bfloat16 on the way count: a program that leaves them out, or rounds other values in their place, can miss the bound.
Values may be sent and summed in bfloat16 or wider, within the bound.
No kernel may reach another device: no remote copies, remote signals or barrier semaphores. Data moves between devices by JAX's collectives and lax.ppermute only.
A program may use at most 128 MiB of HBM per device.

v0:
```python
import jax
import jax.numpy as jnp
from jax import lax
from jax.sharding import PartitionSpec as P

norm_eps = 1e-05
adam_eps = 1e-08
beta_first = 0.9
beta_second = 0.95
learn_rate = 0.001
gain_rate = 0.02
fix_first = 1.0 - 0.9**10
fix_second = 1.0 - 0.95**10


def spread(block, axis, source):
    block = jnp.where(lax.axis_index(axis) == source, block, jnp.zeros_like(block))
    return lax.psum(block, axis)


def normalize(token_rows, gain_vec):
    widened = token_rows.astype(jnp.float32)
    inv_rms = lax.rsqrt(jnp.mean(widened * widened, axis=-1, keepdims=True) + norm_eps)
    unit_rows = widened * inv_rms
    return (unit_rows, (unit_rows * gain_vec.astype(jnp.float32)).astype(jnp.bfloat16))


def adam_step(parameter, gradient, first_moment, second_moment, step_rate):
    first_moment = beta_first * first_moment + (1.0 - beta_first) * gradient
    second_moment = beta_second * second_moment + (1.0 - beta_second) * gradient * gradient
    update = first_moment / fix_first / (jnp.sqrt(second_moment / fix_second) + adam_eps)
    return (
        (parameter.astype(jnp.float32) - step_rate * update).astype(jnp.bfloat16),
        first_moment,
        second_moment,
    )


def body(
    hidden_in,
    value_grad,
    value_weight,
    norm_gain,
    owner_map,
    mat_first,
    mat_second,
    vec_first,
    vec_second,
    next_hidden,
):
    unit_rows, normed = normalize(hidden_in, norm_gain)
    weight_part = lax.dot_general(
        normed, value_grad, (((0,), (0,)), ((), ())), preferred_element_type=jnp.float32
    )
    input_grad = lax.dot_general(
        value_grad, value_weight, (((1,), (1,)), ((), ())), preferred_element_type=jnp.float32
    )
    gain_part = jnp.sum(input_grad * unit_rows, axis=0)
    share_rows = mat_first.shape[1]
    row_start = lax.axis_index("rep") * share_rows
    summed_weight, summed_gain = lax.psum((weight_part, gain_part), ("dp", "rep"))
    grad_weight = lax.dynamic_slice_in_dim(summed_weight, row_start, share_rows, 0)
    grad_gain = lax.dynamic_slice_in_dim(summed_gain, row_start, share_rows, 0)
    owner_weight = owner_map[0]
    owner_gain = owner_map[1]
    position = lax.axis_index("dp")
    own_weight = lax.dynamic_slice_in_dim(value_weight, row_start, share_rows, 0)
    own_gain = lax.dynamic_slice_in_dim(norm_gain, row_start, share_rows, 0)
    rows_new, first_weight, second_weight = adam_step(
        own_weight, grad_weight, mat_first[0], mat_second[0], learn_rate
    )
    gain_new, first_gain, second_gain = adam_step(
        own_gain, grad_gain, vec_first[0], vec_second[0], gain_rate
    )
    holds_weight = position == owner_weight
    holds_gain = position == owner_gain
    new_mat_first = jnp.where(holds_weight, first_weight, mat_first[0])[None]
    new_mat_second = jnp.where(holds_weight, second_weight, mat_second[0])[None]
    new_vec_first = jnp.where(holds_gain, first_gain, vec_first[0])[None]
    new_vec_second = jnp.where(holds_gain, second_gain, vec_second[0])[None]
    group_weight, group_gain = (
        lax.all_gather(rows_new, "rep", axis=0, tiled=True),
        lax.all_gather(gain_new, "rep", axis=0, tiled=True),
    )
    new_weight = spread(group_weight, "dp", owner_weight)
    new_gain = spread(group_gain, "dp", owner_gain)
    next_unit, next_normed = normalize(next_hidden, new_gain)
    next_values = jnp.dot(next_normed, new_weight, preferred_element_type=jnp.float32).astype(
        jnp.bfloat16
    )
    return (
        new_weight,
        new_gain,
        new_mat_first,
        new_mat_second,
        new_vec_first,
        new_vec_second,
        next_values,
    )


def solution(mesh):
    placed = (
        P(("dp", "rep"), None),
        P(("dp", "rep"), None),
        P(),
        P(),
        P(),
        P("dp", "rep", None),
        P("dp", "rep", None),
        P("dp", "rep"),
        P("dp", "rep"),
        P(("dp", "rep"), None),
    )
    return jax.shard_map(
        body,
        mesh=mesh,
        in_specs=placed,
        out_specs=(
            P(),
            P(),
            P("dp", "rep", None),
            P("dp", "rep", None),
            P("dp", "rep"),
            P("dp", "rep"),
            P(("dp", "rep"), None),
        ),
        check_vma=False,
    )
```

profile of v0, /device:TPU:2, one launch (start us, length us, event | category | flops | bytes accessed | tf_op | source)
XLA Modules:
  0.0 569.2 jit_solution(9446492294716992184)
XLA Ops:
  7.2 0.0 copy-start
  7.2 0.0 all-reduce.3.cloned.1.call-start
  7.2 0.0 copy-start.1
  7.2 0.9 convert_element_type.35
  8.1 4.5 fusion.4
  12.6 0.0 copy-done
  12.6 0.0 copy-done.1
  12.6 6.1 %fusion.10 = f32[4096,512]{1,0:T(8,128)} fusion(bf16[768,512]{1,0:T(8,128)(2,1)S(1)} %copy-done, bf16[768,4096]{1,0:T(8,128)(2,1)S(1)} %copy-done.1, f32[4096]{0:T(1024)S(1)} %convert_element_type.35, f32[768]{0:T(1024)S(1)} %add_rsqrt_fusion.1), kind=kOutput, calls=%fused_computation.13 | convolution fusion | flops 3233808384 | bytes 15485952 | tf_op jit(solution)/shard_map/dot_general | solution.py:52
  18.7 0.0 all-reduce.3.cloned.1.call-update
  18.7 0.0 all-gather.2.cloned.1.call-start
  18.8 0.6 copy-done.7
  19.4 0.6 fusion.26
  20.6 162.0 %all-reduce.3.cloned.1.call-done = f32[4096,512]{1,0:T(8,128)} async-done(((f32[4096,512]{1,0:T(8,128)}), f32[4096,512]{1,0:T(8,128)}) %all-reduce.3.cloned.1.call-update) | async-done | bytes 8388624 | tf_op jit(solution)/shard_map/psum | solution.py:61
  182.6 7.3 %fusion.17 = (f32[1,1024,512]{2,1,0:T(8,128)}, bf16[1024,512]{1,0:T(8,128)(2,1)}, f32[1,1024,512]{2,1,0:T(8,128)}) fusion(f32[1,1024,512]{2,1,0:T(8,128)S(1)} %copy-done.3, f32[4096,512]{1,0:T(8,128)} %all-reduce.3.cloned.1.call-done, s32[]{:T(128)S(6)} %select_n.47, pred[]{:T(512)S(6)} %eq.8, f32[1,1024,512]{2,1,0:T(8,128)} %param.15, ...), kind=kLoop, calls=%fused_computation.23 | loop fusion | flops 8912896 | bytes 12582917 | tf_op jit(solution)/shard_map/broadcast_in_dim | solution.py:78
  189.9 0.0 all-gather.2.cloned.1.call-update
  189.9 0.0 all-reduce.5.cloned.1.call-start
  189.9 37.6 %all-gather.2.cloned.1.call-done = bf16[4096,512]{1,0:T(8,128)(2,1)} async-done(((bf16[1024,512]{1,0:T(8,128)(2,1)}), bf16[4096,512]{1,0:T(8,128)(2,1)}) %all-gather.2.cloned.1.call-update) | async-done | bytes 4194320 | tf_op jit(solution)/shard_map/all_gather | solution.py:82
  227.5 2.3 broadcast_select_fusion
  229.8 0.0 all-reduce.5.cloned.1.call-update
  230.5 0.0 copy-start.5
  230.5 0.0 copy-start.6
  230.5 6.9 %fusion.3 = f32[4096]{0:T(1024)S(1)} fusion(bf16[768,4096]{1,0:T(8,128)(2,1)} %param.10, bf16[768,512]{1,0:T(8,128)(2,1)S(1)} %copy-done, bf16[4096,512]{1,0:T(8,128)(2,1)} %param.12, f32[768]{0:T(1024)S(1)} %add_rsqrt_fusion.1), kind=kOutput, calls=%fused_computation.7 | convolution fusion | flops 3233804288 | bytes 11291648 | tf_op jit(solution)/shard_map/dot_general | solution.py:55
  237.4 66.1 %psum.30 = f32[4096]{0:T(1024)S(1)} all-reduce(f32[4096]{0:T(1024)S(1)} %fusion.3), channel_id=1, replica_groups=mesh['dp'=32,'rep'=4] {'dp','rep'}, use_global_device_ids=true, to_apply=%region_4.5 | all-reduce | flops 4096 | bytes 32768 | tf_op jit(solution)/shard_map/psum | solution.py:61
  303.5 1.3 fusion.25
  304.7 6.7 %all_gather.7 = bf16[4096]{0:T(1024)(128)(2,1)S(1)} all-gather(bf16[1024]{0:T(1024)(128)(2,1)S(1)} %get-tuple-element.11), channel_id=1, replica_groups=mesh['dp'=32,'rep'=4] {'rep'}, dimensions={0}, use_global_device_ids=true | all-gather | bytes 10240 | tf_op jit(solution)/shard_map/all_gather | solution.py:83
  311.4 81.2 %psum.31 = bf16[4096]{0:T(1024)(128)(2,1)S(1)} all-reduce(bf16[4096]{0:T(1024)(128)(2,1)S(1)} %broadcast_select_fusion.1), channel_id=1, replica_groups=mesh['dp'=32,'rep'=4] {'dp'}, use_global_device_ids=true, to_apply=%region_5.6 | all-reduce | flops 4096 | bytes 16384 | tf_op jit(solution)/shard_map/psum | solution.py:18
  392.6 0.0 copy-start.4
  392.6 4.1 fusion.5
  396.8 155.4 %all-reduce.5.cloned.1.call-done = bf16[4096,512]{1,0:T(8,128)(2,1)} async-done(((bf16[4096,512]{1,0:T(8,128)(2,1)}), bf16[4096,512]{1,0:T(8,128)(2,1)}) %all-reduce.5.cloned.1.call-update) | async-done | bytes 4194320 | tf_op jit(solution)/shard_map/psum | solution.py:18
  552.2 8.5 %fusion.20 = bf16[768,512]{1,0:T(8,128)(2,1)} fusion(bf16[4096,512]{1,0:T(8,128)(2,1)} %all-reduce.5.cloned.1.call-done, bf16[768,4096]{1,0:T(8,128)(2,1)} %param.19, f32[4096]{0:T(1024)S(1)} %convert_element_type.41, f32[768]{0:T(1024)S(1)} %add_rsqrt_fusion), kind=kOutput, calls=%fused_computation.29 | convolution fusion | flops 3234201600 | bytes 11291648 | tf_op jit(solution)/shard_map/dot_general | solution.py:88
  560.7 0.0 copy-done.4
  560.7 2.0 copy.19
  (11 shorter events, 0.0 us)
Async XLA Ops:
  7.2 5.4 copy-start
  7.2 175.4 %all-reduce.3.cloned.1.call-start = ((), (), s32[]{:S(2)}) async-start(), calls=%async_computation | async-start | bytes 16777216 | tf_op jit(solution)/shard_map/psum | solution.py:61
  7.2 5.4 copy-start.1
  18.7 0.7 copy-start.7
  18.7 163.9 %copy-start.3 = (f32[1,1024,512]{2,1,0:T(8,128)S(1)}, f32[1,1024,512]{2,1,0:T(8,128)}, u32[]{:S(2)}) copy-start(f32[1,1024,512]{2,1,0:T(8,128)} %param.16) | copy-start | bytes 6291460
  18.7 208.8 %all-gather.2.cloned.1.call-start = ((), (), s32[]{:S(2)}) async-start(), calls=%async_computation.1 | async-start | bytes 5242880 | tf_op jit(solution)/shard_map/all_gather | solution.py:82
  189.9 362.3 %all-reduce.5.cloned.1.call-start = ((), (), s32[]{:S(2)}) async-start(), calls=%async_computation.2 | async-start | bytes 8388608 | tf_op jit(solution)/shard_map/psum | solution.py:18
  230.5 73.0 %copy-start.5 = (f32[1,1024]{1,0:T(1,128)S(1)}, f32[1,1024]{1,0:T(1,128)}, u32[]{:S(2)}) copy-start(f32[1,1024]{1,0:T(1,128)} %param.18) | copy-start | bytes 12292
  230.5 73.0 %copy-start.6 = (f32[1,1024]{1,0:T(1,128)S(1)}, f32[1,1024]{1,0:T(1,128)}, u32[]{:S(2)}) copy-start(f32[1,1024]{1,0:T(1,128)} %param.17) | copy-start | bytes 12292
  392.6 168.0 %copy-start.4 = (bf16[4096]{0:T(1024)(128)(2,1)}, bf16[4096]{0:T(1024)(128)(2,1)S(1)}, u32[]{:S(2)}) copy-start(bf16[4096]{0:T(1024)(128)(2,1)S(1)} %psum.31) | copy-start | bytes 24580
  552.2 8.5 %copy-start.2 = (bf16[4096,512]{1,0:T(8,128)(2,1)S(1)}, bf16[4096,512]{1,0:T(8,128)(2,1)}, u32[]{:S(2)}) copy-start(bf16[4096,512]{1,0:T(8,128)(2,1)} %all-reduce.5.cloned.1.call-done) | copy-start | bytes 12582916
Sparse Core Ops, SparseCore 0:
  18.9 163.7 all-reduce.2
  190.0 37.4 all-gather.1
  230.7 321.3 all-reduce.4
where the time goes:
time: 570 us; the launch traced here: 569 us
  waiting for transfers between devices  355 us (62%)
  blocking collectives  154 us (27%)
  matrix products  21.4 us (4%)
  other arithmetic  20.3 us (4%)
  between operations  15.2 us (3%)
    psum x1, waiting for transfers between devices, body(): lax.psum((weight_part, gain_part), ('dp', 'rep'))  162 us
    psum x1, waiting for transfers between devices, spread(): return lax.psum(block, axis)  155 us
    psum x1, blocking collectives, spread(): return lax.psum(block, axis)  81.2 us
    psum x1, blocking collectives, body(): lax.psum((weight_part, gain_part), ('dp', 'rep'))  66.1 us
    all_gather x1, waiting for transfers between devices, body(): lax.all_gather(rows_new, 'rep', axis=0, tiled=True)  37.6 us
  transfers between devices with their start and end apart: 3, of which 3 were waited for; matrix products, arithmetic and copies ran while one was open for 2% of the time, Pallas kernels for 0%

commit v1 on v0

v1 whole, which is shorter than its diff:
```python
import jax
import jax.numpy as jnp
from jax import lax
from jax.experimental import pallas as pl
from jax.experimental.pallas import tpu as pltpu
from jax.sharding import Mesh, PartitionSpec as P

norm_eps = 1e-05
adam_eps = 1e-08
beta_first = 0.9
beta_second = 0.95
learn_rate = 0.001
gain_rate = 0.02
fix_first = 1.0 - 0.9**10
fix_second = 1.0 - 0.95**10

D, KV, TOK = 4096, 512, 768
BLK = 512
AXES = ("y", "zl", "x", "zh", "c")
CHIPS = ("zh", "y", "zl", "x")
PARAMS = pltpu.CompilerParams(vmem_limit_bytes=50 * 1024 * 1024)
LINKS = (1, 8, 4, 3, 24, 36)
DP_LINKS = (1, 8, 4, 3, 24)


def pairs(mask, core=0):
    out = []
    for dev in range(128):
        chip = ((dev >> 1) & 1) * 32 + (dev >> 2)
        to = chip ^ mask
        out.append((dev, ((to & 31) << 2) + ((to >> 5) << 1) + ((dev & 1) ^ core)))
    return out


def swap(block, mask, core=0):
    return lax.ppermute(block, AXES, pairs(mask, core))


def adam_step(parameter, gradient, first_moment, second_moment, step_rate):
    first_moment = beta_first * first_moment + (1.0 - beta_first) * gradient
    second_moment = beta_second * second_moment + (1.0 - beta_second) * gradient * gradient
    update = first_moment / fix_first / (jnp.sqrt(second_moment / fix_second) + adam_eps)
    return (
        (parameter.astype(jnp.float32) - step_rate * update).astype(jnp.bfloat16),
        first_moment,
        second_moment,
    )


def fold(values):
    total = values[:, :128]
    for at in range(128, values.shape[1], 128):
        total = total + values[:, at : at + 128]
    return total


def grad_half(core, hid, gain, grad, inv, out):
    for at in range(4):
        start = ((at // 2) * 2 + core) * 1024 + (at % 2) * BLK
        cols = pl.ds(pl.multiple_of(start, BLK), BLK)
        unit = hid[:, cols].astype(jnp.float32) * inv
        normed = (unit * gain[:, cols].astype(jnp.float32)).astype(jnp.bfloat16)
        out[at // 2, pl.ds((at % 2) * BLK, BLK), :] = lax.dot_general(
            normed, grad, (((0,), (0,)), ((), ())), preferred_element_type=jnp.float32
        )


def send_kernel(core_ref, hid, gain, grad, out, inv_out):
    squares = jnp.zeros((TOK, 128), jnp.float32)
    for at in range(0, D, BLK):
        wide = hid[:, at : at + BLK].astype(jnp.float32)
        squares = squares + fold(wide * wide)
    mean = jnp.sum(squares, axis=1, keepdims=True) * (1.0 / D)
    inv = lax.rsqrt(mean + norm_eps)
    inv_out[...] = jnp.broadcast_to(inv, (TOK, 128))
    grad_half(1 - core_ref[0], hid, gain, grad[...], inv, out)


def keep_kernel(core_ref, hid, gain, grad, inv_ref, out):
    grad_half(core_ref[0], hid, gain, grad[...], inv_ref[:, :1], out)


def gain_kernel(hid, grad, weight, inv_ref, out):
    inv = inv_ref[:, :1]
    for at in range(0, D, BLK):
        back = lax.dot_general(
            grad[...],
            weight[at : at + BLK, :],
            (((1,), (1,)), ((), ())),
            preferred_element_type=jnp.float32,
        )
        unit = hid[:, at : at + BLK].astype(jnp.float32) * inv
        out[:, at : at + BLK] = jnp.sum(back * unit, axis=0, keepdims=True)


def norm_kernel(hid, gain, out):
    rows = hid.shape[0]
    squares = jnp.zeros((rows, 128), jnp.float32)
    for at in range(0, D, BLK):
        wide = hid[:, at : at + BLK].astype(jnp.float32)
        squares = squares + fold(wide * wide)
    inv = lax.rsqrt(jnp.sum(squares, axis=1, keepdims=True) * (1.0 / D) + norm_eps)
    for at in range(0, D, BLK):
        unit = hid[:, at : at + BLK].astype(jnp.float32) * inv
        scale = gain[:, at : at + BLK].astype(jnp.float32)
        out[:, at : at + BLK] = (unit * scale).astype(jnp.bfloat16)


def masks_of(order):
    masks = [0]
    for link in order:
        masks = masks + [m ^ link for m in masks]
    return masks


def turned(links, start):
    return links[start:] + links[:start]


PART_ORDER = tuple(turned(LINKS, p) for p in range(4))
SUM_ORDER = tuple(turned(DP_LINKS, 2 * p) for p in range(2))


def value_kernel(where_ref, *refs):
    own, other = refs[:4], refs[4:8]
    normed, weight, values = refs[8:]
    chip, core = where_ref[0], where_ref[1]
    for parts, side in ((own, core), (other, 1 - core)):
        for p in range(4):
            for j, mask in enumerate(masks_of(PART_ORDER[p])):
                to = lax.bitwise_xor(chip, mask)
                row = ((to >> 5) * 2 + side) * 1024 + lax.bitwise_and(to, 31) * 32
                weight[pl.ds(pl.multiple_of(row, 32), 32), p * 128 : p * 128 + 128] = parts[p][
                    j * 32 : j * 32 + 32, :
                ]
    values[...] = jnp.dot(
        normed[...], weight[...], preferred_element_type=jnp.float32
    ).astype(jnp.bfloat16)


def moment_kernel(where_ref, left, right, first, second, new_first, new_second):
    chip = where_ref[0]
    holds = where_ref[2] == 1
    new_first[...] = first[...]
    new_second[...] = second[...]

    @pl.when(holds)
    def _():
        for p, part in enumerate((left, right)):
            for j, mask in enumerate(masks_of(SUM_ORDER[p])):
                row = lax.bitwise_and(lax.bitwise_xor(chip, mask), 31) * 32
                at = (pl.ds(pl.multiple_of(row, 32), 32), slice(p * 256, p * 256 + 256))
                grad = part[j * 32 : j * 32 + 32, :]
                new_first[at] = beta_first * first[at] + (1.0 - beta_first) * grad
                new_second[at] = beta_second * second[at] + (1.0 - beta_second) * grad * grad


def vmem(n):
    return [pl.BlockSpec(memory_space=pltpu.VMEM)] * n


def smem():
    return [pl.BlockSpec(memory_space=pltpu.SMEM)]


def shape(dims, dtype):
    return jax.ShapeDtypeStruct(dims, dtype)


def body(
    hidden_in,
    value_grad,
    value_weight,
    norm_gain,
    owner_map,
    mat_first,
    mat_second,
    vec_first,
    vec_second,
    next_hidden,
):
    f32, bf16 = jnp.float32, jnp.bfloat16
    y, zl, x = lax.axis_index("y"), lax.axis_index("zl"), lax.axis_index("x")
    zh, core = lax.axis_index("zh"), lax.axis_index("c")
    place = y * 8 + zl * 4 + x
    rep = zh * 2 + core
    owner_weight, owner_gain = owner_map[0], owner_map[1]
    holds_weight = place == owner_weight
    holds_gain = place == owner_gain
    where = jnp.stack([zh * 32 + place, core, holds_weight.astype(jnp.int32)])
    core_at = core.reshape(1)
    gain_row = norm_gain.reshape(1, D)

    moments = jnp.stack([mat_first[0], mat_second[0]]).astype(jnp.float16)
    moments = moments.reshape(2, 4, 2, 4, 32, KV)

    def share(block, axis, at, source, unit):
        def pick(k):
            return lax.dynamic_index_in_dim(block, at ^ k, axis, keepdims=False)

        kept = pick(0)
        for k in range(1, block.shape[axis]):
            got = swap(pick(k), k * unit)
            kept = jnp.where((at ^ k) == source, got, kept)
        return kept

    moments = share(moments, 1, y, owner_weight >> 3, 8)
    moments = share(moments, 2, x, owner_weight & 3, 1)
    moments = share(moments, 1, zl, (owner_weight >> 2) & 1, 4)
    moments = moments.astype(f32)

    send, inv = pl.pallas_call(
        send_kernel,
        out_shape=(shape((2, 1024, KV), f32), shape((TOK, 128), f32)),
        in_specs=smem() + vmem(3),
        out_specs=tuple(vmem(2)),
        compiler_params=PARAMS,
    )(core_at, hidden_in, gain_row, value_grad)
    got = swap(send, 0, 1)
    keep = pl.pallas_call(
        keep_kernel,
        out_shape=shape((2, 1024, KV), f32),
        in_specs=smem() + vmem(4),
        out_specs=vmem(1)[0],
        compiler_params=PARAMS,
    )(core_at, hidden_in, gain_row, value_grad, inv)
    gain_part = pl.pallas_call(
        gain_kernel,
        out_shape=shape((1, D), f32),
        in_specs=vmem(4),
        out_specs=vmem(1)[0],
        compiler_params=PARAMS,
    )(hidden_in, value_grad, value_weight, inv)

    rows = jnp.arange(4)[:, None] == rep
    spread = [
        jnp.where(holds_gain & rows, vec[0][None, :], 0.0).reshape(32, 128)
        for vec in (vec_first, vec_second)
    ]
    sums = jnp.concatenate([gain_part.reshape(32, 128)] + spread)
    for mask in LINKS:
        sums = sums + swap(sums, mask)
    sums = sums + swap(sums, 0, 1)
    grad_gain, old_first, old_second = sums.reshape(3, D)
    new_gain, first_gain, second_gain = adam_step(
        norm_gain, grad_gain, old_first, old_second, gain_rate
    )
    first_rows = lax.dynamic_slice_in_dim(first_gain, rep * 1024, 1024)
    second_rows = lax.dynamic_slice_in_dim(second_gain, rep * 1024, 1024)
    new_vec_first = jnp.where(holds_gain, first_rows, vec_first[0])[None]
    new_vec_second = jnp.where(holds_gain, second_rows, vec_second[0])[None]

    chip_sum = (keep + got).reshape(64 * 32, KV)
    parts = lax.all_to_all(chip_sum, CHIPS, 0, 0, tiled=True)
    grad_rows = jnp.sum(parts.reshape(64, 32, KV), axis=0)

    own_rows = lax.dynamic_slice_in_dim(value_weight, rep * 1024 + place * 32, 32)
    weight_rows = adam_step(own_rows, grad_rows, moments[0], moments[1], learn_rate)[0]

    blocks = [weight_rows[:, p * 128 : p * 128 + 128] for p in range(4)]
    for step in range(6):
        blocks = [
            jnp.concatenate([block, swap(block, PART_ORDER[p][step])])
            for p, block in enumerate(blocks)
        ]
    others = [swap(block, 0, 1) for block in blocks]

    grads = [grad_rows[:, p * 256 : p * 256 + 256] for p in range(2)]
    for step in range(5):
        grads = [
            jnp.concatenate([block, swap(block, SUM_ORDER[p][step])])
            for p, block in enumerate(grads)
        ]

    next_normed = pl.pallas_call(
        norm_kernel,
        grid=(6,),
        out_shape=shape((TOK, D), bf16),
        in_specs=[
            pl.BlockSpec((128, D), lambda i: (i, 0)),
            pl.BlockSpec((1, D), lambda i: (0, 0)),
        ],
        out_specs=pl.BlockSpec((128, D), lambda i: (i, 0)),
        compiler_params=PARAMS,
    )(next_hidden, new_gain.reshape(1, D))

    new_weight, next_values = pl.pallas_call(
        value_kernel,
        out_shape=(shape((D, KV), bf16), shape((TOK, KV), bf16)),
        in_specs=smem() + vmem(9),
        out_specs=tuple(vmem(2)),
        compiler_params=PARAMS,
    )(where, *blocks, *others, next_normed)

    new_mat_first, new_mat_second = pl.pallas_call(
        moment_kernel,
        out_shape=(shape((1024, KV), f32), shape((1024, KV), f32)),
        in_specs=smem() + vmem(4),
        out_specs=tuple(vmem(2)),
        compiler_params=PARAMS,
    )(where, *grads, mat_first[0], mat_second[0])
    return (
        new_weight,
        new_gain,
        new_mat_first[None],
        new_mat_second[None],
        new_vec_first,
        new_vec_second,
        next_values,
    )


def solution(mesh):
    fine = Mesh(mesh.devices.reshape(4, 2, 4, 2, 2), AXES)
    dp, rep = ("y", "zl", "x"), ("zh", "c")
    tokens = P(AXES, None)
    return jax.shard_map(
        body,
        mesh=fine,
        in_specs=(
            tokens,
            tokens,
            P(),
            P(),
            P(),
            P(dp, rep, None),
            P(dp, rep, None),
            P(dp, rep),
            P(dp, rep),
            tokens,
        ),
        out_specs=(
            P(),
            P(),
            P(dp, rep, None),
            P(dp, rep, None),
            P(dp, rep),
            P(dp, rep),
            tokens,
        ),
        check_vma=False,
    )
```

time: 570 us -> 221 us (0.39)
  waiting for transfers between devices: 355 us -> 72.9 us
  blocking collectives: 154 us -> 0 us
  starting transfers between devices: 0.12 us -> 75.4 us
  Pallas kernels: 0 us -> 43.4 us
  matrix products: 21.4 us -> 0 us
  between operations: 15.2 us -> 4.73 us
    psum x2 -> x0, waiting for transfers between devices: 317 us -> none  [the longest x1 162 us: body(): lax.psum((weight_part, gain_part), ('dp', 'rep'))]
    psum x2 -> x0, blocking collectives: 147 us -> none  [the longest x1 81.2 us: spread(): return lax.psum(block, axis)]
    ppermute x0 -> x53, waiting for transfers between devices: none -> 72.9 us  [swap(): return lax.ppermute(block, AXES, pairs(mask, core))]
    ppermute x0 -> x53, starting transfers between devices: none -> 63.7 us  [swap(): return lax.ppermute(block, AXES, pairs(mask, core))]
    pallas_call x0 -> x6, Pallas kernels: none -> 43.4 us  [the longest x1 8.23 us: body(): pl.pallas_call(value_kernel, out_shape=(shape((D, KV), bf16), shape((TOK,...]
    all_gather x1 -> x0, waiting for transfers between devices: 37.6 us -> none  [body(): lax.all_gather(rows_new, 'rep', axis=0, tiled=True)]
    dot_general x3 -> x0, matrix products: 21.4 us -> none  [the longest x1 8.49 us: body(): jnp.dot(next_normed, new_weight, preferred_element_type=jnp.float32)]
    all_to_all x0 -> x1, starting transfers between devices: none -> 11.7 us  [body(): parts = lax.all_to_all(chip_sum, CHIPS, 0, 0, tiled=True)]
  transfers between devices with their start and end apart: 3 -> 54, of which waited for: 3 -> 15; matrix products, arithmetic and copies ran while one was open for 2% -> 4% of each run, Pallas kernels for 0% -> 13%
where the time goes in v1:
time: 221 us; the launch traced here: 217 us
  starting transfers between devices  75.4 us (34%)
  waiting for transfers between devices  72.9 us (33%)
  Pallas kernels  43.4 us (20%)
  other arithmetic  16.1 us (7%)
  between operations  4.73 us (2%)
  local copies, waits for them, and re-layouts  4.41 us (2%)
    ppermute x53, waiting for transfers between devices, swap(): return lax.ppermute(block, AXES, pairs(mask, core))  72.9 us
    ppermute x53, starting transfers between devices, swap(): return lax.ppermute(block, AXES, pairs(mask, core))  63.7 us
    all_to_all x1, starting transfers between devices, body(): parts = lax.all_to_all(chip_sum, CHIPS, 0, 0, tiled=True)  11.7 us
    pallas_call x1, Pallas kernels, body(): pl.pallas_call(value_kernel, out_shape=(shape((D, KV), bf16), shape((TOK,...  8.23 us
    pallas_call x1, Pallas kernels, body(): pl.pallas_call(norm_kernel, grid=(6,), out_shape=shape((TOK, D), bf16), i...  8.22 us
    pallas_call x1, Pallas kernels, body(): pl.pallas_call(send_kernel, out_shape=(shape((2, 1024, KV), f32), shape((...  8.07 us
    pallas_call x1, Pallas kernels, body(): pl.pallas_call(gain_kernel, out_shape=shape((1, D), f32), in_specs=vmem(4...  7.48 us
    pallas_call x1, Pallas kernels, body(): pl.pallas_call(keep_kernel, out_shape=shape((2, 1024, KV), f32), in_specs...  6.92 us
  transfers between devices with their start and end apart: 54, of which 15 were waited for; matrix products, arithmetic and copies ran while one was open for 4% of the time, Pallas kernels for 13%

profile of v1, /device:TPU:2, one launch (start us, length us, event | category | flops | bytes accessed | tf_op | source)
XLA Modules:
  0.0 217.0 jit_solution(11518225269027946902)
XLA Ops:
  2.5 8.1 %shard_map.153 = (f32[2,1024,512]{2,1,0:T(8,128)}, f32[768,128]{1,0:T(8,128)S(1)}) custom-call(s32[1]{0:T(128)} %bitcast.1.core_ref, bf16[768,4096]{1,0:T(8,128)(2,1)} %hid.6, bf16[1,4096]{1,0:T(2,128)(2,1)S(1)} %reshape.67.gain, bf16[768,512]{1,0:T(8,128)(2,1)S(1)} %copy-done), custom_call_target="tpu_custom_call" | custom-call | tf_op jit(solution)/shard_map/pallas_call | solution.py:212
  10.6 6.9 %shard_map.154 = f32[2,1024,512]{2,1,0:T(8,128)} custom-call(s32[1]{0:T(128)} %bitcast.1.core_ref, bf16[768,4096]{1,0:T(8,128)(2,1)} %hid.6, bf16[1,4096]{1,0:T(2,128)(2,1)S(1)} %reshape.67.gain, bf16[768,512]{1,0:T(8,128)(2,1)S(1)} %copy-done, f32[768,128]{1,0:T(8,128)S(1)} %get-tuple-element.13.inv_ref), custom_call_target="tpu_custom_call" | custom-call | tf_op jit(solution)/shard_map/pallas_call | solution.py:220
  17.9 5.2 %add.119 = f32[2,1024,512]{2,1,0:T(8,128)} add(f32[2,1024,512]{2,1,0:T(8,128)} %shard_map.154, f32[2,1024,512]{2,1,0:T(8,128)S(1)} %collective-permute-done.7) | non-fusion elementwise | flops 1048576 | bytes 12582912 | tf_op jit(solution)/shard_map/add | solution.py:253
  23.1 11.7 %all-to-all-start = ((f32[64,32,512]{2,1,0:T(8,128)}), f32[64,32,512]{2,1,0:T(8,128)}, u32[]{:S(2)}, u32[]{:S(2)}) async-start(f32[64,32,512]{2,1,0:T(8,128)} %bitcast.91), calls=%async_computation | async-start | bytes 8388608 | tf_op jit(solution)/shard_map/all_to_all | solution.py:254
  34.9 1.8 convert.9
  36.7 1.8 convert.10
  40.0 2.7 %collective-permute-start = (f16[2,2,4,32,512]{4,3,2,1,0:T(8,128)(2,1)}, f16[2,2,4,32,512]{4,3,2,1,0:T(8,128)(2,1)}, u32[]{:S(2)}, u32[]{:S(2)}) collective-permute-start(f16[2,2,4,32,512]{4,3,2,1,0:T(8,128)(2,1)} %get-tuple-element.23), channel_id=1, source_target_pairs={{0,96},{1,97},{2,98},{3,99},{4,100},{5,101},{6,102},{7,103},{8,104... | collective-permute-start | bytes 1572872 | tf_op jit(solution)/shard_map/ppermute | solution.py:36
  45.6 7.5 %shard_map.155 = f32[1,4096]{1,0:T(1,128)S(1)} custom-call(bf16[768,4096]{1,0:T(8,128)(2,1)} %hid.6, bf16[768,512]{1,0:T(8,128)(2,1)S(1)} %copy-done.1, bf16[4096,512]{1,0:T(8,128)(2,1)} %weight.1, f32[768,128]{1,0:T(8,128)S(1)} %get-tuple-element.13.inv_ref), custom_call_target="tpu_custom_call" | custom-call | tf_op jit(solution)/shard_map/pallas_call | solution.py:227
  53.7 31.1 %collective-permute-done.36 = f32[96,128]{1,0:T(8,128)S(1)} collective-permute-done((f32[96,128]{1,0:T(8,128)S(1)}, f32[96,128]{1,0:T(8,128)S(1)}, u32[]{:S(2)}, u32[]{:S(2)}) %collective-permute-start.36) | collective-permute-done | bytes 49184 | tf_op jit(solution)/shard_map/ppermute | solution.py:36
  84.8 24.1 %collective-permute-done.37 = f32[96,128]{1,0:T(8,128)S(1)} collective-permute-done((f32[96,128]{1,0:T(8,128)S(1)}, f32[96,128]{1,0:T(8,128)S(1)}, u32[]{:S(2)}, u32[]{:S(2)}) %collective-permute-start.37) | collective-permute-done | bytes 49184 | tf_op jit(solution)/shard_map/ppermute | solution.py:36
  108.9 2.9 %collective-permute-start.38 = (f32[96,128]{1,0:T(8,128)S(1)}, f32[96,128]{1,0:T(8,128)S(1)}, u32[]{:S(2)}, u32[]{:S(2)}) collective-permute-start(f32[96,128]{1,0:T(8,128)S(1)} %add.125), channel_id=1, source_target_pairs={{0,16},{1,17},{2,18},{3,19},{4,20},{5,21},{6,22},{7,23},{8,24},{9,... | collective-permute-start | bytes 147464 | tf_op jit(solution)/shard_map/ppermute | solution.py:36
  115.8 1.8 collective-permute-start.3
  117.6 2.7 %collective-permute-start.4 = (f16[2,2,32,512]{3,2,1,0:T(8,128)(2,1)S(1)}, f16[2,2,32,512]{3,2,1,0:T(8,128)(2,1)S(1)}, u32[]{:S(2)}, u32[]{:S(2)}) collective-permute-start(f16[2,2,32,512]{3,2,1,0:T(8,128)(2,1)S(1)} %get-tuple-element.26), channel_id=1, source_target_pairs={{0,8},{1,9},{2,10},{3,11},{4,12},{5,13},{6,14},{7,15},{8,0},{9,1},... | collective-permute-start | bytes 393224 | tf_op jit(solution)/shard_map/ppermute | solution.py:36
  120.3 1.9 collective-permute-start.40
  122.3 3.4 %collective-permute-done.40 = f32[96,128]{1,0:T(8,128)S(1)} collective-permute-done((f32[96,128]{1,0:T(8,128)S(1)}, f32[96,128]{1,0:T(8,128)S(1)}, u32[]{:S(2)}, u32[]{:S(2)}) %collective-permute-start.40) | collective-permute-done | bytes 49184 | tf_op jit(solution)/shard_map/ppermute | solution.py:36
  125.7 3.7 %collective-permute-start.41 = (f32[96,128]{1,0:T(8,128)S(1)}, f32[96,128]{1,0:T(8,128)S(1)}, u32[]{:S(2)}, u32[]{:S(2)}) collective-permute-start(f32[96,128]{1,0:T(8,128)S(1)} %add.128), channel_id=1, source_target_pairs={{0,18},{1,19},{2,16},{3,17},{4,22},{5,23},{6,20},{7,21},{8,26},{9,... | collective-permute-start | bytes 147464 | tf_op jit(solution)/shard_map/ppermute | solution.py:36
  133.0 3.3 %collective-permute-done.6 = f16[2,32,512]{2,1,0:T(8,128)(2,1)S(1)} collective-permute-done((f16[2,32,512]{2,1,0:T(8,128)(2,1)S(1)}, f16[2,32,512]{2,1,0:T(8,128)(2,1)S(1)}, u32[]{:S(2)}, u32[]{:S(2)}) %collective-permute-start.6) | collective-permute-done | bytes 65568 | tf_op jit(solution)/shard_map/ppermute | solution.py:36
  136.3 2.5 %reduce_sum.9 = f32[32,512]{1,0:T(8,128)S(1)} reduce(f32[64,32,512]{2,1,0:T(8,128)} %all-to-all-done, f32[]{:T(128)} %constant.85.clone.1), dimensions={0}, to_apply=%region_0.1 | reduce | flops 1032192 | bytes 4259844 | tf_op jit(solution)/shard_map/reduce_sum | solution.py:255
  139.6 2.1 collective-permute-start.8
  150.3 2.6 %collective-permute-start.27 = (bf16[64,128]{1,0:T(8,128)(2,1)S(1)}, bf16[64,128]{1,0:T(8,128)(2,1)S(1)}, u32[]{:S(2)}, u32[]{:S(2)}) collective-permute-start(bf16[64,128]{1,0:T(8,128)(2,1)S(1)} %pad_maximum_fusion.18), channel_id=1, source_target_pairs={{0,96},{1,97},{2,98},{3,99},{4,100},{5,101},{6,102},{7,103},{8,104... | collective-permute-start | bytes 49160 | tf_op jit(solution)/shard_map/ppermute | solution.py:36
  155.3 2.8 %collective-permute-start.22 = (bf16[128,128]{1,0:T(8,128)(2,1)S(1)}, bf16[128,128]{1,0:T(8,128)(2,1)S(1)}, u32[]{:S(2)}, u32[]{:S(2)}) collective-permute-start(bf16[128,128]{1,0:T(8,128)(2,1)S(1)} %pad_maximum_fusion.13), channel_id=1, source_target_pairs={{0,96},{1,97},{2,98},{3,99},{4,100},{5,101},{6,102},{7,103},{8,104... | collective-permute-start | bytes 98312 | tf_op jit(solution)/shard_map/ppermute | solution.py:36
  158.1 3.1 %collective-permute-start.28 = (bf16[128,128]{1,0:T(8,128)(2,1)S(1)}, bf16[128,128]{1,0:T(8,128)(2,1)S(1)}, u32[]{:S(2)}, u32[]{:S(2)}) collective-permute-start(bf16[128,128]{1,0:T(8,128)(2,1)S(1)} %pad_maximum_fusion.14), channel_id=1, source_target_pairs={{0,18},{1,19},{2,16},{3,17},{4,22},{5,23},{6,20},{7,21},{8,26},{9,... | collective-permute-start | bytes 98312 | tf_op jit(solution)/shard_map/ppermute | solution.py:36
  164.2 2.1 collective-permute-start.23
  168.7 2.7 %collective-permute-start.50 = (f32[128,256]{1,0:T(8,128)S(1)}, f32[128,256]{1,0:T(8,128)S(1)}, u32[]{:S(2)}, u32[]{:S(2)}) collective-permute-start(f32[128,256]{1,0:T(8,128)S(1)} %pad_maximum_fusion.3), channel_id=1, source_target_pairs={{0,96},{1,97},{2,98},{3,99},{4,100},{5,101},{6,102},{7,103},{8,104... | collective-permute-start | bytes 393224 | tf_op jit(solution)/shard_map/ppermute | solution.py:36
  172.2 2.7 %collective-permute-start.18 = (bf16[512,128]{1,0:T(8,128)(2,1)S(1)}, bf16[512,128]{1,0:T(8,128)(2,1)S(1)}, u32[]{:S(2)}, u32[]{:S(2)}) collective-permute-start(bf16[512,128]{1,0:T(8,128)(2,1)S(1)} %get-tuple-element.62), channel_id=1, source_target_pairs={{0,18},{1,19},{2,16},{3,17},{4,22},{5,23},{6,20},{7,21},{8,26},{9,... | collective-permute-start | bytes 393224 | tf_op jit(solution)/shard_map/ppermute | solution.py:36
  177.6 1.8 collective-permute-start.51
  184.0 2.1 collective-permute-start.47
  187.4 1.8 collective-permute-start.52
  191.7 2.7 %collective-permute-done.47 = f32[512,256]{1,0:T(8,128)S(1)} collective-permute-done((f32[512,256]{1,0:T(8,128)S(1)}, f32[512,256]{1,0:T(8,128)S(1)}, u32[]{:S(2)}, u32[]{:S(2)}) %collective-permute-start.47) | collective-permute-done | bytes 524320 | tf_op jit(solution)/shard_map/ppermute | solution.py:36
  194.5 8.2 %shard_map.156.refs_8_ = bf16[768,4096]{1,0:T(8,128)(2,1)} custom-call(bf16[768,4096]{1,0:T(8,128)(2,1)} %hid.7, bf16[1,4096]{1,0:T(2,128)(2,1)S(1)} %reshape.69.gain), custom_call_target="tpu_custom_call" | custom-call | tf_op jit(solution)/shard_map/pallas_call | solution.py:275
  203.4 4.5 %shard_map.158 = (f32[1024,512]{1,0:T(8,128)}, f32[1024,512]{1,0:T(8,128)}) custom-call(s32[3]{0:T(128)S(1)} %pad_add_fusion.where_ref, f32[1024,256]{1,0:T(8,128)S(1)} %constant_dynamic-update-slice_fusion.77.left, f32[1024,256]{1,0:T(8,128)S(1)} %constant_dynamic-update-slice_fusion.88.right, f32[1024,512]{1,0:T(8,128)} %bitcast.96, f32[1024,512]{1,0:T(8,128)} %bitcast.97), custom_call_target="tpu_custom_call" | custom-call | tf_op jit(solution)/shard_map/pallas_call | solution.py:295
  208.8 8.2 %shard_map.157 = (bf16[4096,512]{1,0:T(8,128)(2,1)}, bf16[768,512]{1,0:T(8,128)(2,1)}) custom-call(s32[3]{0:T(128)S(1)} %pad_add_fusion.where_ref, bf16[2048,128]{1,0:T(8,128)(2,1)S(1)} %constant_dynamic-update-slice_fusion.11.refs_0_, bf16[2048,128]{1,0:T(8,128)(2,1)S(1)} %constant_dynamic-update-slice_fusion.29.refs_1_, ...), custom_call_target="tpu_custom_call" | custom-call | tf_op jit(solution)/shard_map/pallas_call | solution.py:287
  (181 shorter events, 41.7 us)
Async XLA Ops:
  10.6 7.4 %collective-permute-start.7 = (f32[2,1024,512]{2,1,0:T(8,128)}, f32[2,1024,512]{2,1,0:T(8,128)S(1)}, u32[]{:S(2)}, u32[]{:S(2)}) collective-permute-start(f32[2,1024,512]{2,1,0:T(8,128)} %get-tuple-element.14), channel_id=1, source_target_pairs={{0,1},{1,0},{2,3},{3,2},{4,5},{5,4},{6,7},{7,6},{8,9},{9,8},{10,11... | collective-permute-start | bytes 12582920 | tf_op jit(solution)/shard_map/ppermute | solution.py:36
  23.1 113.1 %all-to-all-start = ((f32[64,32,512]{2,1,0:T(8,128)}), f32[64,32,512]{2,1,0:T(8,128)}, u32[]{:S(2)}, u32[]{:S(2)}) async-start(f32[64,32,512]{2,1,0:T(8,128)} %bitcast.91), calls=%async_computation | async-start | bytes 8388608 | tf_op jit(solution)/shard_map/all_to_all | solution.py:254
  40.0 74.3 %collective-permute-start = (f16[2,2,4,32,512]{4,3,2,1,0:T(8,128)(2,1)}, f16[2,2,4,32,512]{4,3,2,1,0:T(8,128)(2,1)}, u32[]{:S(2)}, u32[]{:S(2)}) collective-permute-start(f16[2,2,4,32,512]{4,3,2,1,0:T(8,128)(2,1)} %get-tuple-element.23), channel_id=1, source_target_pairs={{0,96},{1,97},{2,98},{3,99},{4,100},{5,101},{6,102},{7,103},{8,104... | collective-permute-start | bytes 1572872 | tf_op jit(solution)/shard_map/ppermute | solution.py:36
  42.7 71.5 %collective-permute-start.1 = (f16[2,2,4,32,512]{4,3,2,1,0:T(8,128)(2,1)}, f16[2,2,4,32,512]{4,3,2,1,0:T(8,128)(2,1)}, u32[]{:S(2)}, u32[]{:S(2)}) collective-permute-start(f16[2,2,4,32,512]{4,3,2,1,0:T(8,128)(2,1)} %get-tuple-element.24), channel_id=1, source_target_pairs={{0,64},{1,65},{2,66},{3,67},{4,68},{5,69},{6,70},{7,71},{8,72},{9,... | collective-permute-start | bytes 1572872 | tf_op jit(solution)/shard_map/ppermute | solution.py:36
  43.5 70.7 %collective-permute-start.2 = (f16[2,2,4,32,512]{4,3,2,1,0:T(8,128)(2,1)}, f16[2,2,4,32,512]{4,3,2,1,0:T(8,128)(2,1)}, u32[]{:S(2)}, u32[]{:S(2)}) collective-permute-start(f16[2,2,4,32,512]{4,3,2,1,0:T(8,128)(2,1)} %get-tuple-element.22), channel_id=1, source_target_pairs={{0,32},{1,33},{2,34},{3,35},{4,36},{5,37},{6,38},{7,39},{8,40},{9,... | collective-permute-start | bytes 1572872 | tf_op jit(solution)/shard_map/ppermute | solution.py:36
  53.0 31.7 %collective-permute-start.36 = (f32[96,128]{1,0:T(8,128)S(1)}, f32[96,128]{1,0:T(8,128)S(1)}, u32[]{:S(2)}, u32[]{:S(2)}) collective-permute-start(f32[96,128]{1,0:T(8,128)S(1)} %pad_maximum_fusion.10), channel_id=1, source_target_pairs={{0,4},{1,5},{2,6},{3,7},{4,0},{5,1},{6,2},{7,3},{8,12},{9,13},{10,... | collective-permute-start | bytes 147464 | tf_op jit(solution)/shard_map/ppermute | solution.py:36
  84.8 24.2 %collective-permute-start.37 = (f32[96,128]{1,0:T(8,128)S(1)}, f32[96,128]{1,0:T(8,128)S(1)}, u32[]{:S(2)}, u32[]{:S(2)}) collective-permute-start(f32[96,128]{1,0:T(8,128)S(1)} %fusion.30), channel_id=1, source_target_pairs={{0,32},{1,33},{2,34},{3,35},{4,36},{5,37},{6,38},{7,39},{8,40},{9,... | collective-permute-start | bytes 147464 | tf_op jit(solution)/shard_map/ppermute | solution.py:36
  115.8 15.7 %collective-permute-start.3 = (f16[2,2,32,512]{3,2,1,0:T(8,128)(2,1)S(1)}, f16[2,2,32,512]{3,2,1,0:T(8,128)(2,1)S(1)}, u32[]{:S(2)}, u32[]{:S(2)}) collective-permute-start(f16[2,2,32,512]{3,2,1,0:T(8,128)(2,1)S(1)} %get-tuple-element.27), channel_id=1, source_target_pairs={{0,12},{1,13},{2,14},{3,15},{4,8},{5,9},{6,10},{7,11},{8,4},{9,5},... | collective-permute-start | bytes 393224 | tf_op jit(solution)/shard_map/ppermute | solution.py:36
  117.6 13.9 %collective-permute-start.4 = (f16[2,2,32,512]{3,2,1,0:T(8,128)(2,1)S(1)}, f16[2,2,32,512]{3,2,1,0:T(8,128)(2,1)S(1)}, u32[]{:S(2)}, u32[]{:S(2)}) collective-permute-start(f16[2,2,32,512]{3,2,1,0:T(8,128)(2,1)S(1)} %get-tuple-element.26), channel_id=1, source_target_pairs={{0,8},{1,9},{2,10},{3,11},{4,12},{5,13},{6,14},{7,15},{8,0},{9,1},... | collective-permute-start | bytes 393224 | tf_op jit(solution)/shard_map/ppermute | solution.py:36
  120.3 11.3 %collective-permute-start.5 = (f16[2,2,32,512]{3,2,1,0:T(8,128)(2,1)S(1)}, f16[2,2,32,512]{3,2,1,0:T(8,128)(2,1)S(1)}, u32[]{:S(2)}, u32[]{:S(2)}) collective-permute-start(f16[2,2,32,512]{3,2,1,0:T(8,128)(2,1)S(1)} %get-tuple-element.25), channel_id=1, source_target_pairs={{0,4},{1,5},{2,6},{3,7},{4,0},{5,1},{6,2},{7,3},{8,12},{9,13},{10,... | collective-permute-start | bytes 393224 | tf_op jit(solution)/shard_map/ppermute | solution.py:36
  143.8 14.3 %collective-permute-start.43 = (f32[32,256]{1,0:T(8,128)S(1)}, f32[32,256]{1,0:T(8,128)S(1)}, u32[]{:S(2)}, u32[]{:S(2)}) collective-permute-start(f32[32,256]{1,0:T(8,128)S(1)} %get-tuple-element.51), channel_id=1, source_target_pairs={{0,4},{1,5},{2,6},{3,7},{4,0},{5,1},{6,2},{7,3},{8,12},{9,13},{10,... | collective-permute-start | bytes 98312 | tf_op jit(solution)/shard_map/ppermute | solution.py:36
  144.9 16.2 %collective-permute-start.48 = (f32[32,256]{1,0:T(8,128)S(1)}, f32[32,256]{1,0:T(8,128)S(1)}, u32[]{:S(2)}, u32[]{:S(2)}) collective-permute-start(f32[32,256]{1,0:T(8,128)S(1)} %get-tuple-element.50), channel_id=1, source_target_pairs={{0,16},{1,17},{2,18},{3,19},{4,20},{5,21},{6,22},{7,23},{8,24},{9,... | collective-permute-start | bytes 98312 | tf_op jit(solution)/shard_map/ppermute | solution.py:36
  153.0 8.3 %collective-permute-start.10 = (bf16[128,128]{1,0:T(8,128)(2,1)S(1)}, bf16[128,128]{1,0:T(8,128)(2,1)S(1)}, u32[]{:S(2)}, u32[]{:S(2)}) collective-permute-start(bf16[128,128]{1,0:T(8,128)(2,1)S(1)} %pad_maximum_fusion.11), channel_id=1, source_target_pairs={{0,16},{1,17},{2,18},{3,19},{4,20},{5,21},{6,22},{7,23},{8,24},{9,... | collective-permute-start | bytes 98312 | tf_op jit(solution)/shard_map/ppermute | solution.py:36
  153.6 9.3 %collective-permute-start.16 = (bf16[128,128]{1,0:T(8,128)(2,1)S(1)}, bf16[128,128]{1,0:T(8,128)(2,1)S(1)}, u32[]{:S(2)}, u32[]{:S(2)}) collective-permute-start(bf16[128,128]{1,0:T(8,128)(2,1)S(1)} %pad_maximum_fusion.12), channel_id=1, source_target_pairs={{0,12},{1,13},{2,14},{3,15},{4,8},{5,9},{6,10},{7,11},{8,4},{9,5},... | collective-permute-start | bytes 98312 | tf_op jit(solution)/shard_map/ppermute | solution.py:36
  155.3 8.3 %collective-permute-start.22 = (bf16[128,128]{1,0:T(8,128)(2,1)S(1)}, bf16[128,128]{1,0:T(8,128)(2,1)S(1)}, u32[]{:S(2)}, u32[]{:S(2)}) collective-permute-start(bf16[128,128]{1,0:T(8,128)(2,1)S(1)} %pad_maximum_fusion.13), channel_id=1, source_target_pairs={{0,96},{1,97},{2,98},{3,99},{4,100},{5,101},{6,102},{7,103},{8,104... | collective-permute-start | bytes 98312 | tf_op jit(solution)/shard_map/ppermute | solution.py:36
  163.6 7.8 %collective-permute-start.17 = (bf16[256,128]{1,0:T(8,128)(2,1)S(1)}, bf16[256,128]{1,0:T(8,128)(2,1)S(1)}, u32[]{:S(2)}, u32[]{:S(2)}) collective-permute-start(bf16[256,128]{1,0:T(8,128)(2,1)S(1)} %pad_maximum_fusion.5), channel_id=1, source_target_pairs={{0,96},{1,97},{2,98},{3,99},{4,100},{5,101},{6,102},{7,103},{8,104... | collective-permute-start | bytes 196616 | tf_op jit(solution)/shard_map/ppermute | solution.py:36
  164.2 8.0 %collective-permute-start.23 = (bf16[256,128]{1,0:T(8,128)(2,1)S(1)}, bf16[256,128]{1,0:T(8,128)(2,1)S(1)}, u32[]{:S(2)}, u32[]{:S(2)}) collective-permute-start(bf16[256,128]{1,0:T(8,128)(2,1)S(1)} %pad_maximum_fusion.6), channel_id=1, source_target_pairs={{0,18},{1,19},{2,16},{3,17},{4,22},{5,23},{6,20},{7,21},{8,26},{9,... | collective-permute-start | bytes 196616 | tf_op jit(solution)/shard_map/ppermute | solution.py:36
  166.3 8.5 %collective-permute-start.29 = (bf16[256,128]{1,0:T(8,128)(2,1)S(1)}, bf16[256,128]{1,0:T(8,128)(2,1)S(1)}, u32[]{:S(2)}, u32[]{:S(2)}) collective-permute-start(bf16[256,128]{1,0:T(8,128)(2,1)S(1)} %pad_maximum_fusion.7), channel_id=1, source_target_pairs={{0,4},{1,5},{2,6},{3,7},{4,0},{5,1},{6,2},{7,3},{8,12},{9,13},{10,... | collective-permute-start | bytes 196616 | tf_op jit(solution)/shard_map/ppermute | solution.py:36
  167.8 7.2 %collective-permute-start.45 = (f32[128,256]{1,0:T(8,128)S(1)}, f32[128,256]{1,0:T(8,128)S(1)}, u32[]{:S(2)}, u32[]{:S(2)}) collective-permute-start(f32[128,256]{1,0:T(8,128)S(1)} %pad_maximum_fusion.2), channel_id=1, source_target_pairs={{0,16},{1,17},{2,18},{3,19},{4,20},{5,21},{6,22},{7,23},{8,24},{9,... | collective-permute-start | bytes 393224 | tf_op jit(solution)/shard_map/ppermute | solution.py:36
  172.2 7.7 %collective-permute-start.18 = (bf16[512,128]{1,0:T(8,128)(2,1)S(1)}, bf16[512,128]{1,0:T(8,128)(2,1)S(1)}, u32[]{:S(2)}, u32[]{:S(2)}) collective-permute-start(bf16[512,128]{1,0:T(8,128)(2,1)S(1)} %get-tuple-element.62), channel_id=1, source_target_pairs={{0,18},{1,19},{2,16},{3,17},{4,22},{5,23},{6,20},{7,21},{8,26},{9,... | collective-permute-start | bytes 393224 | tf_op jit(solution)/shard_map/ppermute | solution.py:36
  175.0 7.6 %collective-permute-start.30 = (bf16[512,128]{1,0:T(8,128)(2,1)S(1)}, bf16[512,128]{1,0:T(8,128)(2,1)S(1)}, u32[]{:S(2)}, u32[]{:S(2)}) collective-permute-start(bf16[512,128]{1,0:T(8,128)(2,1)S(1)} %get-tuple-element.56), channel_id=1, source_target_pairs={{0,32},{1,33},{2,34},{3,35},{4,36},{5,37},{6,38},{7,39},{8,40},{9,... | collective-permute-start | bytes 393224 | tf_op jit(solution)/shard_map/ppermute | solution.py:36
  175.3 7.8 %collective-permute-start.46 = (f32[256,256]{1,0:T(8,128)S(1)}, f32[256,256]{1,0:T(8,128)S(1)}, u32[]{:S(2)}, u32[]{:S(2)}) collective-permute-start(f32[256,256]{1,0:T(8,128)S(1)} %pad_maximum_fusion), channel_id=1, source_target_pairs={{0,12},{1,13},{2,14},{3,15},{4,8},{5,9},{6,10},{7,11},{8,4},{9,5},... | collective-permute-start | bytes 786440 | tf_op jit(solution)/shard_map/ppermute | solution.py:36
  179.8 7.6 %collective-permute-start.13 = (bf16[1024,128]{1,0:T(8,128)(2,1)S(1)}, bf16[1024,128]{1,0:T(8,128)(2,1)S(1)}, u32[]{:S(2)}, u32[]{:S(2)}) collective-permute-start(bf16[1024,128]{1,0:T(8,128)(2,1)S(1)} %get-tuple-element.42), channel_id=1, source_target_pairs={{0,18},{1,19},{2,16},{3,17},{4,22},{5,23},{6,20},{7,21},{8,26},{9,... | collective-permute-start | bytes 786440 | tf_op jit(solution)/shard_map/ppermute | solution.py:36
  181.5 7.7 %collective-permute-start.19 = (bf16[1024,128]{1,0:T(8,128)(2,1)S(1)}, bf16[1024,128]{1,0:T(8,128)(2,1)S(1)}, u32[]{:S(2)}, u32[]{:S(2)}) collective-permute-start(bf16[1024,128]{1,0:T(8,128)(2,1)S(1)} %get-tuple-element.40), channel_id=1, source_target_pairs={{0,4},{1,5},{2,6},{3,7},{4,0},{5,1},{6,2},{7,3},{8,12},{9,13},{10,... | collective-permute-start | bytes 786440 | tf_op jit(solution)/shard_map/ppermute | solution.py:36
  182.6 8.4 %collective-permute-start.25 = (bf16[1024,128]{1,0:T(8,128)(2,1)S(1)}, bf16[1024,128]{1,0:T(8,128)(2,1)S(1)}, u32[]{:S(2)}, u32[]{:S(2)}) collective-permute-start(bf16[1024,128]{1,0:T(8,128)(2,1)S(1)} %get-tuple-element.38), channel_id=1, source_target_pairs={{0,32},{1,33},{2,34},{3,35},{4,36},{5,37},{6,38},{7,39},{8,40},{9,... | collective-permute-start | bytes 786440 | tf_op jit(solution)/shard_map/ppermute | solution.py:36
  183.2 7.8 %collective-permute-start.31 = (bf16[1024,128]{1,0:T(8,128)(2,1)S(1)}, bf16[1024,128]{1,0:T(8,128)(2,1)S(1)}, u32[]{:S(2)}, u32[]{:S(2)}) collective-permute-start(bf16[1024,128]{1,0:T(8,128)(2,1)S(1)} %get-tuple-element.36), channel_id=1, source_target_pairs={{0,16},{1,17},{2,18},{3,19},{4,20},{5,21},{6,22},{7,23},{8,24},{9,... | collective-permute-start | bytes 786440 | tf_op jit(solution)/shard_map/ppermute | solution.py:36
  184.0 10.4 %collective-permute-start.47 = (f32[512,256]{1,0:T(8,128)S(1)}, f32[512,256]{1,0:T(8,128)S(1)}, u32[]{:S(2)}, u32[]{:S(2)}) collective-permute-start(f32[512,256]{1,0:T(8,128)S(1)} %get-tuple-element.30), channel_id=1, source_target_pairs={{0,96},{1,97},{2,98},{3,99},{4,100},{5,101},{6,102},{7,103},{8,104... | collective-permute-start | bytes 1572872 | tf_op jit(solution)/shard_map/ppermute | solution.py:36
  187.4 15.9 %collective-permute-start.52 = (f32[512,256]{1,0:T(8,128)S(1)}, f32[512,256]{1,0:T(8,128)S(1)}, u32[]{:S(2)}, u32[]{:S(2)}) collective-permute-start(f32[512,256]{1,0:T(8,128)S(1)} %get-tuple-element.28), channel_id=1, source_target_pairs={{0,32},{1,33},{2,34},{3,35},{4,36},{5,37},{6,38},{7,39},{8,40},{9,... | collective-permute-start | bytes 1572872 | tf_op jit(solution)/shard_map/ppermute | solution.py:36
  189.2 18.7 %collective-permute-start.32 = (bf16[2048,128]{1,0:T(8,128)(2,1)S(1)}, bf16[2048,128]{1,0:T(8,128)(2,1)S(1)}, u32[]{:S(2)}, u32[]{:S(2)}) collective-permute-start(bf16[2048,128]{1,0:T(8,128)(2,1)S(1)} %constant_dynamic-update-slice_fusion.11.refs_0_), channel_id=1, source_target_pairs={{0,1},{1,0},{2,3},{3,2},{4,5},{5,4},{6,7},{7,6},{8,9},{9,8},{10,11... | collective-permute-start | bytes 1572872 | tf_op jit(solution)/shard_map/ppermute | solution.py:36
  191.0 16.9 %collective-permute-start.33 = (bf16[2048,128]{1,0:T(8,128)(2,1)S(1)}, bf16[2048,128]{1,0:T(8,128)(2,1)S(1)}, u32[]{:S(2)}, u32[]{:S(2)}) collective-permute-start(bf16[2048,128]{1,0:T(8,128)(2,1)S(1)} %constant_dynamic-update-slice_fusion.29.refs_1_), channel_id=1, source_target_pairs={{0,1},{1,0},{2,3},{3,2},{4,5},{5,4},{6,7},{7,6},{8,9},{9,8},{10,11... | collective-permute-start | bytes 1572872 | tf_op jit(solution)/shard_map/ppermute | solution.py:36
  191.0 16.9 %collective-permute-start.34 = (bf16[2048,128]{1,0:T(8,128)(2,1)S(1)}, bf16[2048,128]{1,0:T(8,128)(2,1)S(1)}, u32[]{:S(2)}, u32[]{:S(2)}) collective-permute-start(bf16[2048,128]{1,0:T(8,128)(2,1)S(1)} %constant_dynamic-update-slice_fusion.47.refs_2_), channel_id=1, source_target_pairs={{0,1},{1,0},{2,3},{3,2},{4,5},{5,4},{6,7},{7,6},{8,9},{9,8},{10,11... | collective-permute-start | bytes 1572872 | tf_op jit(solution)/shard_map/ppermute | solution.py:36
  194.4 13.5 %collective-permute-start.35 = (bf16[2048,128]{1,0:T(8,128)(2,1)S(1)}, bf16[2048,128]{1,0:T(8,128)(2,1)S(1)}, u32[]{:S(2)}, u32[]{:S(2)}) collective-permute-start(bf16[2048,128]{1,0:T(8,128)(2,1)S(1)} %constant_dynamic-update-slice_fusion.65.refs_3_), channel_id=1, source_target_pairs={{0,1},{1,0},{2,3},{3,2},{4,5},{5,4},{6,7},{7,6},{8,9},{9,8},{10,11... | collective-permute-start | bytes 1572872 | tf_op jit(solution)/shard_map/ppermute | solution.py:36
  (30 other events, 164.7 us)

commit v2 on v0

v2 whole, which is shorter than its diff:
```python
import jax
import jax.numpy as jnp
from jax import lax
from jax.experimental import pallas as pl
from jax.experimental.pallas import tpu as pltpu
from jax.sharding import Mesh, PartitionSpec as P

norm_eps = 1e-05
adam_eps = 1e-08
beta_first = 0.9
beta_second = 0.95
learn_rate = 0.001
gain_rate = 0.02
fix_first = 1.0 - 0.9**10
fix_second = 1.0 - 0.95**10

D, KV, TOK = 4096, 512, 768
BLK = 512
HALF = D // 2
ROWS = 144
SUM_ROWS = 136
EXTRA = 128
AXES = ("y", "zl", "x", "zh", "c")
CHIPS = ("zh", "y", "zl", "x")
DP = ("y", "zl", "x")
MOST = 149000.0
PARAMS = pltpu.CompilerParams(vmem_limit_bytes=50 * 1024 * 1024)
COST = pl.CostEstimate(flops=1, transcendentals=0, bytes_accessed=1)
f32, bf16, f16 = jnp.float32, jnp.bfloat16, jnp.float16


def pairs(mask, core=0):
    out = []
    for dev in range(128):
        chip = ((dev >> 1) & 1) * 32 + (dev >> 2)
        to = chip ^ mask
        out.append((dev, ((to & 31) << 2) + ((to >> 5) << 1) + ((dev & 1) ^ core)))
    return out


def swap(block, mask, core=0):
    return lax.ppermute(block, AXES, pairs(mask, core))


def adam_step(parameter, gradient, first_moment, second_moment, step_rate):
    first_moment = beta_first * first_moment + (1.0 - beta_first) * gradient
    second_moment = beta_second * second_moment + (1.0 - beta_second) * gradient * gradient
    update = first_moment / fix_first / (jnp.sqrt(second_moment / fix_second) + adam_eps)
    return (
        (parameter.astype(f32) - step_rate * update).astype(bf16),
        first_moment,
        second_moment,
    )


def fold(values):
    total = values[:, :128]
    for at in range(128, values.shape[1], 128):
        total = total + values[:, at : at + 128]
    return total


def inv_rms(hid):
    squares = jnp.zeros((hid.shape[0], 128), f32)
    for at in range(0, D, BLK):
        wide = hid[:, at : at + BLK].astype(f32)
        squares = squares + fold(wide * wide)
    mean = jnp.sum(squares, axis=1, keepdims=True) * (1.0 / D)
    return lax.rsqrt(mean + norm_eps)


def scale_kernel(core, hid, grad, out, theirs):
    most = jnp.max(jnp.abs(grad[...].astype(f32)), keepdims=True)
    lanes = lax.broadcasted_iota(jnp.int32, out.shape, 1)
    for half in range(2):
        start = pl.multiple_of((half * 2 + 1 - core[0]) * 1024, 1024)
        theirs[:, half * 1024 : half * 1024 + 1024] = hid[:, pl.ds(start, 1024)]
    out[...] = jnp.where(lanes < 64, inv_rms(hid), most)


def next_kernel(hid, out):
    out[...] = jnp.broadcast_to(inv_rms(hid), out.shape)


def products(hid, gain, grad, weight, inv):
    unit = hid[...].astype(f32) * inv[:, :1]
    normed = (unit * gain[...].astype(f32)).astype(bf16)
    part = lax.dot_general(
        normed, grad[...], (((0,), (0,)), ((), ())), preferred_element_type=f32
    )
    back = lax.dot_general(
        grad[...], weight[...], (((1,), (1,)), ((), ())), preferred_element_type=f32
    )
    return part, jnp.sum(back * unit, axis=0, keepdims=True)


def chip_kernel(core, hid, got_hid, gain, grad, got_grad, weight, inv, got_inv, out, after):
    after[...] = jnp.zeros_like(after)
    part, gain_part = products(hid, gain, grad, weight, inv)
    got_part, got_gain = products(got_hid, gain, got_grad, weight, got_inv)
    most = jnp.maximum(
        jnp.max(inv[:, 64:], keepdims=True), jnp.max(got_inv[:, 64:], keepdims=True)
    )
    power = jnp.floor(jnp.log(30000.0 / MOST / jnp.maximum(most, 1e-30)) * 1.4426950408889634)
    scale = jnp.exp(power * 0.6931471805599453)
    part = (part + got_part) * scale
    left = (gain_part + got_gain) * (scale * (1.0 / 64.0))
    pieces = []
    for step in (1.0, 256.0, 65536.0):
        rounded = left.astype(bf16).astype(f32)
        pieces.append(rounded * step)
        left = left - rounded
    for j in range(BLK // 32):
        for b in range(4):
            out[j, b * 32 : b * 32 + 32, :] = part[j * 32 : j * 32 + 32, b * 128 : b * 128 + 128]
        lanes = slice((j // 4) * 128, (j // 4) * 128 + 128)
        rows = [piece[:, lanes] for piece in pieces] + [jnp.broadcast_to(power, (1, 128))]
        rows.append(jnp.zeros((SUM_ROWS - EXTRA - 4, 128), f32))
        out[j, EXTRA:, :] = jnp.concatenate(rows)


def value_step(blocks, hid, inv, weight, gain_out):
    lanes = []
    for j in range(BLK // 32):
        for b in range(4):
            weight[j * 32 : j * 32 + 32, b * 128 : b * 128 + 128] = blocks[
                j, b * 32 : b * 32 + 32, :
            ]
    for j in range(0, BLK // 32, 4):
        rows = [blocks[j + k, EXTRA : EXTRA + 16, :].astype(f32)[:1] for k in range(4)]
        lanes.append((rows[0] + rows[1]) + (rows[2] + rows[3]))
    gain = jnp.concatenate(lanes, axis=1)
    gain_out[...] = gain
    unit = hid[...].astype(f32) * inv[:, :1]
    normed = (unit * gain).astype(bf16)
    return jnp.dot(normed, weight[...], preferred_element_type=f32)


def first_kernel(core, blocks, hid, inv, weight, gain, out):
    part = value_step(blocks, hid, inv, weight, gain)

    @pl.when(pl.program_id(0) == 0)
    def _():
        out[...] = part

    @pl.when(pl.program_id(0) > 0)
    def _():
        out[...] += part


def last_kernel(core, blocks, hid, inv, acc, started, gain_started, weight, gain, out, total):
    part = value_step(blocks, hid, inv, weight, gain)

    @pl.when(pl.program_id(0) == 0)
    def _():
        total[...] = acc[...] + part

    @pl.when(pl.program_id(0) > 0)
    def _():
        total[...] += part

    @pl.when(pl.program_id(0) == pl.num_programs(0) - 1)
    def _():
        out[...] = total[...].astype(bf16)


def shape(dims, dtype):
    return jax.ShapeDtypeStruct(dims, dtype)


def whole(dims):
    return pl.BlockSpec(dims, lambda i, *_: (0,) * len(dims))


def column(i, core):
    return ((i // 2) * 2 + core[0]) * 2 + i % 2


def call(kernel, grid, ins, outs, out_shape, scratch=(), prefetch=1, **more):
    return pl.pallas_call(
        kernel,
        grid_spec=pltpu.PrefetchScalarGridSpec(
            num_scalar_prefetch=prefetch,
            grid=(grid,),
            in_specs=ins,
            out_specs=outs,
            scratch_shapes=scratch,
        ),
        out_shape=out_shape,
        compiler_params=PARAMS,
        cost_estimate=COST,
        **more,
    )


def blocked(rows):
    return rows.reshape(32, 4, 128).transpose(1, 0, 2).reshape(128, 128)


def body(
    hidden_in,
    value_grad,
    value_weight,
    norm_gain,
    owner_map,
    mat_first,
    mat_second,
    vec_first,
    vec_second,
    next_hidden,
):
    y, zl, x = lax.axis_index("y"), lax.axis_index("zl"), lax.axis_index("x")
    zh, core = lax.axis_index("zh"), lax.axis_index("c")
    place = y * 8 + zl * 4 + x
    rep = zh * 2 + core
    owner_weight, owner_gain = owner_map[0], owner_map[1]
    holds_weight = place == owner_weight
    holds_gain = place == owner_gain
    core_at, other_at = core.reshape(1), (1 - core).reshape(1)
    gain_row = norm_gain.reshape(1, D)

    hid_spec = pl.BlockSpec((TOK, BLK), lambda i, core: (0, column(i, core)))
    inv, theirs = call(
        scale_kernel,
        3,
        [
            pl.BlockSpec((256, D), lambda i, core: (i, 0)),
            pl.BlockSpec((256, KV), lambda i, core: (i, 0)),
        ],
        (
            pl.BlockSpec((256, 128), lambda i, core: (i, 0)),
            pl.BlockSpec((256, HALF), lambda i, core: (i, 0)),
        ),
        (shape((TOK, 128), f32), shape((TOK, HALF), bf16)),
    )(core_at, hidden_in, value_grad)
    got_hid, got_grad, got_inv = swap(theirs, 0, 1), swap(value_grad, 0, 1), swap(inv, 0, 1)

    owners = (owner_weight, owner_gain)

    def share(picks, at, sources, unit, tie):
        kept = picks[0]
        is_mat = jnp.arange(kept.shape[0])[:, None] < kept.shape[0] - 2
        for k in range(1, len(picks)):
            got = swap(picks[k], k * unit)
            mine = jnp.where(is_mat, (at ^ k) == sources[0], (at ^ k) == sources[1])
            kept = jnp.where(mine, got, kept)
        return kept + tie

    def first_pick(k):
        mats = [
            lax.dynamic_slice_in_dim(m[0], (y ^ k) * 256, 256).astype(f16)
            for m in (mat_first, mat_second)
        ]
        vecs = jnp.concatenate(
            [lax.dynamic_slice_in_dim(v, (y ^ k) * 256, 256, 1) for v in (vec_first, vec_second)],
            axis=1,
        )
        high = lax.reduce_precision(vecs, 5, 10)
        return jnp.concatenate(
            mats + [high.astype(f16), ((vecs - high) * 2048.0).astype(f16)]
        )

    first_picks = [first_pick(k) for k in range(4)]

    side = pl.BlockSpec((1, BLK), lambda i, core: (0, column(i, core)))
    wide = pl.BlockSpec((BLK, KV), lambda i, core: (column(i, core), 0))
    scaled, after = call(
        chip_kernel,
        4,
        [
            hid_spec,
            pl.BlockSpec((TOK, BLK), lambda i, core: (0, i)),
            side,
            whole((TOK, KV)),
            whole((TOK, KV)),
            wide,
            whole((TOK, 128)),
            whole((TOK, 128)),
        ],
        (pl.BlockSpec((16, SUM_ROWS, 128), lambda i, core: (i, 0, 0)), whole((1, KV))),
        (shape((64, SUM_ROWS, 128), f32), shape((1, KV), f32)),
    )(core_at, hidden_in, got_hid, gain_row, value_grad, got_grad, value_weight, inv, got_inv)
    after = after.astype(f16)
    moments = share(first_picks, y, [o >> 3 for o in owners], 8, after)
    next_inv = pl.pallas_call(
        next_kernel,
        grid=(3,),
        in_specs=[pl.BlockSpec((256, D), lambda i: (i, 0))],
        out_specs=pl.BlockSpec((256, 128), lambda i: (i, 0)),
        out_shape=shape((TOK, 128), f32),
        compiler_params=PARAMS,
        cost_estimate=COST,
    )(lax.optimization_barrier((next_hidden, moments))[0])
    rows = moments[:-2].reshape(2, 8, 32, KV)

    def last_pick(k):
        got = lax.dynamic_index_in_dim(rows, (zl * 4 + x) ^ k, 1, keepdims=False)
        return jnp.concatenate([got.reshape(64, KV), moments[-2:]])

    last_picks = [last_pick(k) for k in range(8)]
    moments = share(last_picks, zl * 4 + x, [o & 7 for o in owners], 1, jnp.zeros((), f16))
    moments = moments.astype(f32)
    old_mats = moments[:64]
    old_vecs = lax.dynamic_slice_in_dim(
        moments[64:].reshape(2, 2, 256), (zl * 4 + x) * 32, 32, axis=2
    )
    old_vecs = old_vecs[0] + old_vecs[1] * (1.0 / 2048.0)

    parts = lax.all_to_all(scaled.astype(f16), CHIPS, 0, 0, tiled=True)
    power = parts[:, EXTRA + 3, :1].astype(f32)
    grad_rows = jnp.sum(parts[:, :EXTRA].astype(f32) * jnp.exp2(-power)[:, :, None], axis=0)
    terms = [parts[:, EXTRA + k].astype(f32) * (64.0 / 256.0**k) for k in range(3)]
    lanes = jnp.sum((terms[0] + terms[1] + terms[2]) * jnp.exp2(-power), axis=0)
    first_row = rep * 1024 + place * 32
    own_lanes = (jnp.arange(128) >> 5) == x
    grad_gain = lax.dynamic_slice_in_dim(lanes, x * 32, 32)

    own_rows = blocked(lax.dynamic_slice_in_dim(value_weight, first_row, 32))
    weight_rows = adam_step(
        own_rows, grad_rows, blocked(old_mats[:32]), blocked(old_mats[32:]), learn_rate
    )[0]
    gain_part = lax.dynamic_slice_in_dim(norm_gain, first_row, 32)
    gain_new = adam_step(gain_part, grad_gain, old_vecs[0], old_vecs[1], gain_rate)[0]
    gain_lanes = jnp.where(own_lanes, jnp.tile(gain_new, 4), jnp.zeros((), bf16))
    weight_rows = weight_rows + (next_inv[0, 0] * 0.0).astype(bf16)
    block = jnp.concatenate(
        [weight_rows, gain_lanes[None], jnp.zeros((ROWS - EXTRA - 1, 128), bf16)]
    )
    own = lax.all_to_all(
        jnp.broadcast_to(block[None], (64, ROWS, 128)), CHIPS, 0, 0, tiled=True
    )
    other = swap(own, 0, 1)

    lanes = jnp.where(own_lanes, lanes, 0.0)
    high = lax.reduce_precision(lanes, 8, 10)
    most = jnp.max(jnp.maximum(jnp.abs(grad_rows), jnp.abs(lanes)[None] * (1.0 / 64.0)))
    power = jnp.floor(jnp.log2(16384.0 / jnp.maximum(most, 1e-30)))
    scale = jnp.exp2(power)
    rows = [
        high * (scale * (1.0 / 64.0)),
        (lanes - high) * (scale * 32.0),
        jnp.full((256,), power),
    ]
    natural = (grad_rows * scale).reshape(4, 32, 128).transpose(1, 0, 2).reshape(32, KV)
    sent = jnp.concatenate([natural, jnp.concatenate(rows)[None]]).astype(f16)
    grads = lax.all_to_all(jnp.broadcast_to(sent[None], (32, 33, KV)), DP, 0, 0, tiled=True)

    value_ins = [
        pl.BlockSpec((16, ROWS, 128), lambda i, core: (i, 0, 0)),
        pl.BlockSpec((TOK, BLK), lambda i, core: (0, column(i, core))),
        whole((TOK, 128)),
    ]
    gain_spec = pl.BlockSpec((1, BLK), lambda i, core: (0, column(i, core)))
    any_spec = pl.BlockSpec(memory_space=pl.ANY)
    started, gain_started, acc = call(
        first_kernel,
        4,
        value_ins,
        (wide, gain_spec, whole((TOK, KV))),
        (shape((D, KV), bf16), shape((1, D), f32), shape((TOK, KV), f32)),
    )(core_at, own, next_hidden, next_inv)
    new_weight, new_gain, next_values = call(
        last_kernel,
        4,
        value_ins + [whole((TOK, KV)), any_spec, any_spec],
        (wide, gain_spec, whole((TOK, KV))),
        (shape((D, KV), bf16), shape((1, D), f32), shape((TOK, KV), bf16)),
        [pltpu.VMEM((TOK, KV), f32)],
        input_output_aliases={5: 0, 6: 1},
    )(other_at, other, next_hidden, next_inv, acc, started, gain_started)
    new_gain = new_gain.reshape(D).astype(bf16)

    grads, _ = lax.optimization_barrier((grads, next_values))
    ends = grads[:, 32].astype(f32)
    back = jnp.exp2(-ends[:, 256:384])
    gain_sums = (ends[:, :128] * 64.0 + ends[:, 128:256] * (1.0 / 32.0)) * back
    rep_gain = jnp.sum(gain_sums.reshape(8, 4, 128), axis=1).reshape(1, 1024)
    first_vec = beta_first * vec_first + (1.0 - beta_first) * rep_gain
    second_vec = beta_second * vec_second + (1.0 - beta_second) * rep_gain * rep_gain
    new_vec_first = jnp.where(holds_gain, first_vec, vec_first)
    new_vec_second = jnp.where(holds_gain, second_vec, vec_second)
    rep_rows = grads[:, :32].astype(f32) * back[:, :1, None]
    old_first, old_second = mat_first.reshape(32, 32, KV), mat_second.reshape(32, 32, KV)
    first_mat = beta_first * old_first + (1.0 - beta_first) * rep_rows
    second_mat = beta_second * old_second + (1.0 - beta_second) * rep_rows * rep_rows
    new_mat_first = jnp.where(holds_weight, first_mat, old_first).reshape(1, 1024, KV)
    new_mat_second = jnp.where(holds_weight, second_mat, old_second).reshape(1, 1024, KV)
    return (
        new_weight,
        new_gain,
        new_mat_first,
        new_mat_second,
        new_vec_first,
        new_vec_second,
        next_values,
    )


def solution(mesh):
    fine = Mesh(mesh.devices.reshape(4, 2, 4, 2, 2), AXES)
    rep = ("zh", "c")
    tokens = P(AXES, None)
    return jax.shard_map(
        body,
        mesh=fine,
        in_specs=(
            tokens,
            tokens,
            P(),
            P(),
            P(),
            P(DP, rep, None),
            P(DP, rep, None),
            P(DP, rep),
            P(DP, rep),
            tokens,
        ),
        out_specs=(
            P(),
            P(),
            P(DP, rep, None),
            P(DP, rep, None),
            P(DP, rep),
            P(DP, rep),
            tokens,
        ),
        check_vma=False,
    )
```

time: 570 us -> 163 us (0.29)
  waiting for transfers between devices: 355 us -> 23 us
  blocking collectives: 154 us -> 38.2 us
  Pallas kernels: 0 us -> 34.7 us
  starting transfers between devices: 0.12 us -> 32.5 us
  matrix products: 21.4 us -> 0 us
  between operations: 15.2 us -> 6.7 us
    psum x2 -> x0, waiting for transfers between devices: 317 us -> none  [the longest x1 162 us: body(): lax.psum((weight_part, gain_part), ('dp', 'rep'))]
    psum x2 -> x0, blocking collectives: 147 us -> none  [the longest x1 81.2 us: spread(): return lax.psum(block, axis)]
    all_to_all x0 -> x1, blocking collectives: none -> 38.2 us  [body(): lax.all_to_all(jnp.broadcast_to(block[None], (64, ROWS, 128)), CHIPS, 0,...]
    all_gather x1 -> x0, waiting for transfers between devices: 37.6 us -> none  [body(): lax.all_gather(rows_new, 'rep', axis=0, tiled=True)]
    pallas_call x0 -> x5, Pallas kernels: none -> 34.7 us  [the longest x1 11.3 us: body(): call(chip_kernel, 4, [hid_spec, pl.BlockSpec((TOK, BLK), lambda i, core:...]
    dot_general x3 -> x0, matrix products: 21.4 us -> none  [the longest x1 8.49 us: body(): jnp.dot(next_normed, new_weight, preferred_element_type=jnp.float32)]
    all_to_all x0 -> x2, starting transfers between devices: none -> 17.4 us  [the longest x1 11.6 us: body(): parts = lax.all_to_all(scaled.astype(f16), CHIPS, 0, 0, tiled=True)]
    ppermute x0 -> x14, waiting for transfers between devices: none -> 17.3 us  [swap(): return lax.ppermute(block, AXES, pairs(mask, core))]
  transfers between devices with their start and end apart: 3 -> 16, of which waited for: 3 -> 2; matrix products, arithmetic and copies ran while one was open for 2% -> 11% of each run, Pallas kernels for 0% -> 18%
where the time goes in v2:
time: 163 us; the launch traced here: 162 us
  blocking collectives  38.2 us (23%)
  Pallas kernels  34.7 us (21%)
  starting transfers between devices  32.5 us (20%)
  other arithmetic  23.1 us (14%)
  waiting for transfers between devices  23 us (14%)
  between operations  6.7 us (4%)
  local copies, waits for them, and re-layouts  3.86 us (2%)
    all_to_all x1, blocking collectives, body(): lax.all_to_all(jnp.broadcast_to(block[None], (64, ROWS, 128)), CHIPS, 0,...  38.2 us
    ppermute x14, waiting for transfers between devices, swap(): return lax.ppermute(block, AXES, pairs(mask, core))  17.3 us
    ppermute x14, starting transfers between devices, swap(): return lax.ppermute(block, AXES, pairs(mask, core))  15.2 us
    all_to_all x1, starting transfers between devices, body(): parts = lax.all_to_all(scaled.astype(f16), CHIPS, 0, 0, tiled=True)  11.6 us
    pallas_call x1, Pallas kernels, body(): call(chip_kernel, 4, [hid_spec, pl.BlockSpec((TOK, BLK), lambda i, core:...  11.3 us
    pallas_call x1, Pallas kernels, body(): call(last_kernel, 4, value_ins + [whole((TOK, KV)), any_spec, any_spec],...  6.81 us
    pallas_call x1, Pallas kernels, body(): call(first_kernel, 4, value_ins, (wide, gain_spec, whole((TOK, KV))), (sh...  6.26 us
    pallas_call x1, Pallas kernels, body(): call(scale_kernel, 3, [pl.BlockSpec((256, D), lambda i, core: (i, 0)), pl...  6.18 us
  transfers between devices with their start and end apart: 16, of which 2 were waited for; matrix products, arithmetic and copies ran while one was open for 11% of the time, Pallas kernels for 18%

profile of v2, /device:TPU:2, one launch (start us, length us, event | category | flops | bytes accessed | tf_op | source)
XLA Modules:
  0.0 162.1 jit_solution(3494968297527514424)
XLA Ops:
  0.7 6.2 %shard_map.153 = (f32[768,128]{1,0:T(8,128)S(1)}, bf16[768,2048]{1,0:T(8,128)(2,1)}) custom-call(s32[1]{0:T(128)} %bitcast.13.core, bf16[768,4096]{1,0:T(8,128)(2,1)} %hid.5, bf16[768,512]{1,0:T(8,128)(2,1)} %grad.3), custom_call_target="tpu_custom_call" | custom-call | flops 1 | bytes 1 | tf_op jit(solution)/shard_map/pallas_call | solution.py:223
  8.0 2.8 %fusion.11 = (f16[256,512]{1,0:T(8,128)(2,1)}, f16[256,512]{1,0:T(8,128)(2,1)S(1)}, f16[256,512]{1,0:T(8,128)(2,1)S(1)}, f16[256,512]{1,0:T(8,128)(2,1)S(1)}, f1...) fusion(f32[1,1024,512]{2,1,0:T(8,128)S(1)} %copy-done.1, ...), kind=kLoop, calls=%fused_computation.35 | loop fusion | flops 1048576 | bytes 6291472 | tf_op jit(solution)/shard_map/convert_element_type | solution.py:251
  10.8 1.0 pad_maximum_fusion
  11.8 3.0 %collective-permute-start = (f16[514,512]{1,0:T(8,128)(2,1)}, f16[514,512]{1,0:T(8,128)(2,1)}, u32[]{:S(2)}, u32[]{:S(2)}) collective-permute-start(f16[514,512]{1,0:T(8,128)(2,1)} %pad_maximum_fusion), channel_id=1, source_target_pairs={{0,96},{1,97},{2,98},{3,99},{4,100},{5,101},{6,102},{7,103},{8,104... | collective-permute-start | bytes 1579016 | tf_op jit(solution)/shard_map/ppermute | solution.py:42
  14.8 1.0 pad_maximum_fusion.1
  15.8 0.6 collective-permute-start.1
  16.5 1.0 pad_maximum_fusion.2
  18.0 11.3 %shard_map.154 = (f32[64,136,128]{2,1,0:T(8,128)}, f32[1,512]{1,0:T(1,128)S(1)}) custom-call(s32[1]{0:T(128)} %bitcast.13.core, bf16[768,4096]{1,0:T(8,128)(2,1)} %hid.5, bf16[768,2048]{1,0:T(8,128)(2,1)} %collective-permute-done.3.got_hid, bf16[1,4096]{1,0:T(2,128)(2,1)S(1)} %reshape.632.gain, bf16[768,512]{1,0:T(8,128)(2,1)} %grad.3, ...), custom_call_target="tpu_custom_call" | custom-call | flops 1 | bytes 1 | tf_op jit(solution)/shard_map/pallas_call | solution.py:267
  29.3 3.9 %convert_element_type.247 = f16[64,136,128]{2,1,0:T(8,128)(2,1)} convert(f32[64,136,128]{2,1,0:T(8,128)} %get-tuple-element.22) | non-fusion elementwise | flops 1114112 | bytes 6684672 | tf_op jit(solution)/shard_map/convert_element_type | solution.py:309
  33.2 11.6 %all-to-all-start = ((f16[64,136,128]{2,1,0:T(8,128)(2,1)}), f16[64,136,128]{2,1,0:T(8,128)(2,1)S(1)}, u32[]{:S(2)}, u32[]{:S(2)}) async-start(f16[64,136,128]{2,1,0:T(8,128)(2,1)} %convert_element_type.247), calls=%async_computation | async-start | bytes 4456448 | tf_op jit(solution)/shard_map/all_to_all | solution.py:309
  44.8 0.7 fusion.66
  48.3 0.8 dynamic-slice_convert_fusion.8
  49.4 2.0 %fusion.4 = f16[514,512]{1,0:T(8,128)(2,1)S(1)} fusion(f16[514,512]{1,0:T(8,128)(2,1)} %collective-permute-done, f16[514,512]{1,0:T(8,128)(2,1)} %collective-permute-done.1, f16[514,512]{1,0:T(8,128)(2,1)S(1)} %collective-permute-done.2, f16[1,512]{1,0:T(2,128)(2,1)S(1)} %get-tuple-element.71, f16[1,512]{1,0:T(2,128)(2,1)S(1)} %get-tuple-element.70, ...), kind=kLoop, calls=%fused_computation.12 | loop fusion | flops 1842176 | bytes 2634246 | tf_op jit(solution)/shard_map/add | solution.py:247
  51.8 2.4 %collective-permute-start.6 = (f16[66,512]{1,0:T(8,128)(2,1)S(1)}, f16[66,512]{1,0:T(8,128)(2,1)S(1)}, u32[]{:S(2)}, u32[]{:S(2)}) collective-permute-start(f16[66,512]{1,0:T(8,128)(2,1)S(1)} %get-tuple-element.69), channel_id=1, source_target_pairs={{0,28},{1,29},{2,30},{3,31},{4,24},{5,25},{6,26},{7,27},{8,20},{9,... | collective-permute-start | bytes 202760 | tf_op jit(solution)/shard_map/ppermute | solution.py:42
  54.2 1.1 collective-permute-start.7
  55.3 2.5 %collective-permute-start.8 = (f16[66,512]{1,0:T(8,128)(2,1)S(1)}, f16[66,512]{1,0:T(8,128)(2,1)S(1)}, u32[]{:S(2)}, u32[]{:S(2)}) collective-permute-start(f16[66,512]{1,0:T(8,128)(2,1)S(1)} %get-tuple-element.65), channel_id=1, source_target_pairs={{0,20},{1,21},{2,22},{3,23},{4,16},{5,17},{6,18},{7,19},{8,28},{9,... | collective-permute-start | bytes 202760 | tf_op jit(solution)/shard_map/ppermute | solution.py:42
  58.3 1.5 collective-permute-start.10
  59.8 17.2 %collective-permute-done.6 = f16[66,512]{1,0:T(8,128)(2,1)S(1)} collective-permute-done((f16[66,512]{1,0:T(8,128)(2,1)S(1)}, f16[66,512]{1,0:T(8,128)(2,1)S(1)}, u32[]{:S(2)}, u32[]{:S(2)}) %collective-permute-start.6) | collective-permute-done | bytes 67616 | tf_op jit(solution)/shard_map/ppermute | solution.py:42
  77.4 2.1 %collective-permute-start.12 = (f16[66,512]{1,0:T(8,128)(2,1)S(1)}, f16[66,512]{1,0:T(8,128)(2,1)S(1)}, u32[]{:S(2)}, u32[]{:S(2)}) collective-permute-start(f16[66,512]{1,0:T(8,128)(2,1)S(1)} %get-tuple-element.63), channel_id=1, source_target_pairs={{0,4},{1,5},{2,6},{3,7},{4,0},{5,1},{6,2},{7,3},{8,12},{9,13},{10,... | collective-permute-start | bytes 202760 | tf_op jit(solution)/shard_map/ppermute | solution.py:42
  79.6 4.2 %shard_map.155.inv = f32[768,128]{1,0:T(8,128)S(1)} custom-call(bf16[768,4096]{1,0:T(8,128)(2,1)} %hid.8), custom_call_target="tpu_custom_call" | custom-call | flops 1 | bytes 1 | tf_op jit(solution)/shard_map/pallas_call | solution.py:285
  86.1 0.8 subtract_convert_fusion
  87.9 38.2 %all_to_all.15.blocks = bf16[64,144,128]{2,1,0:T(8,128)(2,1)S(1)} all-to-all(bf16[64,144,128]{2,1,0:T(8,128)(2,1)S(1)} %broadcast_in_dim.185), channel_id=1, replica_groups=mesh['y'=4,'zl'=2,'x'=4,'zh'=2,'c'=2] {'zh','y','zl','x'}, dimensions={0} | all-to-all | bytes 4718592 | tf_op jit(solution)/shard_map/all_to_all | solution.py:329
  126.1 0.7 maximum_reduce_fusion
  127.8 1.1 broadcast_in_dim.188
  128.9 5.7 %all-to-all-start.2 = ((f16[32,33,512]{2,1,0:T(8,128)(2,1)}), f16[32,33,512]{2,1,0:T(8,128)(2,1)}, u32[]{:S(2)}, u32[]{:S(2)}) async-start(f16[32,33,512]{2,1,0:T(8,128)(2,1)} %broadcast_in_dim.188), calls=%async_computation.2 | async-start | bytes 2621440 | tf_op jit(solution)/shard_map/all_to_all | solution.py:346
  136.0 6.3 %shard_map.156 = (bf16[4096,512]{1,0:T(8,128)(2,1)}, f32[1,4096]{1,0:T(1,128)S(1)}, f32[768,512]{1,0:T(8,128)S(1)}) custom-call(s32[1]{0:T(128)} %bitcast.13.core, bf16[64,144,128]{2,1,0:T(8,128)(2,1)} %copy-done, bf16[768,4096]{1,0:T(8,128)(2,1)} %hid.8, f32[768,128]{1,0:T(8,128)S(1)} %shard_map.155.inv), custom_call_target="tpu_custom_call" | custom-call | flops 1 | bytes 1 | tf_op jit(solution)/shard_map/pallas_call | solution.py:355
  142.3 6.8 %shard_map.157 = (bf16[4096,512]{1,0:T(8,128)(2,1)}, f32[1,4096]{1,0:T(1,128)S(1)}, bf16[768,512]{1,0:T(8,128)(2,1)}) custom-call(s32[1]{0:T(128)} %bitcast.core, bf16[64,144,128]{2,1,0:T(8,128)(2,1)} %collective-permute-done.13.blocks, bf16[768,4096]{1,0:T(8,128)(2,1)} %hid.8, ...), custom_call_target="tpu_custom_call", output_to_operand_aliasing={{0}: (5, {}), {1}: (6, {})} | custom-call | flops 1 | bytes 1 | tf_op jit(solution)/shard_map/pallas_call | solution.py:362
  149.1 0.6 convert_reduce_fusion
  149.7 5.8 %all-to-all-done.2 = f16[32,33,512]{2,1,0:T(8,128)(2,1)} async-done(((f16[32,33,512]{2,1,0:T(8,128)(2,1)}), f16[32,33,512]{2,1,0:T(8,128)(2,1)}, u32[]{:S(2)}, u32[]{:S(2)}) %all-to-all-start.2) | async-done | bytes 1081376 | tf_op jit(solution)/shard_map/all_to_all | solution.py:346
  155.5 1.0 slice_convert_fusion
  156.7 0.6 broadcast_select_fusion
  157.3 4.8 %fusion.1 = (f32[32,32,512]{2,1,0:T(8,128)}, f32[32,32,512]{2,1,0:T(8,128)}) fusion(f32[32,32,512]{2,1,0:T(8,128)} %bitcast.99, f32[32]{0:T(128)S(1)} %slice_reduce_fusion, pred[]{:T(512)S(6)} %eq.108, f16[32,33,512]{2,1,0:T(8,128)(2,1)} %all-to-all-done.2, f32[32,32,512]{2,1,0:T(8,128)S(1)} %bitcast.98), kind=kLoop, calls=%fused_computation.3 | loop fusion | flops 5767168 | bytes 9437313 | tf_op jit(solution)/shard_map/jit(_where)/select_n | solution.py:387
  (96 shorter events, 6.0 us)
Async XLA Ops:
  0.6 6.7 %copy-start.6 = (f32[1,1024]{1,0:T(1,128)S(1)}, f32[1,1024]{1,0:T(1,128)}, u32[]{:S(2)}) copy-start(f32[1,1024]{1,0:T(1,128)} %param.18) | copy-start | bytes 12292
  0.6 6.7 %copy-start.7 = (f32[1,1024]{1,0:T(1,128)S(1)}, f32[1,1024]{1,0:T(1,128)}, u32[]{:S(2)}) copy-start(f32[1,1024]{1,0:T(1,128)} %param.17) | copy-start | bytes 12292
  0.7 7.3 %copy-start.1 = (f32[1,1024,512]{2,1,0:T(8,128)S(1)}, f32[1,1024,512]{2,1,0:T(8,128)}, u32[]{:S(2)}) copy-start(f32[1,1024,512]{2,1,0:T(8,128)} %param.15) | copy-start | bytes 6291460
  6.8 11.1 %collective-permute-start.3 = (bf16[768,2048]{1,0:T(8,128)(2,1)}, bf16[768,2048]{1,0:T(8,128)(2,1)}, u32[]{:S(2)}, u32[]{:S(2)}) collective-permute-start(bf16[768,2048]{1,0:T(8,128)(2,1)} %get-tuple-element.19), channel_id=1, source_target_pairs={{0,1},{1,0},{2,3},{3,2},{4,5},{5,4},{6,7},{7,6},{8,9},{9,8},{10,11... | collective-permute-start | bytes 9437192 | tf_op jit(solution)/shard_map/ppermute | solution.py:42
  6.8 11.1 %collective-permute-start.4 = (bf16[768,512]{1,0:T(8,128)(2,1)}, bf16[768,512]{1,0:T(8,128)(2,1)S(1)}, u32[]{:S(2)}, u32[]{:S(2)}) collective-permute-start(bf16[768,512]{1,0:T(8,128)(2,1)} %grad.3), channel_id=1, source_target_pairs={{0,1},{1,0},{2,3},{3,2},{4,5},{5,4},{6,7},{7,6},{8,9},{9,8},{10,11... | collective-permute-start | bytes 2359304 | tf_op jit(solution)/shard_map/ppermute | solution.py:42
  10.8 5.7 %copy-start.8 = (bf16[4096]{0:T(1024)(128)(2,1)S(1)}, bf16[4096]{0:T(1024)(128)(2,1)}, u32[]{:S(2)}) copy-start(bf16[4096]{0:T(1024)(128)(2,1)} %param.13) | copy-start | bytes 24580
  10.8 5.7 %copy-start.10 = (f32[1,256]{1,0:T(1,128)S(1)}, f32[1,256]{1,0:T(1,128)}, u32[]{:S(2)}) copy-start(f32[1,256]{1,0:T(1,128)} %get-tuple-element.88) | copy-start | bytes 3076
  10.8 5.7 %copy-start.3 = (f16[256,512]{1,0:T(8,128)(2,1)S(1)}, f16[256,512]{1,0:T(8,128)(2,1)}, u32[]{:S(2)}) copy-start(f16[256,512]{1,0:T(8,128)(2,1)} %get-tuple-element.84) | copy-start | bytes 786436
  11.8 37.5 %collective-permute-start = (f16[514,512]{1,0:T(8,128)(2,1)}, f16[514,512]{1,0:T(8,128)(2,1)}, u32[]{:S(2)}, u32[]{:S(2)}) collective-permute-start(f16[514,512]{1,0:T(8,128)(2,1)} %pad_maximum_fusion), channel_id=1, source_target_pairs={{0,96},{1,97},{2,98},{3,99},{4,100},{5,101},{6,102},{7,103},{8,104... | collective-permute-start | bytes 1579016 | tf_op jit(solution)/shard_map/ppermute | solution.py:42
  14.8 2.7 %collective-permute-start.5 = (f32[768,128]{1,0:T(8,128)S(1)}, f32[768,128]{1,0:T(8,128)S(1)}, u32[]{:S(2)}, u32[]{:S(2)}) collective-permute-start(f32[768,128]{1,0:T(8,128)S(1)} %get-tuple-element.20.inv), channel_id=1, source_target_pairs={{0,1},{1,0},{2,3},{3,2},{4,5},{5,4},{6,7},{7,6},{8,9},{9,8},{10,11... | collective-permute-start | bytes 1179656 | tf_op jit(solution)/shard_map/ppermute | solution.py:42
  15.8 33.5 %collective-permute-start.1 = (f16[514,512]{1,0:T(8,128)(2,1)}, f16[514,512]{1,0:T(8,128)(2,1)}, u32[]{:S(2)}, u32[]{:S(2)}) collective-permute-start(f16[514,512]{1,0:T(8,128)(2,1)} %pad_maximum_fusion.1), channel_id=1, source_target_pairs={{0,64},{1,65},{2,66},{3,67},{4,68},{5,69},{6,70},{7,71},{8,72},{9,... | collective-permute-start | bytes 1579016 | tf_op jit(solution)/shard_map/ppermute | solution.py:42
  17.5 31.8 %collective-permute-start.2 = (f16[514,512]{1,0:T(8,128)(2,1)}, f16[514,512]{1,0:T(8,128)(2,1)S(1)}, u32[]{:S(2)}, u32[]{:S(2)}) collective-permute-start(f16[514,512]{1,0:T(8,128)(2,1)} %pad_maximum_fusion.2), channel_id=1, source_target_pairs={{0,32},{1,33},{2,34},{3,35},{4,36},{5,37},{6,38},{7,39},{8,40},{9,... | collective-permute-start | bytes 1579016 | tf_op jit(solution)/shard_map/ppermute | solution.py:42
  33.2 11.7 %copy-start.11 = (s32[2]{0:T(128)S(1)}, s32[2]{0:T(128)}, u32[]{:S(2)}) copy-start(s32[2]{0:T(128)} %param.14) | copy-start | bytes 28
  33.2 16.1 %copy-start.9 = (f32[1,256]{1,0:T(1,128)S(1)}, f32[1,256]{1,0:T(1,128)}, u32[]{:S(2)}) copy-start(f32[1,256]{1,0:T(1,128)} %get-tuple-element.89) | copy-start | bytes 3076
  33.2 16.2 %copy-start.4 = (f16[256,512]{1,0:T(8,128)(2,1)S(1)}, f16[256,512]{1,0:T(8,128)(2,1)}, u32[]{:S(2)}) copy-start(f16[256,512]{1,0:T(8,128)(2,1)} %get-tuple-element.31) | copy-start | bytes 786436
  33.2 16.2 %copy-start.5 = (f16[256,512]{1,0:T(8,128)(2,1)S(1)}, f16[256,512]{1,0:T(8,128)(2,1)}, u32[]{:S(2)}) copy-start(f16[256,512]{1,0:T(8,128)(2,1)} %get-tuple-element.85) | copy-start | bytes 786436
  33.2 52.1 %all-to-all-start = ((f16[64,136,128]{2,1,0:T(8,128)(2,1)}), f16[64,136,128]{2,1,0:T(8,128)(2,1)S(1)}, u32[]{:S(2)}, u32[]{:S(2)}) async-start(f16[64,136,128]{2,1,0:T(8,128)(2,1)} %convert_element_type.247), calls=%async_computation | async-start | bytes 4456448 | tf_op jit(solution)/shard_map/all_to_all | solution.py:309
  51.8 25.2 %collective-permute-start.6 = (f16[66,512]{1,0:T(8,128)(2,1)S(1)}, f16[66,512]{1,0:T(8,128)(2,1)S(1)}, u32[]{:S(2)}, u32[]{:S(2)}) collective-permute-start(f16[66,512]{1,0:T(8,128)(2,1)S(1)} %get-tuple-element.69), channel_id=1, source_target_pairs={{0,28},{1,29},{2,30},{3,31},{4,24},{5,25},{6,26},{7,27},{8,20},{9,... | collective-permute-start | bytes 202760 | tf_op jit(solution)/shard_map/ppermute | solution.py:42
  54.2 23.2 %collective-permute-start.7 = (f16[66,512]{1,0:T(8,128)(2,1)S(1)}, f16[66,512]{1,0:T(8,128)(2,1)S(1)}, u32[]{:S(2)}, u32[]{:S(2)}) collective-permute-start(f16[66,512]{1,0:T(8,128)(2,1)S(1)} %get-tuple-element.64), channel_id=1, source_target_pairs={{0,24},{1,25},{2,26},{3,27},{4,28},{5,29},{6,30},{7,31},{8,16},{9,... | collective-permute-start | bytes 202760 | tf_op jit(solution)/shard_map/ppermute | solution.py:42
  55.3 29.7 %collective-permute-start.8 = (f16[66,512]{1,0:T(8,128)(2,1)S(1)}, f16[66,512]{1,0:T(8,128)(2,1)S(1)}, u32[]{:S(2)}, u32[]{:S(2)}) collective-permute-start(f16[66,512]{1,0:T(8,128)(2,1)S(1)} %get-tuple-element.65), channel_id=1, source_target_pairs={{0,20},{1,21},{2,22},{3,23},{4,16},{5,17},{6,18},{7,19},{8,28},{9,... | collective-permute-start | bytes 202760 | tf_op jit(solution)/shard_map/ppermute | solution.py:42
  57.7 27.2 %collective-permute-start.9 = (f16[66,512]{1,0:T(8,128)(2,1)S(1)}, f16[66,512]{1,0:T(8,128)(2,1)S(1)}, u32[]{:S(2)}, u32[]{:S(2)}) collective-permute-start(f16[66,512]{1,0:T(8,128)(2,1)S(1)} %get-tuple-element.66), channel_id=1, source_target_pairs={{0,16},{1,17},{2,18},{3,19},{4,20},{5,21},{6,22},{7,23},{8,24},{9,... | collective-permute-start | bytes 202760 | tf_op jit(solution)/shard_map/ppermute | solution.py:42
  58.3 26.7 %collective-permute-start.10 = (f16[66,512]{1,0:T(8,128)(2,1)S(1)}, f16[66,512]{1,0:T(8,128)(2,1)S(1)}, u32[]{:S(2)}, u32[]{:S(2)}) collective-permute-start(f16[66,512]{1,0:T(8,128)(2,1)S(1)} %get-tuple-element.67), channel_id=1, source_target_pairs={{0,12},{1,13},{2,14},{3,15},{4,8},{5,9},{6,10},{7,11},{8,4},{9,5},... | collective-permute-start | bytes 202760 | tf_op jit(solution)/shard_map/ppermute | solution.py:42
  77.0 8.0 %collective-permute-start.11 = (f16[66,512]{1,0:T(8,128)(2,1)S(1)}, f16[66,512]{1,0:T(8,128)(2,1)S(1)}, u32[]{:S(2)}, u32[]{:S(2)}) collective-permute-start(f16[66,512]{1,0:T(8,128)(2,1)S(1)} %get-tuple-element.68), channel_id=1, source_target_pairs={{0,8},{1,9},{2,10},{3,11},{4,12},{5,13},{6,14},{7,15},{8,0},{9,1},... | collective-permute-start | bytes 202760 | tf_op jit(solution)/shard_map/ppermute | solution.py:42
  77.4 7.5 %collective-permute-start.12 = (f16[66,512]{1,0:T(8,128)(2,1)S(1)}, f16[66,512]{1,0:T(8,128)(2,1)S(1)}, u32[]{:S(2)}, u32[]{:S(2)}) collective-permute-start(f16[66,512]{1,0:T(8,128)(2,1)S(1)} %get-tuple-element.63), channel_id=1, source_target_pairs={{0,4},{1,5},{2,6},{3,7},{4,0},{5,1},{6,2},{7,3},{8,12},{9,13},{10,... | collective-permute-start | bytes 202760 | tf_op jit(solution)/shard_map/ppermute | solution.py:42
  126.1 2.8 %copy-start = (bf16[64,144,128]{2,1,0:T(8,128)(2,1)}, bf16[64,144,128]{2,1,0:T(8,128)(2,1)S(1)}, u32[]{:S(2)}) copy-start(bf16[64,144,128]{2,1,0:T(8,128)(2,1)S(1)} %all_to_all.15.blocks) | copy-start | bytes 7077892
  126.1 16.2 %collective-permute-start.13 = (bf16[64,144,128]{2,1,0:T(8,128)(2,1)S(1)}, bf16[64,144,128]{2,1,0:T(8,128)(2,1)}, u32[]{:S(2)}, u32[]{:S(2)}) collective-permute-start(bf16[64,144,128]{2,1,0:T(8,128)(2,1)S(1)} %all_to_all.15.blocks), channel_id=1, source_target_pairs={{0,1},{1,0},{2,3},{3,2},{4,5},{5,4},{6,7},{7,6},{8,9},{9,8},{10,11... | collective-permute-start | bytes 7077896 | tf_op jit(solution)/shard_map/ppermute | solution.py:42
  128.9 26.6 %all-to-all-start.2 = ((f16[32,33,512]{2,1,0:T(8,128)(2,1)}), f16[32,33,512]{2,1,0:T(8,128)(2,1)}, u32[]{:S(2)}, u32[]{:S(2)}) async-start(f16[32,33,512]{2,1,0:T(8,128)(2,1)} %broadcast_in_dim.188), calls=%async_computation.2 | async-start | bytes 2621440 | tf_op jit(solution)/shard_map/all_to_all | solution.py:346
  142.3 15.0 %copy-start.2 = (f32[1,1024,512]{2,1,0:T(8,128)S(1)}, f32[1,1024,512]{2,1,0:T(8,128)}, u32[]{:S(2)}) copy-start(f32[1,1024,512]{2,1,0:T(8,128)} %param.15) | copy-start | bytes 6291460

commit v3 on v2

--- a/solution.py
+++ b/solution.py
@@ -94,7 +94,7 @@
     return part, jnp.sum(back * unit, axis=0, keepdims=True)
 
 
-def chip_kernel(core, hid, got_hid, gain, grad, got_grad, weight, inv, got_inv, out, after):
+def chip_kernel(core, hid, got_hid, gain, grad, got_grad, weight, inv, got_inv, firsts, seconds, out, after):
     after[...] = jnp.zeros_like(after)
     part, gain_part = products(hid, gain, grad, weight, inv)
     got_part, got_gain = products(got_hid, gain, got_grad, weight, got_inv)
@@ -110,12 +110,17 @@
         rounded = left.astype(bf16).astype(f32)
         pieces.append(rounded * step)
         left = left - rounded
+    vecs = []
+    for vec in (firsts, seconds):
+        whole_part = vec[...] * 4096.0
+        rounded = whole_part.astype(bf16).astype(f32)
+        vecs += [rounded, (whole_part - rounded) * 256.0]
     for j in range(BLK // 32):
         for b in range(4):
             out[j, b * 32 : b * 32 + 32, :] = part[j * 32 : j * 32 + 32, b * 128 : b * 128 + 128]
         lanes = slice((j // 4) * 128, (j // 4) * 128 + 128)
         rows = [piece[:, lanes] for piece in pieces] + [jnp.broadcast_to(power, (1, 128))]
-        rows.append(jnp.zeros((SUM_ROWS - EXTRA - 4, 128), f32))
+        rows += [vec[:, lanes] for vec in vecs]
         out[j, EXTRA:, :] = jnp.concatenate(rows)
 
 
@@ -222,42 +227,31 @@
     hid_spec = pl.BlockSpec((TOK, BLK), lambda i, core: (0, column(i, core)))
     inv, theirs = call(
         scale_kernel,
-        3,
+        2,
         [
-            pl.BlockSpec((256, D), lambda i, core: (i, 0)),
-            pl.BlockSpec((256, KV), lambda i, core: (i, 0)),
+            pl.BlockSpec((384, D), lambda i, core: (i, 0)),
+            pl.BlockSpec((384, KV), lambda i, core: (i, 0)),
         ],
         (
-            pl.BlockSpec((256, 128), lambda i, core: (i, 0)),
-            pl.BlockSpec((256, HALF), lambda i, core: (i, 0)),
+            pl.BlockSpec((384, 128), lambda i, core: (i, 0)),
+            pl.BlockSpec((384, HALF), lambda i, core: (i, 0)),
         ),
         (shape((TOK, 128), f32), shape((TOK, HALF), bf16)),
     )(core_at, hidden_in, value_grad)
     got_hid, got_grad, got_inv = swap(theirs, 0, 1), swap(value_grad, 0, 1), swap(inv, 0, 1)
 
-    owners = (owner_weight, owner_gain)
-
-    def share(picks, at, sources, unit, tie):
+    def share(picks, at, source, unit):
         kept = picks[0]
-        is_mat = jnp.arange(kept.shape[0])[:, None] < kept.shape[0] - 2
         for k in range(1, len(picks)):
-            got = swap(picks[k], k * unit)
-            mine = jnp.where(is_mat, (at ^ k) == sources[0], (at ^ k) == sources[1])
-            kept = jnp.where(mine, got, kept)
-        return kept + tie
+            kept = jnp.where((at ^ k) == source, swap(picks[k], k * unit), kept)
+        return kept
 
     def first_pick(k):
-        mats = [
-            lax.dynamic_slice_in_dim(m[0], (y ^ k) * 256, 256).astype(f16)
-            for m in (mat_first, mat_second)
-        ]
-        vecs = jnp.concatenate(
-            [lax.dynamic_slice_in_dim(v, (y ^ k) * 256, 256, 1) for v in (vec_first, vec_second)],
-            axis=1,
-        )
-        high = lax.reduce_precision(vecs, 5, 10)
         return jnp.concatenate(
-            mats + [high.astype(f16), ((vecs - high) * 2048.0).astype(f16)]
+            [
+                lax.dynamic_slice_in_dim(m[0], (y ^ k) * 256, 256).astype(f16)
+                for m in (mat_first, mat_second)
+            ]
         )
 
     first_picks = [first_pick(k) for k in range(4)]
@@ -276,12 +270,25 @@
             wide,
             whole((TOK, 128)),
             whole((TOK, 128)),
+            pl.BlockSpec((1, BLK), lambda i, core: (0, i % 2)),
+            pl.BlockSpec((1, BLK), lambda i, core: (0, i % 2)),
         ],
         (pl.BlockSpec((16, SUM_ROWS, 128), lambda i, core: (i, 0, 0)), whole((1, KV))),
         (shape((64, SUM_ROWS, 128), f32), shape((1, KV), f32)),
-    )(core_at, hidden_in, got_hid, gain_row, value_grad, got_grad, value_weight, inv, got_inv)
-    after = after.astype(f16)
-    moments = share(first_picks, y, [o >> 3 for o in owners], 8, after)
+    )(
+        core_at,
+        hidden_in,
+        got_hid,
+        gain_row,
+        value_grad,
+        got_grad,
+        value_weight,
+        inv,
+        got_inv,
+        vec_first,
+        vec_second,
+    )
+    moments = share(first_picks, y, owner_weight >> 3, 8) + after.astype(f16)
     next_inv = pl.pallas_call(
         next_kernel,
         grid=(3,),
@@ -289,61 +296,67 @@
         out_specs=pl.BlockSpec((256, 128), lambda i: (i, 0)),
         out_shape=shape((TOK, 128), f32),
         compiler_params=PARAMS,
-        cost_estimate=COST,
+        cost_estimate=pl.CostEstimate(flops=17 * 10**9, transcendentals=0, bytes_accessed=1),
     )(lax.optimization_barrier((next_hidden, moments))[0])
-    rows = moments[:-2].reshape(2, 8, 32, KV)
-
-    def last_pick(k):
-        got = lax.dynamic_index_in_dim(rows, (zl * 4 + x) ^ k, 1, keepdims=False)
-        return jnp.concatenate([got.reshape(64, KV), moments[-2:]])
-
-    last_picks = [last_pick(k) for k in range(8)]
-    moments = share(last_picks, zl * 4 + x, [o & 7 for o in owners], 1, jnp.zeros((), f16))
-    moments = moments.astype(f32)
-    old_mats = moments[:64]
-    old_vecs = lax.dynamic_slice_in_dim(
-        moments[64:].reshape(2, 2, 256), (zl * 4 + x) * 32, 32, axis=2
-    )
-    old_vecs = old_vecs[0] + old_vecs[1] * (1.0 / 2048.0)
+    moments, next_inv = lax.optimization_barrier((moments, next_inv))
+    moments = moments.reshape(2, 8, 32, KV)
+    last_picks = [
+        lax.dynamic_index_in_dim(moments, (zl * 4 + x) ^ k, 1, keepdims=False).reshape(64, KV)
+        for k in range(8)
+    ]
+    arrived = [swap(last_picks[k], k) for k in range(1, 8)]
 
     parts = lax.all_to_all(scaled.astype(f16), CHIPS, 0, 0, tiled=True)
-    power = parts[:, EXTRA + 3, :1].astype(f32)
-    grad_rows = jnp.sum(parts[:, :EXTRA].astype(f32) * jnp.exp2(-power)[:, :, None], axis=0)
-    terms = [parts[:, EXTRA + k].astype(f32) * (64.0 / 256.0**k) for k in range(3)]
-    lanes = jnp.sum((terms[0] + terms[1] + terms[2]) * jnp.exp2(-power), axis=0)
+    parts, early = lax.optimization_barrier((parts, arrived[:5]))
+    arrived = early + arrived[5:]
+    back = jnp.exp2(-parts[:, EXTRA + 3, :1].astype(f32))
+    summed = jnp.sum(parts.astype(f32) * back[:, :, None], axis=0)
+    grad_rows = summed[:EXTRA]
+    lanes = summed[EXTRA] * 64.0 + summed[EXTRA + 1] * (64.0 / 256.0)
+    lanes = lanes + summed[EXTRA + 2] * (64.0 / 65536.0)
+    own_lanes = (jnp.arange(128) >> 5) == x
+    lanes = jnp.where(own_lanes, lanes, 0.0)
+    high = lax.reduce_precision(lanes, 8, 10)
+    most = jnp.maximum(jnp.max(jnp.abs(grad_rows), axis=0), jnp.abs(lanes) * (1.0 / 64.0))
+    power = jnp.floor(jnp.log2(16384.0 / jnp.maximum(most, 1e-30)))
+    scale = jnp.exp2(power)
+    gain_row = [high * (scale * (1.0 / 64.0)), (lanes - high) * (scale * 32.0)]
+    gain_row = jnp.concatenate(gain_row + [jnp.zeros((256,), f32)])
+    natural = (grad_rows * scale).reshape(4, 32, 128).transpose(1, 0, 2).reshape(32, KV)
+    sent = jnp.concatenate([natural, gain_row[None], jnp.tile(power, 4)[None]]).astype(f16)
+    sent = jnp.broadcast_to(sent[None], (32, 34, KV))
+    old_vecs = lax.dynamic_index_in_dim(parts, zh * 32 + owner_gain, 0, keepdims=False)
+    old_vecs = old_vecs[EXTRA + 4 :].astype(f32) * (1.0 / 4096.0)
+    old_vecs = lax.dynamic_slice_in_dim(old_vecs, x * 32, 32, 1)
+    old_vecs = old_vecs[0::2] + old_vecs[1::2] * (1.0 / 256.0)
     first_row = rep * 1024 + place * 32
-    own_lanes = (jnp.arange(128) >> 5) == x
     grad_gain = lax.dynamic_slice_in_dim(lanes, x * 32, 32)
+
+    gain_part = lax.dynamic_slice_in_dim(norm_gain, first_row, 32)
+    gain_new = adam_step(gain_part, grad_gain, old_vecs[0], old_vecs[1], gain_rate)[0]
+    gain_lanes = jnp.where(own_lanes, jnp.tile(gain_new, 4), jnp.zeros((), bf16))
+    arrived, grad_rows, sent, gain_lanes = lax.optimization_barrier(
+        (arrived, grad_rows, sent, gain_lanes)
+    )
+    old_mats = last_picks[0]
+    for k in range(1, 8):
+        source = (zl * 4 + x) ^ k == (owner_weight & 7)
+        old_mats = jnp.where(source, arrived[k - 1], old_mats)
+    old_mats = old_mats.astype(f32)
 
     own_rows = blocked(lax.dynamic_slice_in_dim(value_weight, first_row, 32))
     weight_rows = adam_step(
         own_rows, grad_rows, blocked(old_mats[:32]), blocked(old_mats[32:]), learn_rate
     )[0]
-    gain_part = lax.dynamic_slice_in_dim(norm_gain, first_row, 32)
-    gain_new = adam_step(gain_part, grad_gain, old_vecs[0], old_vecs[1], gain_rate)[0]
-    gain_lanes = jnp.where(own_lanes, jnp.tile(gain_new, 4), jnp.zeros((), bf16))
-    weight_rows = weight_rows + (next_inv[0, 0] * 0.0).astype(bf16)
     block = jnp.concatenate(
         [weight_rows, gain_lanes[None], jnp.zeros((ROWS - EXTRA - 1, 128), bf16)]
     )
+
     own = lax.all_to_all(
         jnp.broadcast_to(block[None], (64, ROWS, 128)), CHIPS, 0, 0, tiled=True
     )
     other = swap(own, 0, 1)
-
-    lanes = jnp.where(own_lanes, lanes, 0.0)
-    high = lax.reduce_precision(lanes, 8, 10)
-    most = jnp.max(jnp.maximum(jnp.abs(grad_rows), jnp.abs(lanes)[None] * (1.0 / 64.0)))
-    power = jnp.floor(jnp.log2(16384.0 / jnp.maximum(most, 1e-30)))
-    scale = jnp.exp2(power)
-    rows = [
-        high * (scale * (1.0 / 64.0)),
-        (lanes - high) * (scale * 32.0),
-        jnp.full((256,), power),
-    ]
-    natural = (grad_rows * scale).reshape(4, 32, 128).transpose(1, 0, 2).reshape(32, KV)
-    sent = jnp.concatenate([natural, jnp.concatenate(rows)[None]]).astype(f16)
-    grads = lax.all_to_all(jnp.broadcast_to(sent[None], (32, 33, KV)), DP, 0, 0, tiled=True)
+    grads = lax.all_to_all(sent, DP, 0, 0, tiled=True)
 
     value_ins = [
         pl.BlockSpec((16, ROWS, 128), lambda i, core: (i, 0, 0)),
@@ -371,15 +384,14 @@
     new_gain = new_gain.reshape(D).astype(bf16)
 
     grads, _ = lax.optimization_barrier((grads, next_values))
-    ends = grads[:, 32].astype(f32)
-    back = jnp.exp2(-ends[:, 256:384])
-    gain_sums = (ends[:, :128] * 64.0 + ends[:, 128:256] * (1.0 / 32.0)) * back
+    ends, back = grads[:, 32].astype(f32), jnp.exp2(-grads[:, 33].astype(f32))
+    gain_sums = (ends[:, :128] * 64.0 + ends[:, 128:256] * (1.0 / 32.0)) * back[:, :128]
     rep_gain = jnp.sum(gain_sums.reshape(8, 4, 128), axis=1).reshape(1, 1024)
     first_vec = beta_first * vec_first + (1.0 - beta_first) * rep_gain
     second_vec = beta_second * vec_second + (1.0 - beta_second) * rep_gain * rep_gain
     new_vec_first = jnp.where(holds_gain, first_vec, vec_first)
     new_vec_second = jnp.where(holds_gain, second_vec, vec_second)
-    rep_rows = grads[:, :32].astype(f32) * back[:, :1, None]
+    rep_rows = grads[:, :32].astype(f32) * back[:, None]
     old_first, old_second = mat_first.reshape(32, 32, KV), mat_second.reshape(32, 32, KV)
     first_mat = beta_first * old_first + (1.0 - beta_first) * rep_rows
     second_mat = beta_second * old_second + (1.0 - beta_second) * rep_rows * rep_rows

time: 163 us -> 157 us (0.963)
  between operations: 6.7 us -> 4.12 us
    add x4 -> x2, other arithmetic: 2.25 us -> 0.39 us  [the longest x1 0.39 us: body(): moments = share(first_picks, y, owner_weight >> 3, 8) + after.astype(f16)]
  transfers between devices with their start and end apart: 16 -> 16, of which waited for: 2 -> 2; matrix products, arithmetic and copies ran while one was open for 11% -> 10% of each run, Pallas kernels for 18% -> 18%
where the time goes in v3:
time: 157 us
  blocking collectives  38.4 us (24%)
  Pallas kernels  33.2 us (21%)
  starting transfers between devices  32.9 us (21%)
  waiting for transfers between devices  23.1 us (15%)
  other arithmetic  21.9 us (14%)
  between operations  4.12 us (3%)
  local copies, waits for them, and re-layouts  3.07 us (2%)
    all_to_all x1, blocking collectives, body(): lax.all_to_all(jnp.broadcast_to(block[None], (64, ROWS, 128)), CHIPS, 0,...  38.4 us
    ppermute x14, waiting for transfers between devices, swap(): return lax.ppermute(block, AXES, pairs(mask, core))  16.4 us
    ppermute x14, starting transfers between devices, swap(): return lax.ppermute(block, AXES, pairs(mask, core))  16.3 us
    all_to_all x1, starting transfers between devices, body(): parts = lax.all_to_all(scaled.astype(f16), CHIPS, 0, 0, tiled=True)  11.7 us
    pallas_call x1, Pallas kernels, body(): call(chip_kernel, 4, [hid_spec, pl.BlockSpec((TOK, BLK), lambda i, core:...  11 us
    pallas_call x1, Pallas kernels, body(): call(last_kernel, 4, value_ins + [whole((TOK, KV)), any_spec, any_spec],...  6.71 us
    all_to_all x1, waiting for transfers between devices, body(): grads = lax.all_to_all(sent, DP, 0, 0, tiled=True)  6.66 us
    pallas_call x1, Pallas kernels, body(): call(first_kernel, 4, value_ins, (wide, gain_spec, whole((TOK, KV))), (sh...  6.33 us
  transfers between devices with their start and end apart: 16, of which 2 were waited for; matrix products, arithmetic and copies ran while one was open for 10% of the time, Pallas kernels for 18%

profile of v3, /device:TPU:2, one launch (start us, length us, event | category | flops | bytes accessed | tf_op | source)
XLA Modules:
  0.0 156.6 jit_solution(4642805626860616184)
XLA Ops:
  0.6 4.9 %shard_map.153 = (f32[768,128]{1,0:T(8,128)S(1)}, bf16[768,2048]{1,0:T(8,128)(2,1)}) custom-call(s32[1]{0:T(128)} %bitcast.4.core, bf16[768,4096]{1,0:T(8,128)(2,1)} %hid.5, bf16[768,512]{1,0:T(8,128)(2,1)} %grad.3), custom_call_target="tpu_custom_call" | custom-call | flops 1 | bytes 1 | tf_op jit(solution)/shard_map/pallas_call | solution.py:228
  6.0 2.7 %fusion.11 = (f16[256,512]{1,0:T(8,128)(2,1)S(1)}, f16[256,512]{1,0:T(8,128)(2,1)S(1)}, f16[256,512]{1,0:T(8,128)(2,1)S(1)}, f16[256,512]{1,0:T(8,128)(2,1)S(1)}...) fusion(f32[1,1024,512]{2,1,0:T(8,128)} %param.15, ...), kind=kLoop, calls=%fused_computation.27 | loop fusion | flops 1048576 | bytes 6291472 | tf_op jit(solution)/shard_map/convert_element_type | solution.py:252
  8.8 0.9 pad_maximum_fusion
  9.7 3.0 %collective-permute-start.3 = (f16[512,512]{1,0:T(8,128)(2,1)}, f16[512,512]{1,0:T(8,128)(2,1)S(1)}, u32[]{:S(2)}, u32[]{:S(2)}) collective-permute-start(f16[512,512]{1,0:T(8,128)(2,1)} %pad_maximum_fusion), channel_id=1, source_target_pairs={{0,96},{1,97},{2,98},{3,99},{4,100},{5,101},{6,102},{7,103},{8,104... | collective-permute-start | bytes 1572872 | tf_op jit(solution)/shard_map/ppermute | solution.py:42
  12.7 0.9 pad_maximum_fusion.1
  13.6 0.6 collective-permute-start.4
  14.3 0.9 pad_maximum_fusion.2
  15.6 0.6 fusion.44
  18.3 11.0 %shard_map.154 = (f32[64,136,128]{2,1,0:T(8,128)}, f32[1,512]{1,0:T(1,128)S(1)}) custom-call(s32[1]{0:T(128)} %bitcast.4.core, bf16[768,4096]{1,0:T(8,128)(2,1)} %hid.5, bf16[768,2048]{1,0:T(8,128)(2,1)} %collective-permute-done.got_hid, bf16[1,4096]{1,0:T(2,128)(2,1)S(1)} %reshape.228.gain, bf16[768,512]{1,0:T(8,128)(2,1)} %grad.3, ...), custom_call_target="tpu_custom_call" | custom-call | flops 1 | bytes 1 | tf_op jit(solution)/shard_map/pallas_call | solution.py:261
  29.3 3.9 %convert_element_type.120 = f16[64,136,128]{2,1,0:T(8,128)(2,1)} convert(f32[64,136,128]{2,1,0:T(8,128)} %get-tuple-element.39) | non-fusion elementwise | flops 1114112 | bytes 6684672 | tf_op jit(solution)/shard_map/convert_element_type | solution.py:309
  33.2 11.7 %all-to-all-start = ((f16[64,136,128]{2,1,0:T(8,128)(2,1)}), f16[64,136,128]{2,1,0:T(8,128)(2,1)}, u32[]{:S(2)}, u32[]{:S(2)}) async-start(f16[64,136,128]{2,1,0:T(8,128)(2,1)} %convert_element_type.120), calls=%async_computation | async-start | bytes 4456448 | tf_op jit(solution)/shard_map/all_to_all | solution.py:309
  45.3 4.2 %shard_map.155.inv = f32[768,128]{1,0:T(8,128)S(1)} custom-call(bf16[768,4096]{1,0:T(8,128)(2,1)} %hid.8), custom_call_target="tpu_custom_call" | custom-call | flops 16999999488 | bytes 1 | tf_op jit(solution)/shard_map/pallas_call | solution.py:292
  49.6 1.5 collective-permute-start.10
  51.7 2.1 %collective-permute-start.8 = (f16[64,512]{1,0:T(8,128)(2,1)S(1)}, f16[64,512]{1,0:T(8,128)(2,1)S(1)}, u32[]{:S(2)}, u32[]{:S(2)}) collective-permute-start(f16[64,512]{1,0:T(8,128)(2,1)S(1)} %bitcast.140), channel_id=1, source_target_pairs={{0,12},{1,13},{2,14},{3,15},{4,8},{5,9},{6,10},{7,11},{8,4},{9,5},... | collective-permute-start | bytes 196616 | tf_op jit(solution)/shard_map/ppermute | solution.py:42
  53.8 1.5 collective-permute-start.7
  55.3 0.6 collective-permute-start.6
  55.9 0.8 copy_bitcast_fusion
  56.6 16.4 %collective-permute-done.10 = f16[64,512]{1,0:T(8,128)(2,1)S(1)} collective-permute-done((f16[64,512]{1,0:T(8,128)(2,1)S(1)}, f16[64,512]{1,0:T(8,128)(2,1)S(1)}, u32[]{:S(2)}, u32[]{:S(2)}) %collective-permute-start.10) | collective-permute-done | bytes 65568 | tf_op jit(solution)/shard_map/ppermute | solution.py:42
  73.0 2.3 %collective-permute-start.12 = (f16[64,512]{1,0:T(8,128)(2,1)S(1)}, f16[64,512]{1,0:T(8,128)(2,1)S(1)}, u32[]{:S(2)}, u32[]{:S(2)}) collective-permute-start(f16[64,512]{1,0:T(8,128)(2,1)S(1)} %bitcast.137), channel_id=1, source_target_pairs={{0,28},{1,29},{2,30},{3,31},{4,24},{5,25},{6,26},{7,27},{8,20},{9,... | collective-permute-start | bytes 196616 | tf_op jit(solution)/shard_map/ppermute | solution.py:42
  75.3 3.1 %collective-permute-start.11 = (f16[64,512]{1,0:T(8,128)(2,1)S(1)}, f16[64,512]{1,0:T(8,128)(2,1)S(1)}, u32[]{:S(2)}, u32[]{:S(2)}) collective-permute-start(f16[64,512]{1,0:T(8,128)(2,1)S(1)} %bitcast.136), channel_id=1, source_target_pairs={{0,24},{1,25},{2,26},{3,27},{4,28},{5,29},{6,30},{7,31},{8,16},{9,... | collective-permute-start | bytes 196616 | tf_op jit(solution)/shard_map/ppermute | solution.py:42
  78.4 1.5 exponential_reduce_fusion
  79.9 0.7 convert_multiply_fusion.1
  80.7 2.1 %multiply_reduce_fusion = f32[136,128]{1,0:T(8,128)S(1)} fusion(f16[64,136,128]{2,1,0:T(8,128)(2,1)} %all-to-all-done, f32[64]{0:T(128)S(1)} %exponential_reduce_fusion), kind=kLoop, calls=%fused_computation | loop fusion | flops 3324928 | bytes 2298112 | tf_op jit(solution)/shard_map/reduce_sum | solution.py:313
  83.3 1.1 broadcast_in_dim.38
  85.2 38.4 %all_to_all.15.blocks = bf16[64,144,128]{2,1,0:T(8,128)(2,1)} all-to-all(bf16[64,144,128]{2,1,0:T(8,128)(2,1)S(1)} %broadcast_in_dim.42), channel_id=1, replica_groups=mesh['y'=4,'zl'=2,'x'=4,'zh'=2,'c'=2] {'zh','y','zl','x'}, dimensions={0} | all-to-all | bytes 4718592 | tf_op jit(solution)/shard_map/all_to_all | solution.py:355
  123.5 5.0 %all-to-all-start.2 = ((f16[32,34,512]{2,1,0:T(8,128)(2,1)}), f16[32,34,512]{2,1,0:T(8,128)(2,1)S(1)}, u32[]{:S(2)}, u32[]{:S(2)}) async-start(f16[32,34,512]{2,1,0:T(8,128)(2,1)} %broadcast_in_dim.38), calls=%async_computation.2 | async-start | bytes 2621440 | tf_op jit(solution)/shard_map/all_to_all | solution.py:359
  129.8 6.3 %shard_map.156 = (bf16[4096,512]{1,0:T(8,128)(2,1)}, f32[1,4096]{1,0:T(1,128)S(1)}, f32[768,512]{1,0:T(8,128)S(1)}) custom-call(s32[1]{0:T(128)} %bitcast.4.core, bf16[64,144,128]{2,1,0:T(8,128)(2,1)} %all_to_all.15.blocks, bf16[768,4096]{1,0:T(8,128)(2,1)} %hid.8, f32[768,128]{1,0:T(8,128)S(1)} %shard_map.155.inv), custom_call_target="tpu_custom_call" | custom-call | flops 1 | bytes 1 | tf_op jit(solution)/shard_map/pallas_call | solution.py:368
  136.1 6.7 %shard_map.157 = (bf16[4096,512]{1,0:T(8,128)(2,1)}, f32[1,4096]{1,0:T(1,128)S(1)}, bf16[768,512]{1,0:T(8,128)(2,1)}) custom-call(s32[1]{0:T(128)} %bitcast.core, bf16[64,144,128]{2,1,0:T(8,128)(2,1)} %collective-permute-done.13.blocks, bf16[768,4096]{1,0:T(8,128)(2,1)} %hid.8, ...), custom_call_target="tpu_custom_call", output_to_operand_aliasing={{0}: (5, {}), {1}: (6, {})} | custom-call | flops 1 | bytes 1 | tf_op jit(solution)/shard_map/pallas_call | solution.py:375
  142.8 6.7 %all-to-all-done.2 = f16[32,34,512]{2,1,0:T(8,128)(2,1)S(1)} async-done(((f16[32,34,512]{2,1,0:T(8,128)(2,1)}), f16[32,34,512]{2,1,0:T(8,128)(2,1)S(1)}, u32[]{:S(2)}, u32[]{:S(2)}) %all-to-all-start.2) | async-done | bytes 1114144 | tf_op jit(solution)/shard_map/all_to_all | solution.py:359
  150.0 0.6 convert_reduce_fusion
  150.7 0.6 broadcast_select_fusion
  151.3 5.3 %fusion.1 = (f32[32,32,512]{2,1,0:T(8,128)}, f32[32,32,512]{2,1,0:T(8,128)}) fusion(f32[32,32,512]{2,1,0:T(8,128)} %bitcast.126, f32[32,512]{1,0:T(8,128)S(1)} %exponential_bitcast_fusion, pred[]{:T(512)S(6)} %eq.68, f16[32,34,512]{2,1,0:T(8,128)(2,1)S(1)} %all-to-all-done.2, f32[32,32,512]{2,1,0:T(8,128)} %bitcast.125), kind=kLoop, calls=%fused_computation.3 | loop fusion | flops 5767168 | bytes 9502721 | tf_op jit(solution)/shard_map/jit(_where)/select_n | solution.py:399
  (71 shorter events, 3.8 us)
Async XLA Ops:
  5.5 12.7 %collective-permute-start = (bf16[768,2048]{1,0:T(8,128)(2,1)}, bf16[768,2048]{1,0:T(8,128)(2,1)}, u32[]{:S(2)}, u32[]{:S(2)}) collective-permute-start(bf16[768,2048]{1,0:T(8,128)(2,1)} %get-tuple-element.37), channel_id=1, source_target_pairs={{0,1},{1,0},{2,3},{3,2},{4,5},{5,4},{6,7},{7,6},{8,9},{9,8},{10,11... | collective-permute-start | bytes 9437192 | tf_op jit(solution)/shard_map/ppermute | solution.py:42
  5.5 12.7 %collective-permute-start.1 = (bf16[768,512]{1,0:T(8,128)(2,1)}, bf16[768,512]{1,0:T(8,128)(2,1)S(1)}, u32[]{:S(2)}, u32[]{:S(2)}) collective-permute-start(bf16[768,512]{1,0:T(8,128)(2,1)} %grad.3), channel_id=1, source_target_pairs={{0,1},{1,0},{2,3},{3,2},{4,5},{5,4},{6,7},{7,6},{8,9},{9,8},{10,11... | collective-permute-start | bytes 2359304 | tf_op jit(solution)/shard_map/ppermute | solution.py:42
  6.0 9.1 %collective-permute-start.2 = (f32[768,128]{1,0:T(8,128)S(1)}, f32[768,128]{1,0:T(8,128)S(1)}, u32[]{:S(2)}, u32[]{:S(2)}) collective-permute-start(f32[768,128]{1,0:T(8,128)S(1)} %get-tuple-element.38.inv), channel_id=1, source_target_pairs={{0,1},{1,0},{2,3},{3,2},{4,5},{5,4},{6,7},{7,6},{8,9},{9,8},{10,11... | collective-permute-start | bytes 1179656 | tf_op jit(solution)/shard_map/ppermute | solution.py:42
  8.7 6.9 %copy-start.3 = (s32[2]{0:T(128)S(1)}, s32[2]{0:T(128)}, u32[]{:S(2)}) copy-start(s32[2]{0:T(128)} %param.14) | copy-start | bytes 28
  8.7 9.3 %copy-start.2 = (bf16[4096]{0:T(1024)(128)(2,1)S(1)}, bf16[4096]{0:T(1024)(128)(2,1)}, u32[]{:S(2)}) copy-start(bf16[4096]{0:T(1024)(128)(2,1)} %param.13) | copy-start | bytes 24580
  8.8 9.5 %copy-start = (f32[1,1024]{1,0:T(1,128)S(1)}, f32[1,1024]{1,0:T(1,128)}, u32[]{:S(2)}) copy-start(f32[1,1024]{1,0:T(1,128)} %firsts.1) | copy-start | bytes 12292
  8.8 9.5 %copy-start.1 = (f32[1,1024]{1,0:T(1,128)S(1)}, f32[1,1024]{1,0:T(1,128)}, u32[]{:S(2)}) copy-start(f32[1,1024]{1,0:T(1,128)} %seconds.1) | copy-start | bytes 12292
  9.7 35.2 %collective-permute-start.3 = (f16[512,512]{1,0:T(8,128)(2,1)}, f16[512,512]{1,0:T(8,128)(2,1)S(1)}, u32[]{:S(2)}, u32[]{:S(2)}) collective-permute-start(f16[512,512]{1,0:T(8,128)(2,1)} %pad_maximum_fusion), channel_id=1, source_target_pairs={{0,96},{1,97},{2,98},{3,99},{4,100},{5,101},{6,102},{7,103},{8,104... | collective-permute-start | bytes 1572872 | tf_op jit(solution)/shard_map/ppermute | solution.py:42
  13.6 31.3 %collective-permute-start.4 = (f16[512,512]{1,0:T(8,128)(2,1)}, f16[512,512]{1,0:T(8,128)(2,1)S(1)}, u32[]{:S(2)}, u32[]{:S(2)}) collective-permute-start(f16[512,512]{1,0:T(8,128)(2,1)} %pad_maximum_fusion.1), channel_id=1, source_target_pairs={{0,64},{1,65},{2,66},{3,67},{4,68},{5,69},{6,70},{7,71},{8,72},{9,... | collective-permute-start | bytes 1572872 | tf_op jit(solution)/shard_map/ppermute | solution.py:42
  15.2 29.7 %collective-permute-start.5 = (f16[512,512]{1,0:T(8,128)(2,1)}, f16[512,512]{1,0:T(8,128)(2,1)}, u32[]{:S(2)}, u32[]{:S(2)}) collective-permute-start(f16[512,512]{1,0:T(8,128)(2,1)} %pad_maximum_fusion.2), channel_id=1, source_target_pairs={{0,32},{1,33},{2,34},{3,35},{4,36},{5,37},{6,38},{7,39},{8,40},{9,... | collective-permute-start | bytes 1572872 | tf_op jit(solution)/shard_map/ppermute | solution.py:42
  33.2 45.2 %all-to-all-start = ((f16[64,136,128]{2,1,0:T(8,128)(2,1)}), f16[64,136,128]{2,1,0:T(8,128)(2,1)}, u32[]{:S(2)}, u32[]{:S(2)}) async-start(f16[64,136,128]{2,1,0:T(8,128)(2,1)} %convert_element_type.120), calls=%async_computation | async-start | bytes 4456448 | tf_op jit(solution)/shard_map/all_to_all | solution.py:309
  49.6 23.4 %collective-permute-start.10 = (f16[64,512]{1,0:T(8,128)(2,1)S(1)}, f16[64,512]{1,0:T(8,128)(2,1)S(1)}, u32[]{:S(2)}, u32[]{:S(2)}) collective-permute-start(f16[64,512]{1,0:T(8,128)(2,1)S(1)} %bitcast.142), channel_id=1, source_target_pairs={{0,20},{1,21},{2,22},{3,23},{4,16},{5,17},{6,18},{7,19},{8,28},{9,... | collective-permute-start | bytes 196616 | tf_op jit(solution)/shard_map/ppermute | solution.py:42
  51.2 24.1 %collective-permute-start.9 = (f16[64,512]{1,0:T(8,128)(2,1)S(1)}, f16[64,512]{1,0:T(8,128)(2,1)S(1)}, u32[]{:S(2)}, u32[]{:S(2)}) collective-permute-start(f16[64,512]{1,0:T(8,128)(2,1)S(1)} %bitcast.141), channel_id=1, source_target_pairs={{0,16},{1,17},{2,18},{3,19},{4,20},{5,21},{6,22},{7,23},{8,24},{9,... | collective-permute-start | bytes 196616 | tf_op jit(solution)/shard_map/ppermute | solution.py:42
  51.7 26.7 %collective-permute-start.8 = (f16[64,512]{1,0:T(8,128)(2,1)S(1)}, f16[64,512]{1,0:T(8,128)(2,1)S(1)}, u32[]{:S(2)}, u32[]{:S(2)}) collective-permute-start(f16[64,512]{1,0:T(8,128)(2,1)S(1)} %bitcast.140), channel_id=1, source_target_pairs={{0,12},{1,13},{2,14},{3,15},{4,8},{5,9},{6,10},{7,11},{8,4},{9,5},... | collective-permute-start | bytes 196616 | tf_op jit(solution)/shard_map/ppermute | solution.py:42
  53.8 24.6 %collective-permute-start.7 = (f16[64,512]{1,0:T(8,128)(2,1)S(1)}, f16[64,512]{1,0:T(8,128)(2,1)S(1)}, u32[]{:S(2)}, u32[]{:S(2)}) collective-permute-start(f16[64,512]{1,0:T(8,128)(2,1)S(1)} %bitcast.139), channel_id=1, source_target_pairs={{0,8},{1,9},{2,10},{3,11},{4,12},{5,13},{6,14},{7,15},{8,0},{9,1},... | collective-permute-start | bytes 196616 | tf_op jit(solution)/shard_map/ppermute | solution.py:42
  55.3 23.1 %collective-permute-start.6 = (f16[64,512]{1,0:T(8,128)(2,1)S(1)}, f16[64,512]{1,0:T(8,128)(2,1)S(1)}, u32[]{:S(2)}, u32[]{:S(2)}) collective-permute-start(f16[64,512]{1,0:T(8,128)(2,1)S(1)} %bitcast.138), channel_id=1, source_target_pairs={{0,4},{1,5},{2,6},{3,7},{4,0},{5,1},{6,2},{7,3},{8,12},{9,13},{10,... | collective-permute-start | bytes 196616 | tf_op jit(solution)/shard_map/ppermute | solution.py:42
  73.0 10.3 %collective-permute-start.12 = (f16[64,512]{1,0:T(8,128)(2,1)S(1)}, f16[64,512]{1,0:T(8,128)(2,1)S(1)}, u32[]{:S(2)}, u32[]{:S(2)}) collective-permute-start(f16[64,512]{1,0:T(8,128)(2,1)S(1)} %bitcast.137), channel_id=1, source_target_pairs={{0,28},{1,29},{2,30},{3,31},{4,24},{5,25},{6,26},{7,27},{8,20},{9,... | collective-permute-start | bytes 196616 | tf_op jit(solution)/shard_map/ppermute | solution.py:42
  75.3 8.1 %collective-permute-start.11 = (f16[64,512]{1,0:T(8,128)(2,1)S(1)}, f16[64,512]{1,0:T(8,128)(2,1)S(1)}, u32[]{:S(2)}, u32[]{:S(2)}) collective-permute-start(f16[64,512]{1,0:T(8,128)(2,1)S(1)} %bitcast.136), channel_id=1, source_target_pairs={{0,24},{1,25},{2,26},{3,27},{4,28},{5,29},{6,30},{7,31},{8,16},{9,... | collective-permute-start | bytes 196616 | tf_op jit(solution)/shard_map/ppermute | solution.py:42
  123.5 12.6 %collective-permute-start.13 = (bf16[64,144,128]{2,1,0:T(8,128)(2,1)}, bf16[64,144,128]{2,1,0:T(8,128)(2,1)}, u32[]{:S(2)}, u32[]{:S(2)}) collective-permute-start(bf16[64,144,128]{2,1,0:T(8,128)(2,1)} %all_to_all.15.blocks), channel_id=1, source_target_pairs={{0,1},{1,0},{2,3},{3,2},{4,5},{5,4},{6,7},{7,6},{8,9},{9,8},{10,11... | collective-permute-start | bytes 7077896 | tf_op jit(solution)/shard_map/ppermute | solution.py:42
  123.5 26.0 %all-to-all-start.2 = ((f16[32,34,512]{2,1,0:T(8,128)(2,1)}), f16[32,34,512]{2,1,0:T(8,128)(2,1)S(1)}, u32[]{:S(2)}, u32[]{:S(2)}) async-start(f16[32,34,512]{2,1,0:T(8,128)(2,1)} %broadcast_in_dim.38), calls=%async_computation.2 | async-start | bytes 2621440 | tf_op jit(solution)/shard_map/all_to_all | solution.py:359

commit v4 on v3

--- a/solution.py
+++ b/solution.py
@@ -51,6 +51,10 @@
         first_moment,
         second_moment,
     )
+
+
+def hbm(x):
+    return pltpu.with_memory_space_constraint(x, pltpu.HBM)
 
 
 def fold(values):
@@ -181,7 +185,7 @@
     return ((i // 2) * 2 + core[0]) * 2 + i % 2
 
 
-def call(kernel, grid, ins, outs, out_shape, scratch=(), prefetch=1, **more):
+def call(kernel, grid, ins, outs, out_shape, scratch=(), prefetch=1, params=PARAMS, **more):
     return pl.pallas_call(
         kernel,
         grid_spec=pltpu.PrefetchScalarGridSpec(
@@ -192,7 +196,7 @@
             scratch_shapes=scratch,
         ),
         out_shape=out_shape,
-        compiler_params=PARAMS,
+        compiler_params=params,
         cost_estimate=COST,
         **more,
     )
@@ -275,16 +279,17 @@
         ],
         (pl.BlockSpec((16, SUM_ROWS, 128), lambda i, core: (i, 0, 0)), whole((1, KV))),
         (shape((64, SUM_ROWS, 128), f32), shape((1, KV), f32)),
+        params=pltpu.CompilerParams(vmem_limit_bytes=40 * 1024 * 1024),
     )(
         core_at,
-        hidden_in,
-        got_hid,
+        hbm(hidden_in),
+        hbm(got_hid),
         gain_row,
-        value_grad,
-        got_grad,
-        value_weight,
-        inv,
-        got_inv,
+        hbm(value_grad),
+        hbm(got_grad),
+        hbm(value_weight),
+        hbm(inv),
+        hbm(got_inv),
         vec_first,
         vec_second,
     )
@@ -309,22 +314,18 @@
     parts = lax.all_to_all(scaled.astype(f16), CHIPS, 0, 0, tiled=True)
     parts, early = lax.optimization_barrier((parts, arrived[:5]))
     arrived = early + arrived[5:]
-    back = jnp.exp2(-parts[:, EXTRA + 3, :1].astype(f32))
-    summed = jnp.sum(parts.astype(f32) * back[:, :, None], axis=0)
+    back = jnp.exp2(-parts[:, EXTRA + 3].astype(f32))
+    summed = jnp.sum(parts.astype(f32) * back[:, None], axis=0)
     grad_rows = summed[:EXTRA]
     lanes = summed[EXTRA] * 64.0 + summed[EXTRA + 1] * (64.0 / 256.0)
     lanes = lanes + summed[EXTRA + 2] * (64.0 / 65536.0)
     own_lanes = (jnp.arange(128) >> 5) == x
     lanes = jnp.where(own_lanes, lanes, 0.0)
-    high = lax.reduce_precision(lanes, 8, 10)
-    most = jnp.maximum(jnp.max(jnp.abs(grad_rows), axis=0), jnp.abs(lanes) * (1.0 / 64.0))
-    power = jnp.floor(jnp.log2(16384.0 / jnp.maximum(most, 1e-30)))
-    scale = jnp.exp2(power)
-    gain_row = [high * (scale * (1.0 / 64.0)), (lanes - high) * (scale * 32.0)]
-    gain_row = jnp.concatenate(gain_row + [jnp.zeros((256,), f32)])
-    natural = (grad_rows * scale).reshape(4, 32, 128).transpose(1, 0, 2).reshape(32, KV)
-    sent = jnp.concatenate([natural, gain_row[None], jnp.tile(power, 4)[None]]).astype(f16)
-    sent = jnp.broadcast_to(sent[None], (32, 34, KV))
+    most = jnp.maximum(jnp.max(jnp.abs(grad_rows), axis=0), 1e-30)
+    power = jnp.floor(jnp.log2(16384.0 / most))
+    sent = (grad_rows * jnp.exp2(power)).reshape(4, 32, 128).transpose(1, 0, 2)
+    sent = sent.reshape(32, KV).astype(f16)
+    sent = jnp.broadcast_to(sent[None], (32, 32, KV))
     old_vecs = lax.dynamic_index_in_dim(parts, zh * 32 + owner_gain, 0, keepdims=False)
     old_vecs = old_vecs[EXTRA + 4 :].astype(f32) * (1.0 / 4096.0)
     old_vecs = lax.dynamic_slice_in_dim(old_vecs, x * 32, 32, 1)
@@ -335,9 +336,11 @@
     gain_part = lax.dynamic_slice_in_dim(norm_gain, first_row, 32)
     gain_new = adam_step(gain_part, grad_gain, old_vecs[0], old_vecs[1], gain_rate)[0]
     gain_lanes = jnp.where(own_lanes, jnp.tile(gain_new, 4), jnp.zeros((), bf16))
-    arrived, grad_rows, sent, gain_lanes = lax.optimization_barrier(
-        (arrived, grad_rows, sent, gain_lanes)
-    )
+    high = lax.reduce_precision(lanes, 8, 7)
+    middle = lax.reduce_precision(lanes - high, 8, 7)
+    rows = [gain_lanes, power, high, middle, lanes - high - middle]
+    rows = jnp.stack([row.astype(bf16) for row in rows])
+    arrived, grad_rows, sent, rows = lax.optimization_barrier((arrived, grad_rows, sent, rows))
     old_mats = last_picks[0]
     for k in range(1, 8):
         source = (zl * 4 + x) ^ k == (owner_weight & 7)
@@ -349,7 +352,7 @@
         own_rows, grad_rows, blocked(old_mats[:32]), blocked(old_mats[32:]), learn_rate
     )[0]
     block = jnp.concatenate(
-        [weight_rows, gain_lanes[None], jnp.zeros((ROWS - EXTRA - 1, 128), bf16)]
+        [weight_rows, rows, jnp.zeros((ROWS - EXTRA - 5, 128), bf16)]
     )
 
     own = lax.all_to_all(
@@ -383,15 +386,16 @@
     )(other_at, other, next_hidden, next_inv, acc, started, gain_started)
     new_gain = new_gain.reshape(D).astype(bf16)
 
-    grads, _ = lax.optimization_barrier((grads, next_values))
-    ends, back = grads[:, 32].astype(f32), jnp.exp2(-grads[:, 33].astype(f32))
-    gain_sums = (ends[:, :128] * 64.0 + ends[:, 128:256] * (1.0 / 32.0)) * back[:, :128]
-    rep_gain = jnp.sum(gain_sums.reshape(8, 4, 128), axis=1).reshape(1, 1024)
+    ends = lax.dynamic_slice_in_dim(own[:, EXTRA + 1 : EXTRA + 5], zh * 32, 32).astype(f32)
+    rep_gain = ends[:, 1] + ends[:, 2] + ends[:, 3]
+    rep_gain = jnp.sum(rep_gain.reshape(8, 4, 128), axis=1).reshape(1, 1024)
     first_vec = beta_first * vec_first + (1.0 - beta_first) * rep_gain
     second_vec = beta_second * vec_second + (1.0 - beta_second) * rep_gain * rep_gain
     new_vec_first = jnp.where(holds_gain, first_vec, vec_first)
     new_vec_second = jnp.where(holds_gain, second_vec, vec_second)
-    rep_rows = grads[:, :32].astype(f32) * back[:, None]
+    back = jnp.tile(jnp.exp2(-ends[:, 0]), (1, 4))
+    grads, back, _ = lax.optimization_barrier((grads, back, next_values))
+    rep_rows = grads.astype(f32) * back[:, None]
     old_first, old_second = mat_first.reshape(32, 32, KV), mat_second.reshape(32, 32, KV)
     first_mat = beta_first * old_first + (1.0 - beta_first) * rep_rows
     second_mat = beta_second * old_second + (1.0 - beta_second) * rep_rows * rep_rows

time: 157 us -> 148 us (0.943)
  other arithmetic: 21.9 us -> 16.9 us
  waiting for transfers between devices: 23.1 us -> 18.4 us
    all_to_all x1, waiting for transfers between devices: 6.66 us -> 1.92 us  [body(): grads = lax.all_to_all(sent, DP, 0, 0, tiled=True)]
    convert_element_type x1, other arithmetic: 3.91 us -> 1.65 us  [body(): parts = lax.all_to_all(scaled.astype(f16), CHIPS, 0, 0, tiled=True)]
    concatenate x3, other arithmetic: 2.75 us -> 1.17 us  [first_pick(): jnp.concatenate([lax.dynamic_slice_in_dim(m[0], (y ^ k) * 256, 256).astyp...]
  transfers between devices with their start and end apart: 16 -> 16, of which waited for: 2 -> 2; matrix products, arithmetic and copies ran while one was open for 10% -> 9% of each run, Pallas kernels for 18% -> 19%
where the time goes in v4:
time: 148 us
  blocking collectives  38.3 us (26%)
  starting transfers between devices  33.5 us (23%)
  Pallas kernels  32.6 us (22%)
  waiting for transfers between devices  18.4 us (12%)
  other arithmetic  16.9 us (11%)
  between operations  4.37 us (3%)
  local copies, waits for them, and re-layouts  3.53 us (2%)
    all_to_all x1, blocking collectives, body(): lax.all_to_all(jnp.broadcast_to(block[None], (64, ROWS, 128)), CHIPS, 0,...  38.3 us
    ppermute x14, starting transfers between devices, swap(): return lax.ppermute(block, AXES, pairs(mask, core))  17.1 us
    ppermute x14, waiting for transfers between devices, swap(): return lax.ppermute(block, AXES, pairs(mask, core))  16.5 us
    all_to_all x1, starting transfers between devices, body(): parts = lax.all_to_all(scaled.astype(f16), CHIPS, 0, 0, tiled=True)  11.4 us
    pallas_call x1, Pallas kernels, body(): call(chip_kernel, 4, [hid_spec, pl.BlockSpec((TOK, BLK), lambda i, core:...  10.5 us
    pallas_call x1, Pallas kernels, body(): call(last_kernel, 4, value_ins + [whole((TOK, KV)), any_spec, any_spec],...  6.66 us
    pallas_call x1, Pallas kernels, body(): call(first_kernel, 4, value_ins, (wide, gain_spec, whole((TOK, KV))), (sh...  6.25 us
    select_n x1, other arithmetic, body(): jnp.where(holds_weight, second_mat, old_second).reshape(1, 1024, KV)  5.28 us
  transfers between devices with their start and end apart: 16, of which 2 were waited for; matrix products, arithmetic and copies ran while one was open for 9% of the time, Pallas kernels for 19%

profile of v4, /device:TPU:2, one launch (start us, length us, event | category | flops | bytes accessed | tf_op | source)
XLA Modules:
  0.0 147.6 jit_solution(14561574548205646637)
XLA Ops:
  0.6 5.0 %shard_map.153 = (f32[768,128]{1,0:T(8,128)S(1)}, bf16[768,2048]{1,0:T(8,128)(2,1)}) custom-call(s32[1]{0:T(128)} %bitcast.4.core, bf16[768,4096]{1,0:T(8,128)(2,1)} %hid.5, bf16[768,512]{1,0:T(8,128)(2,1)} %grad.3), custom_call_target="tpu_custom_call" | custom-call | flops 1 | bytes 1 | tf_op jit(solution)/shard_map/pallas_call | solution.py:232
  6.3 2.0 %fusion.11 = (f16[256,512]{1,0:T(8,128)(2,1)S(1)}, f16[256,512]{1,0:T(8,128)(2,1)S(1)}, f16[256,512]{1,0:T(8,128)(2,1)S(1)}, f16[256,512]{1,0:T(8,128)(2,1)S(1)}...) fusion(f32[1,1024,512]{2,1,0:T(8,128)S(1)} %copy-done.3, ...), kind=kLoop, calls=%fused_computation.27 | loop fusion | flops 1048576 | bytes 6291472 | tf_op jit(solution)/shard_map/convert_element_type | solution.py:256
  8.5 3.1 %collective-permute-start.3 = (f16[512,512]{1,0:T(8,128)(2,1)S(1)}, f16[512,512]{1,0:T(8,128)(2,1)S(1)}, u32[]{:S(2)}, u32[]{:S(2)}) collective-permute-start(f16[512,512]{1,0:T(8,128)(2,1)S(1)} %pad_maximum_fusion), channel_id=1, source_target_pairs={{0,96},{1,97},{2,98},{3,99},{4,100},{5,101},{6,102},{7,103},{8,104... | collective-permute-start | bytes 1572872 | tf_op jit(solution)/shard_map/ppermute | solution.py:42
  11.7 0.7 collective-permute-start.4
  12.4 0.9 pad_maximum_fusion.2
  13.3 0.8 collective-permute-start.5
  14.2 0.6 fusion.40
  16.9 10.5 %shard_map.154 = (f32[64,136,128]{2,1,0:T(8,128)S(1)}, f32[1,512]{1,0:T(1,128)S(1)}) custom-call(s32[1]{0:T(128)} %bitcast.4.core, bf16[768,4096]{1,0:T(8,128)(2,1)} %hid.5, bf16[768,2048]{1,0:T(8,128)(2,1)} %collective-permute-done.got_hid, bf16[1,4096]{1,0:T(2,128)(2,1)S(1)} %reshape.252.gain, bf16[768,512]{1,0:T(8,128)(2,1)} %grad.3, ...), custom_call_target="tpu_custom_call" | custom-call | flops 1 | bytes 1 | tf_op jit(solution)/shard_map/pallas_call | solution.py:265
  27.4 1.7 %convert_element_type.143 = f16[64,136,128]{2,1,0:T(8,128)(2,1)} convert(f32[64,136,128]{2,1,0:T(8,128)S(1)} %get-tuple-element.40) | non-fusion elementwise | flops 1114112 | bytes 6684672 | tf_op jit(solution)/shard_map/convert_element_type | solution.py:314
  29.1 11.4 %all-to-all-start = ((f16[64,136,128]{2,1,0:T(8,128)(2,1)}), f16[64,136,128]{2,1,0:T(8,128)(2,1)}, u32[]{:S(2)}, u32[]{:S(2)}) async-start(f16[64,136,128]{2,1,0:T(8,128)(2,1)} %convert_element_type.143), calls=%async_computation | async-start | bytes 4456448 | tf_op jit(solution)/shard_map/all_to_all | solution.py:314
  40.9 4.2 %shard_map.155.inv = f32[768,128]{1,0:T(8,128)S(1)} custom-call(bf16[768,4096]{1,0:T(8,128)(2,1)} %hid.8), custom_call_target="tpu_custom_call" | custom-call | flops 16999999488 | bytes 1 | tf_op jit(solution)/shard_map/pallas_call | solution.py:297
  45.2 1.5 %collective-permute-start.10 = (f16[64,512]{1,0:T(8,128)(2,1)S(1)}, f16[64,512]{1,0:T(8,128)(2,1)S(1)}, u32[]{:S(2)}, u32[]{:S(2)}) collective-permute-start(f16[64,512]{1,0:T(8,128)(2,1)S(1)} %bitcast.126), channel_id=1, source_target_pairs={{0,20},{1,21},{2,22},{3,23},{4,16},{5,17},{6,18},{7,19},{8,28},{9,... | collective-permute-start | bytes 196616 | tf_op jit(solution)/shard_map/ppermute | solution.py:42
  47.2 2.1 %collective-permute-start.8 = (f16[64,512]{1,0:T(8,128)(2,1)S(1)}, f16[64,512]{1,0:T(8,128)(2,1)S(1)}, u32[]{:S(2)}, u32[]{:S(2)}) collective-permute-start(f16[64,512]{1,0:T(8,128)(2,1)S(1)} %bitcast.124), channel_id=1, source_target_pairs={{0,12},{1,13},{2,14},{3,15},{4,8},{5,9},{6,10},{7,11},{8,4},{9,5},... | collective-permute-start | bytes 196616 | tf_op jit(solution)/shard_map/ppermute | solution.py:42
  49.4 1.5 collective-permute-start.7
  50.8 0.6 collective-permute-start.6
  51.4 0.8 copy_bitcast_fusion.1
  52.2 16.5 %collective-permute-done.10 = f16[64,512]{1,0:T(8,128)(2,1)S(1)} collective-permute-done((f16[64,512]{1,0:T(8,128)(2,1)S(1)}, f16[64,512]{1,0:T(8,128)(2,1)S(1)}, u32[]{:S(2)}, u32[]{:S(2)}) %collective-permute-start.10) | collective-permute-done | bytes 65568 | tf_op jit(solution)/shard_map/ppermute | solution.py:42
  68.6 2.5 %collective-permute-start.12 = (f16[64,512]{1,0:T(8,128)(2,1)S(1)}, f16[64,512]{1,0:T(8,128)(2,1)S(1)}, u32[]{:S(2)}, u32[]{:S(2)}) collective-permute-start(f16[64,512]{1,0:T(8,128)(2,1)S(1)} %bitcast.121), channel_id=1, source_target_pairs={{0,28},{1,29},{2,30},{3,31},{4,24},{5,25},{6,26},{7,27},{8,20},{9,... | collective-permute-start | bytes 196616 | tf_op jit(solution)/shard_map/ppermute | solution.py:42
  71.1 3.2 %collective-permute-start.11 = (f16[64,512]{1,0:T(8,128)(2,1)S(1)}, f16[64,512]{1,0:T(8,128)(2,1)S(1)}, u32[]{:S(2)}, u32[]{:S(2)}) collective-permute-start(f16[64,512]{1,0:T(8,128)(2,1)S(1)} %bitcast.120), channel_id=1, source_target_pairs={{0,24},{1,25},{2,26},{3,27},{4,28},{5,29},{6,30},{7,31},{8,16},{9,... | collective-permute-start | bytes 196616 | tf_op jit(solution)/shard_map/ppermute | solution.py:42
  74.4 0.7 convert_multiply_fusion.1
  75.2 1.0 multiply_exponential_fusion
  76.1 2.1 %multiply_reduce_fusion = f32[136,128]{1,0:T(8,128)S(1)} fusion(f16[64,136,128]{2,1,0:T(8,128)(2,1)} %all-to-all-done, f32[64,128]{1,0:T(8,128)S(1)} %bitcast.116), kind=kLoop, calls=%fused_computation | loop fusion | flops 3324928 | bytes 2330624 | tf_op jit(solution)/shard_map/reduce_sum | solution.py:318
  78.7 1.1 broadcast_in_dim.28
  80.5 38.3 %all_to_all.15.blocks = bf16[64,144,128]{2,1,0:T(8,128)(2,1)} all-to-all(bf16[64,144,128]{2,1,0:T(8,128)(2,1)S(1)} %broadcast_in_dim.33), channel_id=1, replica_groups=mesh['y'=4,'zl'=2,'x'=4,'zh'=2,'c'=2] {'zh','y','zl','x'}, dimensions={0} | all-to-all | bytes 4718592 | tf_op jit(solution)/shard_map/all_to_all | solution.py:358
  118.7 5.0 %all-to-all-start.2 = ((f16[32,32,512]{2,1,0:T(8,128)(2,1)}), f16[32,32,512]{2,1,0:T(8,128)(2,1)S(1)}, u32[]{:S(2)}, u32[]{:S(2)}) async-start(f16[32,32,512]{2,1,0:T(8,128)(2,1)} %broadcast_in_dim.28), calls=%async_computation.2 | async-start | bytes 2097152 | tf_op jit(solution)/shard_map/all_to_all | solution.py:362
  125.1 6.3 %shard_map.156 = (bf16[4096,512]{1,0:T(8,128)(2,1)}, f32[1,4096]{1,0:T(1,128)S(1)}, f32[768,512]{1,0:T(8,128)S(1)}) custom-call(s32[1]{0:T(128)} %bitcast.4.core, bf16[64,144,128]{2,1,0:T(8,128)(2,1)} %all_to_all.15.blocks, bf16[768,4096]{1,0:T(8,128)(2,1)} %hid.8, f32[768,128]{1,0:T(8,128)S(1)} %shard_map.155.inv), custom_call_target="tpu_custom_call" | custom-call | flops 1 | bytes 1 | tf_op jit(solution)/shard_map/pallas_call | solution.py:371
  131.3 0.9 slice.83
  132.4 0.6 broadcast_select_fusion
  133.0 6.7 %shard_map.157 = (bf16[4096,512]{1,0:T(8,128)(2,1)}, f32[1,4096]{1,0:T(1,128)S(1)}, bf16[768,512]{1,0:T(8,128)(2,1)}) custom-call(s32[1]{0:T(128)} %bitcast.core, bf16[64,144,128]{2,1,0:T(8,128)(2,1)} %collective-permute-done.13.blocks, bf16[768,4096]{1,0:T(8,128)(2,1)} %hid.8, ...), custom_call_target="tpu_custom_call", output_to_operand_aliasing={{0}: (5, {}), {1}: (6, {})} | custom-call | flops 1 | bytes 1 | tf_op jit(solution)/shard_map/pallas_call | solution.py:378
  139.7 1.9 %all-to-all-done.2 = f16[32,32,512]{2,1,0:T(8,128)(2,1)S(1)} async-done(((f16[32,32,512]{2,1,0:T(8,128)(2,1)}), f16[32,32,512]{2,1,0:T(8,128)(2,1)S(1)}, u32[]{:S(2)}, u32[]{:S(2)}) %all-to-all-start.2) | async-done | bytes 1048608 | tf_op jit(solution)/shard_map/all_to_all | solution.py:362
  141.6 0.6 convert_reduce_fusion
  142.3 5.3 %fusion.1 = (f32[32,32,512]{2,1,0:T(8,128)}, f32[32,32,512]{2,1,0:T(8,128)}) fusion(f32[32,32,512]{2,1,0:T(8,128)} %bitcast.108, f16[32,32,512]{2,1,0:T(8,128)(2,1)S(1)} %all-to-all-done.2, f32[32,512]{1,0:T(8,128)S(1)} %bitcast.112, pred[]{:T(512)S(6)} %eq.73, f32[32,32,512]{2,1,0:T(8,128)} %bitcast.107), kind=kLoop, calls=%fused_computation.3 | loop fusion | flops 5767168 | bytes 9502721 | tf_op jit(solution)/shard_map/jit(_where)/select_n | solution.py:403
  (71 shorter events, 3.2 us)
Async XLA Ops:
  0.6 5.6 %copy-start.3 = (f32[1,1024,512]{2,1,0:T(8,128)S(1)}, f32[1,1024,512]{2,1,0:T(8,128)}, u32[]{:S(2)}) copy-start(f32[1,1024,512]{2,1,0:T(8,128)} %param.15) | copy-start | bytes 6291460
  5.7 2.6 %copy-start = (f32[768,128]{1,0:T(8,128)}, f32[768,128]{1,0:T(8,128)S(1)}, u32[]{:S(2)}) copy-start(f32[768,128]{1,0:T(8,128)S(1)} %get-tuple-element.39.inv) | copy-start | bytes 1179652
  5.7 11.3 %collective-permute-start = (bf16[768,2048]{1,0:T(8,128)(2,1)}, bf16[768,2048]{1,0:T(8,128)(2,1)}, u32[]{:S(2)}, u32[]{:S(2)}) collective-permute-start(bf16[768,2048]{1,0:T(8,128)(2,1)} %get-tuple-element.38), channel_id=1, source_target_pairs={{0,1},{1,0},{2,3},{3,2},{4,5},{5,4},{6,7},{7,6},{8,9},{9,8},{10,11... | collective-permute-start | bytes 9437192 | tf_op jit(solution)/shard_map/ppermute | solution.py:42
  5.7 11.2 %collective-permute-start.1 = (bf16[768,512]{1,0:T(8,128)(2,1)}, bf16[768,512]{1,0:T(8,128)(2,1)}, u32[]{:S(2)}, u32[]{:S(2)}) collective-permute-start(bf16[768,512]{1,0:T(8,128)(2,1)} %grad.3), channel_id=1, source_target_pairs={{0,1},{1,0},{2,3},{3,2},{4,5},{5,4},{6,7},{7,6},{8,9},{9,8},{10,11... | collective-permute-start | bytes 2359304 | tf_op jit(solution)/shard_map/ppermute | solution.py:42
  6.2 7.2 %collective-permute-start.2 = (f32[768,128]{1,0:T(8,128)S(1)}, f32[768,128]{1,0:T(8,128)}, u32[]{:S(2)}, u32[]{:S(2)}) collective-permute-start(f32[768,128]{1,0:T(8,128)S(1)} %get-tuple-element.39.inv), channel_id=1, source_target_pairs={{0,1},{1,0},{2,3},{3,2},{4,5},{5,4},{6,7},{7,6},{8,9},{9,8},{10,11... | collective-permute-start | bytes 1179656 | tf_op jit(solution)/shard_map/ppermute | solution.py:42
  8.3 5.9 %copy-start.5 = (s32[2]{0:T(128)S(1)}, s32[2]{0:T(128)}, u32[]{:S(2)}) copy-start(s32[2]{0:T(128)} %param.14) | copy-start | bytes 28
  8.3 8.4 %copy-start.4 = (bf16[4096]{0:T(1024)(128)(2,1)S(1)}, bf16[4096]{0:T(1024)(128)(2,1)}, u32[]{:S(2)}) copy-start(bf16[4096]{0:T(1024)(128)(2,1)} %param.13) | copy-start | bytes 24580
  8.3 8.6 %copy-start.1 = (f32[1,1024]{1,0:T(1,128)S(1)}, f32[1,1024]{1,0:T(1,128)}, u32[]{:S(2)}) copy-start(f32[1,1024]{1,0:T(1,128)} %firsts.1) | copy-start | bytes 12292
  8.4 8.6 %copy-start.2 = (f32[1,1024]{1,0:T(1,128)S(1)}, f32[1,1024]{1,0:T(1,128)}, u32[]{:S(2)}) copy-start(f32[1,1024]{1,0:T(1,128)} %seconds.1) | copy-start | bytes 12292
  8.5 32.0 %collective-permute-start.3 = (f16[512,512]{1,0:T(8,128)(2,1)S(1)}, f16[512,512]{1,0:T(8,128)(2,1)S(1)}, u32[]{:S(2)}, u32[]{:S(2)}) collective-permute-start(f16[512,512]{1,0:T(8,128)(2,1)S(1)} %pad_maximum_fusion), channel_id=1, source_target_pairs={{0,96},{1,97},{2,98},{3,99},{4,100},{5,101},{6,102},{7,103},{8,104... | collective-permute-start | bytes 1572872 | tf_op jit(solution)/shard_map/ppermute | solution.py:42
  11.7 28.7 %collective-permute-start.4 = (f16[512,512]{1,0:T(8,128)(2,1)S(1)}, f16[512,512]{1,0:T(8,128)(2,1)S(1)}, u32[]{:S(2)}, u32[]{:S(2)}) collective-permute-start(f16[512,512]{1,0:T(8,128)(2,1)S(1)} %pad_maximum_fusion.1), channel_id=1, source_target_pairs={{0,64},{1,65},{2,66},{3,67},{4,68},{5,69},{6,70},{7,71},{8,72},{9,... | collective-permute-start | bytes 1572872 | tf_op jit(solution)/shard_map/ppermute | solution.py:42
  13.3 27.1 %collective-permute-start.5 = (f16[512,512]{1,0:T(8,128)(2,1)}, f16[512,512]{1,0:T(8,128)(2,1)S(1)}, u32[]{:S(2)}, u32[]{:S(2)}) collective-permute-start(f16[512,512]{1,0:T(8,128)(2,1)} %pad_maximum_fusion.2), channel_id=1, source_target_pairs={{0,32},{1,33},{2,34},{3,35},{4,36},{5,37},{6,38},{7,39},{8,40},{9,... | collective-permute-start | bytes 1572872 | tf_op jit(solution)/shard_map/ppermute | solution.py:42
  29.1 45.3 %all-to-all-start = ((f16[64,136,128]{2,1,0:T(8,128)(2,1)}), f16[64,136,128]{2,1,0:T(8,128)(2,1)}, u32[]{:S(2)}, u32[]{:S(2)}) async-start(f16[64,136,128]{2,1,0:T(8,128)(2,1)} %convert_element_type.143), calls=%async_computation | async-start | bytes 4456448 | tf_op jit(solution)/shard_map/all_to_all | solution.py:314
  45.2 23.5 %collective-permute-start.10 = (f16[64,512]{1,0:T(8,128)(2,1)S(1)}, f16[64,512]{1,0:T(8,128)(2,1)S(1)}, u32[]{:S(2)}, u32[]{:S(2)}) collective-permute-start(f16[64,512]{1,0:T(8,128)(2,1)S(1)} %bitcast.126), channel_id=1, source_target_pairs={{0,20},{1,21},{2,22},{3,23},{4,16},{5,17},{6,18},{7,19},{8,28},{9,... | collective-permute-start | bytes 196616 | tf_op jit(solution)/shard_map/ppermute | solution.py:42
  46.7 24.4 %collective-permute-start.9 = (f16[64,512]{1,0:T(8,128)(2,1)S(1)}, f16[64,512]{1,0:T(8,128)(2,1)S(1)}, u32[]{:S(2)}, u32[]{:S(2)}) collective-permute-start(f16[64,512]{1,0:T(8,128)(2,1)S(1)} %bitcast.125), channel_id=1, source_target_pairs={{0,16},{1,17},{2,18},{3,19},{4,20},{5,21},{6,22},{7,23},{8,24},{9,... | collective-permute-start | bytes 196616 | tf_op jit(solution)/shard_map/ppermute | solution.py:42
  47.2 27.1 %collective-permute-start.8 = (f16[64,512]{1,0:T(8,128)(2,1)S(1)}, f16[64,512]{1,0:T(8,128)(2,1)S(1)}, u32[]{:S(2)}, u32[]{:S(2)}) collective-permute-start(f16[64,512]{1,0:T(8,128)(2,1)S(1)} %bitcast.124), channel_id=1, source_target_pairs={{0,12},{1,13},{2,14},{3,15},{4,8},{5,9},{6,10},{7,11},{8,4},{9,5},... | collective-permute-start | bytes 196616 | tf_op jit(solution)/shard_map/ppermute | solution.py:42
  49.4 25.0 %collective-permute-start.7 = (f16[64,512]{1,0:T(8,128)(2,1)S(1)}, f16[64,512]{1,0:T(8,128)(2,1)S(1)}, u32[]{:S(2)}, u32[]{:S(2)}) collective-permute-start(f16[64,512]{1,0:T(8,128)(2,1)S(1)} %bitcast.123), channel_id=1, source_target_pairs={{0,8},{1,9},{2,10},{3,11},{4,12},{5,13},{6,14},{7,15},{8,0},{9,1},... | collective-permute-start | bytes 196616 | tf_op jit(solution)/shard_map/ppermute | solution.py:42
  50.8 23.5 %collective-permute-start.6 = (f16[64,512]{1,0:T(8,128)(2,1)S(1)}, f16[64,512]{1,0:T(8,128)(2,1)S(1)}, u32[]{:S(2)}, u32[]{:S(2)}) collective-permute-start(f16[64,512]{1,0:T(8,128)(2,1)S(1)} %bitcast.122), channel_id=1, source_target_pairs={{0,4},{1,5},{2,6},{3,7},{4,0},{5,1},{6,2},{7,3},{8,12},{9,13},{10,... | collective-permute-start | bytes 196616 | tf_op jit(solution)/shard_map/ppermute | solution.py:42
  68.6 10.1 %collective-permute-start.12 = (f16[64,512]{1,0:T(8,128)(2,1)S(1)}, f16[64,512]{1,0:T(8,128)(2,1)S(1)}, u32[]{:S(2)}, u32[]{:S(2)}) collective-permute-start(f16[64,512]{1,0:T(8,128)(2,1)S(1)} %bitcast.121), channel_id=1, source_target_pairs={{0,28},{1,29},{2,30},{3,31},{4,24},{5,25},{6,26},{7,27},{8,20},{9,... | collective-permute-start | bytes 196616 | tf_op jit(solution)/shard_map/ppermute | solution.py:42
  71.1 7.6 %collective-permute-start.11 = (f16[64,512]{1,0:T(8,128)(2,1)S(1)}, f16[64,512]{1,0:T(8,128)(2,1)S(1)}, u32[]{:S(2)}, u32[]{:S(2)}) collective-permute-start(f16[64,512]{1,0:T(8,128)(2,1)S(1)} %bitcast.120), channel_id=1, source_target_pairs={{0,24},{1,25},{2,26},{3,27},{4,28},{5,29},{6,30},{7,31},{8,16},{9,... | collective-permute-start | bytes 196616 | tf_op jit(solution)/shard_map/ppermute | solution.py:42
  118.7 14.3 %collective-permute-start.13 = (bf16[64,144,128]{2,1,0:T(8,128)(2,1)}, bf16[64,144,128]{2,1,0:T(8,128)(2,1)}, u32[]{:S(2)}, u32[]{:S(2)}) collective-permute-start(bf16[64,144,128]{2,1,0:T(8,128)(2,1)} %all_to_all.15.blocks), channel_id=1, source_target_pairs={{0,1},{1,0},{2,3},{3,2},{4,5},{5,4},{6,7},{7,6},{8,9},{9,8},{10,11... | collective-permute-start | bytes 7077896 | tf_op jit(solution)/shard_map/ppermute | solution.py:42
  118.7 22.9 %all-to-all-start.2 = ((f16[32,32,512]{2,1,0:T(8,128)(2,1)}), f16[32,32,512]{2,1,0:T(8,128)(2,1)S(1)}, u32[]{:S(2)}, u32[]{:S(2)}) async-start(f16[32,32,512]{2,1,0:T(8,128)(2,1)} %broadcast_in_dim.28), calls=%async_computation.2 | async-start | bytes 2097152 | tf_op jit(solution)/shard_map/all_to_all | solution.py:362

commit v5 on v4

--- a/solution.py
+++ b/solution.py
@@ -17,8 +17,7 @@
 D, KV, TOK = 4096, 512, 768
 BLK = 512
 HALF = D // 2
-ROWS = 144
-SUM_ROWS = 136
+ROWS = 136
 EXTRA = 128
 AXES = ("y", "zl", "x", "zh", "c")
 CHIPS = ("zh", "y", "zl", "x")
@@ -136,7 +135,7 @@
                 j, b * 32 : b * 32 + 32, :
             ]
     for j in range(0, BLK // 32, 4):
-        rows = [blocks[j + k, EXTRA : EXTRA + 16, :].astype(f32)[:1] for k in range(4)]
+        rows = [blocks[j + k, EXTRA : EXTRA + 8, :].astype(f32)[:1] for k in range(4)]
         lanes.append((rows[0] + rows[1]) + (rows[2] + rows[3]))
     gain = jnp.concatenate(lanes, axis=1)
     gain_out[...] = gain
@@ -277,8 +276,8 @@
             pl.BlockSpec((1, BLK), lambda i, core: (0, i % 2)),
             pl.BlockSpec((1, BLK), lambda i, core: (0, i % 2)),
         ],
-        (pl.BlockSpec((16, SUM_ROWS, 128), lambda i, core: (i, 0, 0)), whole((1, KV))),
-        (shape((64, SUM_ROWS, 128), f32), shape((1, KV), f32)),
+        (pl.BlockSpec((16, ROWS, 128), lambda i, core: (i, 0, 0)), whole((1, KV))),
+        (shape((64, ROWS, 128), f32), shape((1, KV), f32)),
         params=pltpu.CompilerParams(vmem_limit_bytes=40 * 1024 * 1024),
     )(
         core_at,
@@ -394,7 +393,7 @@
     new_vec_first = jnp.where(holds_gain, first_vec, vec_first)
     new_vec_second = jnp.where(holds_gain, second_vec, vec_second)
     back = jnp.tile(jnp.exp2(-ends[:, 0]), (1, 4))
-    grads, back, _ = lax.optimization_barrier((grads, back, next_values))
+    grads, back, new_gain = lax.optimization_barrier((grads, back, new_gain))
     rep_rows = grads.astype(f32) * back[:, None]
     old_first, old_second = mat_first.reshape(32, 32, KV), mat_second.reshape(32, 32, KV)
     first_mat = beta_first * old_first + (1.0 - beta_first) * rep_rows

time: 148 us -> 146 us (0.986)
  no operation moved by 1% of the time
where the time goes in v5:
time: 146 us
  blocking collectives  36.9 us (25%)
  starting transfers between devices  33.6 us (23%)
  Pallas kernels  32.5 us (22%)
  waiting for transfers between devices  17.8 us (12%)
  other arithmetic  16.9 us (12%)
  between operations  4.37 us (3%)
  local copies, waits for them, and re-layouts  3.52 us (2%)
    all_to_all x1, blocking collectives, body(): lax.all_to_all(jnp.broadcast_to(block[None], (64, ROWS, 128)), CHIPS, 0,...  36.9 us
    ppermute x14, starting transfers between devices, swap(): return lax.ppermute(block, AXES, pairs(mask, core))  17.1 us
    ppermute x14, waiting for transfers between devices, swap(): return lax.ppermute(block, AXES, pairs(mask, core))  16.5 us
    all_to_all x1, starting transfers between devices, body(): parts = lax.all_to_all(scaled.astype(f16), CHIPS, 0, 0, tiled=True)  11.4 us
    pallas_call x1, Pallas kernels, body(): call(chip_kernel, 4, [hid_spec, pl.BlockSpec((TOK, BLK), lambda i, core:...  10.5 us
    pallas_call x1, Pallas kernels, body(): call(last_kernel, 4, value_ins + [whole((TOK, KV)), any_spec, any_spec],...  6.63 us
    pallas_call x1, Pallas kernels, body(): call(first_kernel, 4, value_ins, (wide, gain_spec, whole((TOK, KV))), (sh...  6.22 us
    select_n x1, other arithmetic, body(): jnp.where(holds_weight, second_mat, old_second).reshape(1, 1024, KV)  5.28 us
  transfers between devices with their start and end apart: 16, of which 2 were waited for; matrix products, arithmetic and copies ran while one was open for 9% of the time, Pallas kernels for 19%

profile of v5, /device:TPU:2, one launch (start us, length us, event | category | flops | bytes accessed | tf_op | source)
XLA Modules:
  0.0 145.5 jit_solution(2760118455261341755)
XLA Ops:
  0.6 5.0 %shard_map.153 = (f32[768,128]{1,0:T(8,128)S(1)}, bf16[768,2048]{1,0:T(8,128)(2,1)}) custom-call(s32[1]{0:T(128)} %bitcast.4.core, bf16[768,4096]{1,0:T(8,128)(2,1)} %hid.5, bf16[768,512]{1,0:T(8,128)(2,1)} %grad.3), custom_call_target="tpu_custom_call" | custom-call | flops 1 | bytes 1 | tf_op jit(solution)/shard_map/pallas_call | solution.py:231
  6.3 2.0 %fusion.11 = (f16[256,512]{1,0:T(8,128)(2,1)S(1)}, f16[256,512]{1,0:T(8,128)(2,1)S(1)}, f16[256,512]{1,0:T(8,128)(2,1)S(1)}, f16[256,512]{1,0:T(8,128)(2,1)S(1)}...) fusion(f32[1,1024,512]{2,1,0:T(8,128)S(1)} %copy-done.3, ...), kind=kLoop, calls=%fused_computation.27 | loop fusion | flops 1048576 | bytes 6291472 | tf_op jit(solution)/shard_map/convert_element_type | solution.py:255
  8.5 3.1 %collective-permute-start.3 = (f16[512,512]{1,0:T(8,128)(2,1)S(1)}, f16[512,512]{1,0:T(8,128)(2,1)S(1)}, u32[]{:S(2)}, u32[]{:S(2)}) collective-permute-start(f16[512,512]{1,0:T(8,128)(2,1)S(1)} %pad_maximum_fusion), channel_id=1, source_target_pairs={{0,96},{1,97},{2,98},{3,99},{4,100},{5,101},{6,102},{7,103},{8,104... | collective-permute-start | bytes 1572872 | tf_op jit(solution)/shard_map/ppermute | solution.py:41
  11.7 0.7 collective-permute-start.4
  12.4 0.9 pad_maximum_fusion.2
  13.3 0.8 collective-permute-start.5
  14.2 0.6 fusion.40
  16.9 10.5 %shard_map.154 = (f32[64,136,128]{2,1,0:T(8,128)S(1)}, f32[1,512]{1,0:T(1,128)S(1)}) custom-call(s32[1]{0:T(128)} %bitcast.4.core, bf16[768,4096]{1,0:T(8,128)(2,1)} %hid.5, bf16[768,2048]{1,0:T(8,128)(2,1)} %collective-permute-done.got_hid, bf16[1,4096]{1,0:T(2,128)(2,1)S(1)} %reshape.252.gain, bf16[768,512]{1,0:T(8,128)(2,1)} %grad.3, ...), custom_call_target="tpu_custom_call" | custom-call | flops 1 | bytes 1 | tf_op jit(solution)/shard_map/pallas_call | solution.py:264
  27.4 1.7 %convert_element_type.143 = f16[64,136,128]{2,1,0:T(8,128)(2,1)} convert(f32[64,136,128]{2,1,0:T(8,128)S(1)} %get-tuple-element.41) | non-fusion elementwise | flops 1114112 | bytes 6684672 | tf_op jit(solution)/shard_map/convert_element_type | solution.py:313
  29.1 11.4 %all-to-all-start = ((f16[64,136,128]{2,1,0:T(8,128)(2,1)}), f16[64,136,128]{2,1,0:T(8,128)(2,1)}, u32[]{:S(2)}, u32[]{:S(2)}) async-start(f16[64,136,128]{2,1,0:T(8,128)(2,1)} %convert_element_type.143), calls=%async_computation | async-start | bytes 4456448 | tf_op jit(solution)/shard_map/all_to_all | solution.py:313
  40.9 4.2 %shard_map.155.inv = f32[768,128]{1,0:T(8,128)S(1)} custom-call(bf16[768,4096]{1,0:T(8,128)(2,1)} %hid.8), custom_call_target="tpu_custom_call" | custom-call | flops 16999999488 | bytes 1 | tf_op jit(solution)/shard_map/pallas_call | solution.py:296
  45.2 1.5 %collective-permute-start.10 = (f16[64,512]{1,0:T(8,128)(2,1)S(1)}, f16[64,512]{1,0:T(8,128)(2,1)S(1)}, u32[]{:S(2)}, u32[]{:S(2)}) collective-permute-start(f16[64,512]{1,0:T(8,128)(2,1)S(1)} %bitcast.126), channel_id=1, source_target_pairs={{0,20},{1,21},{2,22},{3,23},{4,16},{5,17},{6,18},{7,19},{8,28},{9,... | collective-permute-start | bytes 196616 | tf_op jit(solution)/shard_map/ppermute | solution.py:41
  47.2 2.1 %collective-permute-start.8 = (f16[64,512]{1,0:T(8,128)(2,1)S(1)}, f16[64,512]{1,0:T(8,128)(2,1)S(1)}, u32[]{:S(2)}, u32[]{:S(2)}) collective-permute-start(f16[64,512]{1,0:T(8,128)(2,1)S(1)} %bitcast.124), channel_id=1, source_target_pairs={{0,12},{1,13},{2,14},{3,15},{4,8},{5,9},{6,10},{7,11},{8,4},{9,5},... | collective-permute-start | bytes 196616 | tf_op jit(solution)/shard_map/ppermute | solution.py:41
  49.4 1.5 %collective-permute-start.7 = (f16[64,512]{1,0:T(8,128)(2,1)S(1)}, f16[64,512]{1,0:T(8,128)(2,1)S(1)}, u32[]{:S(2)}, u32[]{:S(2)}) collective-permute-start(f16[64,512]{1,0:T(8,128)(2,1)S(1)} %bitcast.123), channel_id=1, source_target_pairs={{0,8},{1,9},{2,10},{3,11},{4,12},{5,13},{6,14},{7,15},{8,0},{9,1},... | collective-permute-start | bytes 196616 | tf_op jit(solution)/shard_map/ppermute | solution.py:41
  50.8 0.6 collective-permute-start.6
  51.4 0.8 copy_bitcast_fusion.1
  52.2 16.5 %collective-permute-done.10 = f16[64,512]{1,0:T(8,128)(2,1)S(1)} collective-permute-done((f16[64,512]{1,0:T(8,128)(2,1)S(1)}, f16[64,512]{1,0:T(8,128)(2,1)S(1)}, u32[]{:S(2)}, u32[]{:S(2)}) %collective-permute-start.10) | collective-permute-done | bytes 65568 | tf_op jit(solution)/shard_map/ppermute | solution.py:41
  68.6 2.5 %collective-permute-start.12 = (f16[64,512]{1,0:T(8,128)(2,1)S(1)}, f16[64,512]{1,0:T(8,128)(2,1)S(1)}, u32[]{:S(2)}, u32[]{:S(2)}) collective-permute-start(f16[64,512]{1,0:T(8,128)(2,1)S(1)} %bitcast.121), channel_id=1, source_target_pairs={{0,28},{1,29},{2,30},{3,31},{4,24},{5,25},{6,26},{7,27},{8,20},{9,... | collective-permute-start | bytes 196616 | tf_op jit(solution)/shard_map/ppermute | solution.py:41
  71.1 3.2 %collective-permute-start.11 = (f16[64,512]{1,0:T(8,128)(2,1)S(1)}, f16[64,512]{1,0:T(8,128)(2,1)S(1)}, u32[]{:S(2)}, u32[]{:S(2)}) collective-permute-start(f16[64,512]{1,0:T(8,128)(2,1)S(1)} %bitcast.120), channel_id=1, source_target_pairs={{0,24},{1,25},{2,26},{3,27},{4,28},{5,29},{6,30},{7,31},{8,16},{9,... | collective-permute-start | bytes 196616 | tf_op jit(solution)/shard_map/ppermute | solution.py:41
  74.4 0.7 convert_multiply_fusion.1
  75.2 1.0 multiply_exponential_fusion
  76.1 2.1 %multiply_reduce_fusion = f32[136,128]{1,0:T(8,128)S(1)} fusion(f16[64,136,128]{2,1,0:T(8,128)(2,1)} %all-to-all-done, f32[64,128]{1,0:T(8,128)S(1)} %bitcast.116), kind=kLoop, calls=%fused_computation | loop fusion | flops 3324928 | bytes 2330624 | tf_op jit(solution)/shard_map/reduce_sum | solution.py:317
  78.7 1.1 broadcast_in_dim.28
  80.5 36.9 %all_to_all.15.blocks = bf16[64,136,128]{2,1,0:T(8,128)(2,1)} all-to-all(bf16[64,136,128]{2,1,0:T(8,128)(2,1)S(1)} %broadcast_in_dim.33), channel_id=1, replica_groups=mesh['y'=4,'zl'=2,'x'=4,'zh'=2,'c'=2] {'zh','y','zl','x'}, dimensions={0} | all-to-all | bytes 4456448 | tf_op jit(solution)/shard_map/all_to_all | solution.py:357
  117.3 5.1 %all-to-all-start.2 = ((f16[32,32,512]{2,1,0:T(8,128)(2,1)}), f16[32,32,512]{2,1,0:T(8,128)(2,1)S(1)}, u32[]{:S(2)}, u32[]{:S(2)}) async-start(f16[32,32,512]{2,1,0:T(8,128)(2,1)} %broadcast_in_dim.28), calls=%async_computation.2 | async-start | bytes 2097152 | tf_op jit(solution)/shard_map/all_to_all | solution.py:361
  123.7 6.2 %shard_map.156 = (bf16[4096,512]{1,0:T(8,128)(2,1)}, f32[1,4096]{1,0:T(1,128)S(1)}, f32[768,512]{1,0:T(8,128)S(1)}) custom-call(s32[1]{0:T(128)} %bitcast.4.core, bf16[64,136,128]{2,1,0:T(8,128)(2,1)} %all_to_all.15.blocks, bf16[768,4096]{1,0:T(8,128)(2,1)} %hid.8, f32[768,128]{1,0:T(8,128)S(1)} %shard_map.155.inv), custom_call_target="tpu_custom_call" | custom-call | flops 1 | bytes 1 | tf_op jit(solution)/shard_map/pallas_call | solution.py:370
  129.9 0.9 slice.83
  131.0 0.6 broadcast_select_fusion
  131.6 6.6 %shard_map.157 = (bf16[4096,512]{1,0:T(8,128)(2,1)}, f32[1,4096]{1,0:T(1,128)S(1)}, bf16[768,512]{1,0:T(8,128)(2,1)}) custom-call(s32[1]{0:T(128)} %bitcast.core, bf16[64,136,128]{2,1,0:T(8,128)(2,1)} %collective-permute-done.13.blocks, bf16[768,4096]{1,0:T(8,128)(2,1)} %hid.8, ...), custom_call_target="tpu_custom_call", output_to_operand_aliasing={{0}: (5, {}), {1}: (6, {})} | custom-call | flops 1 | bytes 1 | tf_op jit(solution)/shard_map/pallas_call | solution.py:377
  138.2 0.6 convert_reduce_fusion
  138.9 1.3 all-to-all-done.2
  140.2 5.3 %fusion.1 = (f32[32,32,512]{2,1,0:T(8,128)}, f32[32,32,512]{2,1,0:T(8,128)}) fusion(f32[32,32,512]{2,1,0:T(8,128)} %bitcast.108, f16[32,32,512]{2,1,0:T(8,128)(2,1)S(1)} %all-to-all-done.2, f32[32,512]{1,0:T(8,128)S(1)} %bitcast.112, pred[]{:T(512)S(6)} %eq.73, f32[32,32,512]{2,1,0:T(8,128)} %bitcast.107), kind=kLoop, calls=%fused_computation.3 | loop fusion | flops 5767168 | bytes 9502721 | tf_op jit(solution)/shard_map/jit(_where)/select_n | solution.py:402
  (71 shorter events, 3.2 us)
Async XLA Ops:
  0.6 5.6 %copy-start.3 = (f32[1,1024,512]{2,1,0:T(8,128)S(1)}, f32[1,1024,512]{2,1,0:T(8,128)}, u32[]{:S(2)}) copy-start(f32[1,1024,512]{2,1,0:T(8,128)} %param.15) | copy-start | bytes 6291460
  5.7 2.6 %copy-start = (f32[768,128]{1,0:T(8,128)}, f32[768,128]{1,0:T(8,128)S(1)}, u32[]{:S(2)}) copy-start(f32[768,128]{1,0:T(8,128)S(1)} %get-tuple-element.40.inv) | copy-start | bytes 1179652
  5.7 11.3 %collective-permute-start = (bf16[768,2048]{1,0:T(8,128)(2,1)}, bf16[768,2048]{1,0:T(8,128)(2,1)}, u32[]{:S(2)}, u32[]{:S(2)}) collective-permute-start(bf16[768,2048]{1,0:T(8,128)(2,1)} %get-tuple-element.39), channel_id=1, source_target_pairs={{0,1},{1,0},{2,3},{3,2},{4,5},{5,4},{6,7},{7,6},{8,9},{9,8},{10,11... | collective-permute-start | bytes 9437192 | tf_op jit(solution)/shard_map/ppermute | solution.py:41
  5.7 11.2 %collective-permute-start.1 = (bf16[768,512]{1,0:T(8,128)(2,1)}, bf16[768,512]{1,0:T(8,128)(2,1)}, u32[]{:S(2)}, u32[]{:S(2)}) collective-permute-start(bf16[768,512]{1,0:T(8,128)(2,1)} %grad.3), channel_id=1, source_target_pairs={{0,1},{1,0},{2,3},{3,2},{4,5},{5,4},{6,7},{7,6},{8,9},{9,8},{10,11... | collective-permute-start | bytes 2359304 | tf_op jit(solution)/shard_map/ppermute | solution.py:41
  6.2 7.2 %collective-permute-start.2 = (f32[768,128]{1,0:T(8,128)S(1)}, f32[768,128]{1,0:T(8,128)}, u32[]{:S(2)}, u32[]{:S(2)}) collective-permute-start(f32[768,128]{1,0:T(8,128)S(1)} %get-tuple-element.40.inv), channel_id=1, source_target_pairs={{0,1},{1,0},{2,3},{3,2},{4,5},{5,4},{6,7},{7,6},{8,9},{9,8},{10,11... | collective-permute-start | bytes 1179656 | tf_op jit(solution)/shard_map/ppermute | solution.py:41
  8.3 5.9 %copy-start.5 = (s32[2]{0:T(128)S(1)}, s32[2]{0:T(128)}, u32[]{:S(2)}) copy-start(s32[2]{0:T(128)} %param.14) | copy-start | bytes 28
  8.3 8.4 %copy-start.4 = (bf16[4096]{0:T(1024)(128)(2,1)S(1)}, bf16[4096]{0:T(1024)(128)(2,1)}, u32[]{:S(2)}) copy-start(bf16[4096]{0:T(1024)(128)(2,1)} %param.13) | copy-start | bytes 24580
  8.3 8.6 %copy-start.1 = (f32[1,1024]{1,0:T(1,128)S(1)}, f32[1,1024]{1,0:T(1,128)}, u32[]{:S(2)}) copy-start(f32[1,1024]{1,0:T(1,128)} %firsts.1) | copy-start | bytes 12292
  8.4 8.6 %copy-start.2 = (f32[1,1024]{1,0:T(1,128)S(1)}, f32[1,1024]{1,0:T(1,128)}, u32[]{:S(2)}) copy-start(f32[1,1024]{1,0:T(1,128)} %seconds.1) | copy-start | bytes 12292
  8.5 32.0 %collective-permute-start.3 = (f16[512,512]{1,0:T(8,128)(2,1)S(1)}, f16[512,512]{1,0:T(8,128)(2,1)S(1)}, u32[]{:S(2)}, u32[]{:S(2)}) collective-permute-start(f16[512,512]{1,0:T(8,128)(2,1)S(1)} %pad_maximum_fusion), channel_id=1, source_target_pairs={{0,96},{1,97},{2,98},{3,99},{4,100},{5,101},{6,102},{7,103},{8,104... | collective-permute-start | bytes 1572872 | tf_op jit(solution)/shard_map/ppermute | solution.py:41
  11.7 28.7 %collective-permute-start.4 = (f16[512,512]{1,0:T(8,128)(2,1)S(1)}, f16[512,512]{1,0:T(8,128)(2,1)S(1)}, u32[]{:S(2)}, u32[]{:S(2)}) collective-permute-start(f16[512,512]{1,0:T(8,128)(2,1)S(1)} %pad_maximum_fusion.1), channel_id=1, source_target_pairs={{0,64},{1,65},{2,66},{3,67},{4,68},{5,69},{6,70},{7,71},{8,72},{9,... | collective-permute-start | bytes 1572872 | tf_op jit(solution)/shard_map/ppermute | solution.py:41
  13.3 27.1 %collective-permute-start.5 = (f16[512,512]{1,0:T(8,128)(2,1)}, f16[512,512]{1,0:T(8,128)(2,1)S(1)}, u32[]{:S(2)}, u32[]{:S(2)}) collective-permute-start(f16[512,512]{1,0:T(8,128)(2,1)} %pad_maximum_fusion.2), channel_id=1, source_target_pairs={{0,32},{1,33},{2,34},{3,35},{4,36},{5,37},{6,38},{7,39},{8,40},{9,... | collective-permute-start | bytes 1572872 | tf_op jit(solution)/shard_map/ppermute | solution.py:41
  29.1 45.3 %all-to-all-start = ((f16[64,136,128]{2,1,0:T(8,128)(2,1)}), f16[64,136,128]{2,1,0:T(8,128)(2,1)}, u32[]{:S(2)}, u32[]{:S(2)}) async-start(f16[64,136,128]{2,1,0:T(8,128)(2,1)} %convert_element_type.143), calls=%async_computation | async-start | bytes 4456448 | tf_op jit(solution)/shard_map/all_to_all | solution.py:313
  45.2 23.5 %collective-permute-start.10 = (f16[64,512]{1,0:T(8,128)(2,1)S(1)}, f16[64,512]{1,0:T(8,128)(2,1)S(1)}, u32[]{:S(2)}, u32[]{:S(2)}) collective-permute-start(f16[64,512]{1,0:T(8,128)(2,1)S(1)} %bitcast.126), channel_id=1, source_target_pairs={{0,20},{1,21},{2,22},{3,23},{4,16},{5,17},{6,18},{7,19},{8,28},{9,... | collective-permute-start | bytes 196616 | tf_op jit(solution)/shard_map/ppermute | solution.py:41
  46.7 24.4 %collective-permute-start.9 = (f16[64,512]{1,0:T(8,128)(2,1)S(1)}, f16[64,512]{1,0:T(8,128)(2,1)S(1)}, u32[]{:S(2)}, u32[]{:S(2)}) collective-permute-start(f16[64,512]{1,0:T(8,128)(2,1)S(1)} %bitcast.125), channel_id=1, source_target_pairs={{0,16},{1,17},{2,18},{3,19},{4,20},{5,21},{6,22},{7,23},{8,24},{9,... | collective-permute-start | bytes 196616 | tf_op jit(solution)/shard_map/ppermute | solution.py:41
  47.2 27.1 %collective-permute-start.8 = (f16[64,512]{1,0:T(8,128)(2,1)S(1)}, f16[64,512]{1,0:T(8,128)(2,1)S(1)}, u32[]{:S(2)}, u32[]{:S(2)}) collective-permute-start(f16[64,512]{1,0:T(8,128)(2,1)S(1)} %bitcast.124), channel_id=1, source_target_pairs={{0,12},{1,13},{2,14},{3,15},{4,8},{5,9},{6,10},{7,11},{8,4},{9,5},... | collective-permute-start | bytes 196616 | tf_op jit(solution)/shard_map/ppermute | solution.py:41
  49.4 25.0 %collective-permute-start.7 = (f16[64,512]{1,0:T(8,128)(2,1)S(1)}, f16[64,512]{1,0:T(8,128)(2,1)S(1)}, u32[]{:S(2)}, u32[]{:S(2)}) collective-permute-start(f16[64,512]{1,0:T(8,128)(2,1)S(1)} %bitcast.123), channel_id=1, source_target_pairs={{0,8},{1,9},{2,10},{3,11},{4,12},{5,13},{6,14},{7,15},{8,0},{9,1},... | collective-permute-start | bytes 196616 | tf_op jit(solution)/shard_map/ppermute | solution.py:41
  50.8 23.5 %collective-permute-start.6 = (f16[64,512]{1,0:T(8,128)(2,1)S(1)}, f16[64,512]{1,0:T(8,128)(2,1)S(1)}, u32[]{:S(2)}, u32[]{:S(2)}) collective-permute-start(f16[64,512]{1,0:T(8,128)(2,1)S(1)} %bitcast.122), channel_id=1, source_target_pairs={{0,4},{1,5},{2,6},{3,7},{4,0},{5,1},{6,2},{7,3},{8,12},{9,13},{10,... | collective-permute-start | bytes 196616 | tf_op jit(solution)/shard_map/ppermute | solution.py:41
  68.6 10.1 %collective-permute-start.12 = (f16[64,512]{1,0:T(8,128)(2,1)S(1)}, f16[64,512]{1,0:T(8,128)(2,1)S(1)}, u32[]{:S(2)}, u32[]{:S(2)}) collective-permute-start(f16[64,512]{1,0:T(8,128)(2,1)S(1)} %bitcast.121), channel_id=1, source_target_pairs={{0,28},{1,29},{2,30},{3,31},{4,24},{5,25},{6,26},{7,27},{8,20},{9,... | collective-permute-start | bytes 196616 | tf_op jit(solution)/shard_map/ppermute | solution.py:41
  71.1 7.6 %collective-permute-start.11 = (f16[64,512]{1,0:T(8,128)(2,1)S(1)}, f16[64,512]{1,0:T(8,128)(2,1)S(1)}, u32[]{:S(2)}, u32[]{:S(2)}) collective-permute-start(f16[64,512]{1,0:T(8,128)(2,1)S(1)} %bitcast.120), channel_id=1, source_target_pairs={{0,24},{1,25},{2,26},{3,27},{4,28},{5,29},{6,30},{7,31},{8,16},{9,... | collective-permute-start | bytes 196616 | tf_op jit(solution)/shard_map/ppermute | solution.py:41
  117.3 14.3 %collective-permute-start.13 = (bf16[64,136,128]{2,1,0:T(8,128)(2,1)}, bf16[64,136,128]{2,1,0:T(8,128)(2,1)}, u32[]{:S(2)}, u32[]{:S(2)}) collective-permute-start(bf16[64,136,128]{2,1,0:T(8,128)(2,1)} %all_to_all.15.blocks), channel_id=1, source_target_pairs={{0,1},{1,0},{2,3},{3,2},{4,5},{5,4},{6,7},{7,6},{8,9},{9,8},{10,11... | collective-permute-start | bytes 6684680 | tf_op jit(solution)/shard_map/ppermute | solution.py:41
  117.3 22.9 %all-to-all-start.2 = ((f16[32,32,512]{2,1,0:T(8,128)(2,1)}), f16[32,32,512]{2,1,0:T(8,128)(2,1)S(1)}, u32[]{:S(2)}, u32[]{:S(2)}) async-start(f16[32,32,512]{2,1,0:T(8,128)(2,1)} %broadcast_in_dim.28), calls=%async_computation.2 | async-start | bytes 2097152 | tf_op jit(solution)/shard_map/all_to_all | solution.py:361

commit v6 on v5

--- a/solution.py
+++ b/solution.py
@@ -303,16 +303,17 @@
         cost_estimate=pl.CostEstimate(flops=17 * 10**9, transcendentals=0, bytes_accessed=1),
     )(lax.optimization_barrier((next_hidden, moments))[0])
     moments, next_inv = lax.optimization_barrier((moments, next_inv))
-    moments = moments.reshape(2, 8, 32, KV)
-    last_picks = [
-        lax.dynamic_index_in_dim(moments, (zl * 4 + x) ^ k, 1, keepdims=False).reshape(64, KV)
-        for k in range(8)
-    ]
-    arrived = [swap(last_picks[k], k) for k in range(1, 8)]
+    moments = moments.reshape(2, 2, 4, 32, KV)
+    near = [lax.dynamic_index_in_dim(moments, x ^ k, 2, keepdims=False) for k in range(4)]
+    arrived = [swap(near[k], k) for k in range(1, 4)]
 
     parts = lax.all_to_all(scaled.astype(f16), CHIPS, 0, 0, tiled=True)
-    parts, early = lax.optimization_barrier((parts, arrived[:5]))
-    arrived = early + arrived[5:]
+    parts, arrived = lax.optimization_barrier((parts, arrived))
+    near = near[0]
+    for k in range(1, 4):
+        near = jnp.where((x ^ k) == (owner_weight & 3), arrived[k - 1], near)
+    kept, passed = [lax.dynamic_index_in_dim(near, zl ^ k, 1, keepdims=False) for k in range(2)]
+    arrived = swap(passed, 4)
     back = jnp.exp2(-parts[:, EXTRA + 3].astype(f32))
     summed = jnp.sum(parts.astype(f32) * back[:, None], axis=0)
     grad_rows = summed[:EXTRA]
@@ -340,10 +341,7 @@
     rows = [gain_lanes, power, high, middle, lanes - high - middle]
     rows = jnp.stack([row.astype(bf16) for row in rows])
     arrived, grad_rows, sent, rows = lax.optimization_barrier((arrived, grad_rows, sent, rows))
-    old_mats = last_picks[0]
-    for k in range(1, 8):
-        source = (zl * 4 + x) ^ k == (owner_weight & 7)
-        old_mats = jnp.where(source, arrived[k - 1], old_mats)
+    old_mats = jnp.where(((owner_weight >> 2) & 1) == zl, kept, arrived).reshape(64, KV)
     old_mats = old_mats.astype(f32)
 
     own_rows = blocked(lax.dynamic_slice_in_dim(value_weight, first_row, 32))

time: 146 us -> 149 us (1.021)
  starting transfers between devices: 33.6 us -> 27.8 us
  waiting for transfers between devices: 17.8 us -> 23.4 us
    ppermute x14 -> x11, starting transfers between devices: 17.1 us -> 11.2 us  [swap(): return lax.ppermute(block, AXES, pairs(mask, core))]
    ppermute x14 -> x11, waiting for transfers between devices: 16.5 us -> 21.5 us  [swap(): return lax.ppermute(block, AXES, pairs(mask, core))]
  transfers between devices with their start and end apart: 16 -> 13, of which waited for: 2 -> 4; matrix products, arithmetic and copies ran while one was open for 9% -> 7% of each run, Pallas kernels for 19% -> 19%
where the time goes in v6:
time: 149 us; the launch traced here: 148 us
  blocking collectives  37.7 us (25%)
  Pallas kernels  32.7 us (22%)
  starting transfers between devices  27.8 us (19%)
  waiting for transfers between devices  23.4 us (16%)
  other arithmetic  16.9 us (11%)
  between operations  4.96 us (3%)
  local copies, waits for them, and re-layouts  4.22 us (3%)
    all_to_all x1, blocking collectives, body(): lax.all_to_all(jnp.broadcast_to(block[None], (64, ROWS, 128)), CHIPS, 0,...  37.7 us
    ppermute x11, waiting for transfers between devices, swap(): return lax.ppermute(block, AXES, pairs(mask, core))  21.5 us
    all_to_all x1, starting transfers between devices, body(): parts = lax.all_to_all(scaled.astype(f16), CHIPS, 0, 0, tiled=True)  11.4 us
    ppermute x11, starting transfers between devices, swap(): return lax.ppermute(block, AXES, pairs(mask, core))  11.2 us
    pallas_call x1, Pallas kernels, body(): call(chip_kernel, 4, [hid_spec, pl.BlockSpec((TOK, BLK), lambda i, core:...  10.5 us
    pallas_call x1, Pallas kernels, body(): call(last_kernel, 4, value_ins + [whole((TOK, KV)), any_spec, any_spec],...  6.68 us
    pallas_call x1, Pallas kernels, body(): call(first_kernel, 4, value_ins, (wide, gain_spec, whole((TOK, KV))), (sh...  6.31 us
    select_n x1, other arithmetic, body(): jnp.where(holds_weight, second_mat, old_second).reshape(1, 1024, KV)  5.32 us
  transfers between devices with their start and end apart: 13, of which 4 were waited for; matrix products, arithmetic and copies ran while one was open for 7% of the time, Pallas kernels for 19%

profile of v6, /device:TPU:2, one launch (start us, length us, event | category | flops | bytes accessed | tf_op | source)
XLA Modules:
  0.0 147.7 jit_solution(8235657000007177619)
XLA Ops:
  0.6 5.0 %shard_map.153 = (f32[768,128]{1,0:T(8,128)S(1)}, bf16[768,2048]{1,0:T(8,128)(2,1)}) custom-call(s32[1]{0:T(128)} %bitcast.4.core, bf16[768,4096]{1,0:T(8,128)(2,1)} %hid.5, bf16[768,512]{1,0:T(8,128)(2,1)} %grad.3), custom_call_target="tpu_custom_call" | custom-call | flops 1 | bytes 1 | tf_op jit(solution)/shard_map/pallas_call | solution.py:231
  6.3 2.1 %fusion.11 = (f16[256,512]{1,0:T(8,128)(2,1)S(1)}, f16[256,512]{1,0:T(8,128)(2,1)S(1)}, f16[256,512]{1,0:T(8,128)(2,1)S(1)}, f16[256,512]{1,0:T(8,128)(2,1)S(1)}...) fusion(f32[1,1024,512]{2,1,0:T(8,128)S(1)} %copy-done.3, ...), kind=kLoop, calls=%fused_computation.27 | loop fusion | flops 1048576 | bytes 6291472 | tf_op jit(solution)/shard_map/convert_element_type | solution.py:255
  8.5 3.1 %collective-permute-start.3 = (f16[512,512]{1,0:T(8,128)(2,1)S(1)}, f16[512,512]{1,0:T(8,128)(2,1)S(1)}, u32[]{:S(2)}, u32[]{:S(2)}) collective-permute-start(f16[512,512]{1,0:T(8,128)(2,1)S(1)} %pad_maximum_fusion), channel_id=1, source_target_pairs={{0,96},{1,97},{2,98},{3,99},{4,100},{5,101},{6,102},{7,103},{8,104... | collective-permute-start | bytes 1572872 | tf_op jit(solution)/shard_map/ppermute | solution.py:41
  11.7 0.7 collective-permute-start.4
  12.4 0.9 pad_maximum_fusion.2
  13.4 0.8 collective-permute-start.5
  14.2 1.3 fusion.36
  16.2 10.5 %shard_map.154 = (f32[64,136,128]{2,1,0:T(8,128)S(1)}, f32[1,512]{1,0:T(1,128)S(1)}) custom-call(s32[1]{0:T(128)} %bitcast.4.core, bf16[768,4096]{1,0:T(8,128)(2,1)} %hid.5, bf16[768,2048]{1,0:T(8,128)(2,1)} %collective-permute-done.got_hid, bf16[1,4096]{1,0:T(2,128)(2,1)S(1)} %reshape.226.gain, bf16[768,512]{1,0:T(8,128)(2,1)} %grad.3, ...), custom_call_target="tpu_custom_call" | custom-call | flops 1 | bytes 1 | tf_op jit(solution)/shard_map/pallas_call | solution.py:264
  26.7 1.7 %convert_element_type.144 = f16[64,136,128]{2,1,0:T(8,128)(2,1)} convert(f32[64,136,128]{2,1,0:T(8,128)S(1)} %get-tuple-element.33) | non-fusion elementwise | flops 1114112 | bytes 6684672 | tf_op jit(solution)/shard_map/convert_element_type | solution.py:310
  28.3 11.4 %all-to-all-start = ((f16[64,136,128]{2,1,0:T(8,128)(2,1)}), f16[64,136,128]{2,1,0:T(8,128)(2,1)}, u32[]{:S(2)}, u32[]{:S(2)}) async-start(f16[64,136,128]{2,1,0:T(8,128)(2,1)} %convert_element_type.144), calls=%async_computation | async-start | bytes 4456448 | tf_op jit(solution)/shard_map/all_to_all | solution.py:310
  40.1 4.2 %shard_map.155.inv = f32[768,128]{1,0:T(8,128)S(1)} custom-call(bf16[768,4096]{1,0:T(8,128)(2,1)} %hid.8), custom_call_target="tpu_custom_call" | custom-call | flops 16999999488 | bytes 1 | tf_op jit(solution)/shard_map/pallas_call | solution.py:296
  44.4 1.5 %collective-permute-start.8 = (f16[2,2,32,512]{3,2,1,0:T(8,128)(2,1)S(1)}, f16[2,2,32,512]{3,2,1,0:T(8,128)(2,1)S(1)}, u32[]{:S(2)}, u32[]{:S(2)}) collective-permute-start(f16[2,2,32,512]{3,2,1,0:T(8,128)(2,1)S(1)} %get-tuple-element.70), channel_id=1, source_target_pairs={{0,12},{1,13},{2,14},{3,15},{4,8},{5,9},{6,10},{7,11},{8,4},{9,5},... | collective-permute-start | bytes 393224 | tf_op jit(solution)/shard_map/ppermute | solution.py:41
  46.0 1.1 collective-permute-start.7
  47.1 1.5 %collective-permute-start.6 = (f16[2,2,32,512]{3,2,1,0:T(8,128)(2,1)S(1)}, f16[2,2,32,512]{3,2,1,0:T(8,128)(2,1)S(1)}, u32[]{:S(2)}, u32[]{:S(2)}) collective-permute-start(f16[2,2,32,512]{3,2,1,0:T(8,128)(2,1)S(1)} %get-tuple-element.72), channel_id=1, source_target_pairs={{0,4},{1,5},{2,6},{3,7},{4,0},{5,1},{6,2},{7,3},{8,12},{9,13},{10,... | collective-permute-start | bytes 393224 | tf_op jit(solution)/shard_map/ppermute | solution.py:41
  50.7 0.8 copy_bitcast_fusion.1
  51.4 19.1 %collective-permute-done.8 = f16[2,2,32,512]{3,2,1,0:T(8,128)(2,1)S(1)} collective-permute-done((f16[2,2,32,512]{3,2,1,0:T(8,128)(2,1)S(1)}, f16[2,2,32,512]{3,2,1,0:T(8,128)(2,1)S(1)}, u32[]{:S(2)}, u32[]{:S(2)}) %collective-permute-start.8) | collective-permute-done | bytes 131104 | tf_op jit(solution)/shard_map/ppermute | solution.py:41
  70.5 0.7 all-to-all-done
  71.2 0.7 convert_multiply_fusion.1
  72.0 1.0 multiply_exponential_fusion
  73.0 2.1 %multiply_reduce_fusion = f32[136,128]{1,0:T(8,128)S(1)} fusion(f16[64,136,128]{2,1,0:T(8,128)(2,1)} %all-to-all-done, f32[64,128]{1,0:T(8,128)S(1)} %bitcast.112), kind=kLoop, calls=%fused_computation | loop fusion | flops 3324928 | bytes 2330624 | tf_op jit(solution)/shard_map/reduce_sum | solution.py:318
  75.6 1.9 %collective-permute-start.9 = (f16[2,32,512]{2,1,0:T(8,128)(2,1)S(1)}, f16[2,32,512]{2,1,0:T(8,128)(2,1)S(1)}, u32[]{:S(2)}, u32[]{:S(2)}) collective-permute-start(f16[2,32,512]{2,1,0:T(8,128)(2,1)S(1)} %dynamic-slice_bitcast_fusion.3), channel_id=1, source_target_pairs={{0,16},{1,17},{2,18},{3,19},{4,20},{5,21},{6,22},{7,23},{8,24},{9,... | collective-permute-start | bytes 196616 | tf_op jit(solution)/shard_map/ppermute | solution.py:41
  77.5 2.4 %collective-permute-done.9 = f16[2,32,512]{2,1,0:T(8,128)(2,1)S(1)} collective-permute-done((f16[2,32,512]{2,1,0:T(8,128)(2,1)S(1)}, f16[2,32,512]{2,1,0:T(8,128)(2,1)S(1)}, u32[]{:S(2)}, u32[]{:S(2)}) %collective-permute-start.9) | collective-permute-done | bytes 65568 | tf_op jit(solution)/shard_map/ppermute | solution.py:41
  79.9 1.1 broadcast_in_dim.28
  81.6 37.7 %all_to_all.15.blocks = bf16[64,136,128]{2,1,0:T(8,128)(2,1)} all-to-all(bf16[64,136,128]{2,1,0:T(8,128)(2,1)S(1)} %broadcast_in_dim.33), channel_id=1, replica_groups=mesh['y'=4,'zl'=2,'x'=4,'zh'=2,'c'=2] {'zh','y','zl','x'}, dimensions={0} | all-to-all | bytes 4456448 | tf_op jit(solution)/shard_map/all_to_all | solution.py:355
  119.3 5.2 %all-to-all-start.2 = ((f16[32,32,512]{2,1,0:T(8,128)(2,1)}), f16[32,32,512]{2,1,0:T(8,128)(2,1)S(1)}, u32[]{:S(2)}, u32[]{:S(2)}) async-start(f16[32,32,512]{2,1,0:T(8,128)(2,1)} %broadcast_in_dim.28), calls=%async_computation.2 | async-start | bytes 2097152 | tf_op jit(solution)/shard_map/all_to_all | solution.py:359
  125.9 6.3 %shard_map.156 = (bf16[4096,512]{1,0:T(8,128)(2,1)}, f32[1,4096]{1,0:T(1,128)S(1)}, f32[768,512]{1,0:T(8,128)S(1)}) custom-call(s32[1]{0:T(128)} %bitcast.4.core, bf16[64,136,128]{2,1,0:T(8,128)(2,1)} %all_to_all.15.blocks, bf16[768,4096]{1,0:T(8,128)(2,1)} %hid.8, f32[768,128]{1,0:T(8,128)S(1)} %shard_map.155.inv), custom_call_target="tpu_custom_call" | custom-call | flops 1 | bytes 1 | tf_op jit(solution)/shard_map/pallas_call | solution.py:368
  132.2 0.9 slice.85
  133.3 0.6 broadcast_select_fusion
  133.9 6.7 %shard_map.157 = (bf16[4096,512]{1,0:T(8,128)(2,1)}, f32[1,4096]{1,0:T(1,128)S(1)}, bf16[768,512]{1,0:T(8,128)(2,1)}) custom-call(s32[1]{0:T(128)} %bitcast.core, bf16[64,136,128]{2,1,0:T(8,128)(2,1)} %collective-permute-done.10.blocks, bf16[768,4096]{1,0:T(8,128)(2,1)} %hid.8, ...), custom_call_target="tpu_custom_call", output_to_operand_aliasing={{0}: (5, {}), {1}: (6, {})} | custom-call | flops 1 | bytes 1 | tf_op jit(solution)/shard_map/pallas_call | solution.py:375
  140.6 0.6 convert_reduce_fusion
  141.2 1.2 all-to-all-done.2
  142.4 5.3 %fusion.1 = (f32[32,32,512]{2,1,0:T(8,128)}, f32[32,32,512]{2,1,0:T(8,128)}) fusion(f32[32,32,512]{2,1,0:T(8,128)} %bitcast.103, f16[32,32,512]{2,1,0:T(8,128)(2,1)S(1)} %all-to-all-done.2, f32[32,512]{1,0:T(8,128)S(1)} %bitcast.108, pred[]{:T(512)S(6)} %eq.61, f32[32,32,512]{2,1,0:T(8,128)} %bitcast.102), kind=kLoop, calls=%fused_computation.3 | loop fusion | flops 5767168 | bytes 9502721 | tf_op jit(solution)/shard_map/jit(_where)/select_n | solution.py:400
  (65 shorter events, 2.7 us)
Async XLA Ops:
  0.6 5.6 %copy-start.3 = (f32[1,1024,512]{2,1,0:T(8,128)S(1)}, f32[1,1024,512]{2,1,0:T(8,128)}, u32[]{:S(2)}) copy-start(f32[1,1024,512]{2,1,0:T(8,128)} %param.15) | copy-start | bytes 6291460
  5.7 2.7 %copy-start = (f32[768,128]{1,0:T(8,128)}, f32[768,128]{1,0:T(8,128)S(1)}, u32[]{:S(2)}) copy-start(f32[768,128]{1,0:T(8,128)S(1)} %get-tuple-element.32.inv) | copy-start | bytes 1179652
  5.7 10.5 %collective-permute-start = (bf16[768,2048]{1,0:T(8,128)(2,1)}, bf16[768,2048]{1,0:T(8,128)(2,1)}, u32[]{:S(2)}, u32[]{:S(2)}) collective-permute-start(bf16[768,2048]{1,0:T(8,128)(2,1)} %get-tuple-element.31), channel_id=1, source_target_pairs={{0,1},{1,0},{2,3},{3,2},{4,5},{5,4},{6,7},{7,6},{8,9},{9,8},{10,11... | collective-permute-start | bytes 9437192 | tf_op jit(solution)/shard_map/ppermute | solution.py:41
  5.7 10.5 %collective-permute-start.1 = (bf16[768,512]{1,0:T(8,128)(2,1)}, bf16[768,512]{1,0:T(8,128)(2,1)}, u32[]{:S(2)}, u32[]{:S(2)}) collective-permute-start(bf16[768,512]{1,0:T(8,128)(2,1)} %grad.3), channel_id=1, source_target_pairs={{0,1},{1,0},{2,3},{3,2},{4,5},{5,4},{6,7},{7,6},{8,9},{9,8},{10,11... | collective-permute-start | bytes 2359304 | tf_op jit(solution)/shard_map/ppermute | solution.py:41
  6.2 7.2 %collective-permute-start.2 = (f32[768,128]{1,0:T(8,128)S(1)}, f32[768,128]{1,0:T(8,128)}, u32[]{:S(2)}, u32[]{:S(2)}) collective-permute-start(f32[768,128]{1,0:T(8,128)S(1)} %get-tuple-element.32.inv), channel_id=1, source_target_pairs={{0,1},{1,0},{2,3},{3,2},{4,5},{5,4},{6,7},{7,6},{8,9},{9,8},{10,11... | collective-permute-start | bytes 1179656 | tf_op jit(solution)/shard_map/ppermute | solution.py:41
  8.3 7.8 %copy-start.4 = (bf16[4096]{0:T(1024)(128)(2,1)S(1)}, bf16[4096]{0:T(1024)(128)(2,1)}, u32[]{:S(2)}) copy-start(bf16[4096]{0:T(1024)(128)(2,1)} %param.13) | copy-start | bytes 24580
  8.3 7.9 %copy-start.1 = (f32[1,1024]{1,0:T(1,128)S(1)}, f32[1,1024]{1,0:T(1,128)}, u32[]{:S(2)}) copy-start(f32[1,1024]{1,0:T(1,128)} %firsts.1) | copy-start | bytes 12292
  8.4 7.9 %copy-start.2 = (f32[1,1024]{1,0:T(1,128)S(1)}, f32[1,1024]{1,0:T(1,128)}, u32[]{:S(2)}) copy-start(f32[1,1024]{1,0:T(1,128)} %seconds.1) | copy-start | bytes 12292
  8.5 31.2 %collective-permute-start.3 = (f16[512,512]{1,0:T(8,128)(2,1)S(1)}, f16[512,512]{1,0:T(8,128)(2,1)S(1)}, u32[]{:S(2)}, u32[]{:S(2)}) collective-permute-start(f16[512,512]{1,0:T(8,128)(2,1)S(1)} %pad_maximum_fusion), channel_id=1, source_target_pairs={{0,96},{1,97},{2,98},{3,99},{4,100},{5,101},{6,102},{7,103},{8,104... | collective-permute-start | bytes 1572872 | tf_op jit(solution)/shard_map/ppermute | solution.py:41
  11.7 28.0 %collective-permute-start.4 = (f16[512,512]{1,0:T(8,128)(2,1)S(1)}, f16[512,512]{1,0:T(8,128)(2,1)S(1)}, u32[]{:S(2)}, u32[]{:S(2)}) collective-permute-start(f16[512,512]{1,0:T(8,128)(2,1)S(1)} %pad_maximum_fusion.1), channel_id=1, source_target_pairs={{0,64},{1,65},{2,66},{3,67},{4,68},{5,69},{6,70},{7,71},{8,72},{9,... | collective-permute-start | bytes 1572872 | tf_op jit(solution)/shard_map/ppermute | solution.py:41
  13.4 26.4 %collective-permute-start.5 = (f16[512,512]{1,0:T(8,128)(2,1)}, f16[512,512]{1,0:T(8,128)(2,1)S(1)}, u32[]{:S(2)}, u32[]{:S(2)}) collective-permute-start(f16[512,512]{1,0:T(8,128)(2,1)} %pad_maximum_fusion.2), channel_id=1, source_target_pairs={{0,32},{1,33},{2,34},{3,35},{4,36},{5,37},{6,38},{7,39},{8,40},{9,... | collective-permute-start | bytes 1572872 | tf_op jit(solution)/shard_map/ppermute | solution.py:41
  28.3 42.9 %all-to-all-start = ((f16[64,136,128]{2,1,0:T(8,128)(2,1)}), f16[64,136,128]{2,1,0:T(8,128)(2,1)}, u32[]{:S(2)}, u32[]{:S(2)}) async-start(f16[64,136,128]{2,1,0:T(8,128)(2,1)} %convert_element_type.144), calls=%async_computation | async-start | bytes 4456448 | tf_op jit(solution)/shard_map/all_to_all | solution.py:310
  44.4 26.1 %collective-permute-start.8 = (f16[2,2,32,512]{3,2,1,0:T(8,128)(2,1)S(1)}, f16[2,2,32,512]{3,2,1,0:T(8,128)(2,1)S(1)}, u32[]{:S(2)}, u32[]{:S(2)}) collective-permute-start(f16[2,2,32,512]{3,2,1,0:T(8,128)(2,1)S(1)} %get-tuple-element.70), channel_id=1, source_target_pairs={{0,12},{1,13},{2,14},{3,15},{4,8},{5,9},{6,10},{7,11},{8,4},{9,5},... | collective-permute-start | bytes 393224 | tf_op jit(solution)/shard_map/ppermute | solution.py:41
  46.0 24.5 %collective-permute-start.7 = (f16[2,2,32,512]{3,2,1,0:T(8,128)(2,1)S(1)}, f16[2,2,32,512]{3,2,1,0:T(8,128)(2,1)S(1)}, u32[]{:S(2)}, u32[]{:S(2)}) collective-permute-start(f16[2,2,32,512]{3,2,1,0:T(8,128)(2,1)S(1)} %get-tuple-element.71), channel_id=1, source_target_pairs={{0,8},{1,9},{2,10},{3,11},{4,12},{5,13},{6,14},{7,15},{8,0},{9,1},... | collective-permute-start | bytes 393224 | tf_op jit(solution)/shard_map/ppermute | solution.py:41
  47.1 23.4 %collective-permute-start.6 = (f16[2,2,32,512]{3,2,1,0:T(8,128)(2,1)S(1)}, f16[2,2,32,512]{3,2,1,0:T(8,128)(2,1)S(1)}, u32[]{:S(2)}, u32[]{:S(2)}) collective-permute-start(f16[2,2,32,512]{3,2,1,0:T(8,128)(2,1)S(1)} %get-tuple-element.72), channel_id=1, source_target_pairs={{0,4},{1,5},{2,6},{3,7},{4,0},{5,1},{6,2},{7,3},{8,12},{9,13},{10,... | collective-permute-start | bytes 393224 | tf_op jit(solution)/shard_map/ppermute | solution.py:41
  75.6 4.3 %collective-permute-start.9 = (f16[2,32,512]{2,1,0:T(8,128)(2,1)S(1)}, f16[2,32,512]{2,1,0:T(8,128)(2,1)S(1)}, u32[]{:S(2)}, u32[]{:S(2)}) collective-permute-start(f16[2,32,512]{2,1,0:T(8,128)(2,1)S(1)} %dynamic-slice_bitcast_fusion.3), channel_id=1, source_target_pairs={{0,16},{1,17},{2,18},{3,19},{4,20},{5,21},{6,22},{7,23},{8,24},{9,... | collective-permute-start | bytes 196616 | tf_op jit(solution)/shard_map/ppermute | solution.py:41
  119.3 14.6 %collective-permute-start.10 = (bf16[64,136,128]{2,1,0:T(8,128)(2,1)}, bf16[64,136,128]{2,1,0:T(8,128)(2,1)}, u32[]{:S(2)}, u32[]{:S(2)}) collective-permute-start(bf16[64,136,128]{2,1,0:T(8,128)(2,1)} %all_to_all.15.blocks), channel_id=1, source_target_pairs={{0,1},{1,0},{2,3},{3,2},{4,5},{5,4},{6,7},{7,6},{8,9},{9,8},{10,11... | collective-permute-start | bytes 6684680 | tf_op jit(solution)/shard_map/ppermute | solution.py:41
  119.3 23.1 %all-to-all-start.2 = ((f16[32,32,512]{2,1,0:T(8,128)(2,1)}), f16[32,32,512]{2,1,0:T(8,128)(2,1)S(1)}, u32[]{:S(2)}, u32[]{:S(2)}) async-start(f16[32,32,512]{2,1,0:T(8,128)(2,1)} %broadcast_in_dim.28), calls=%async_computation.2 | async-start | bytes 2097152 | tf_op jit(solution)/shard_map/all_to_all | solution.py:359
